TPU v7x, 32 devices: a whole 2x2x4 slice. The times are simulated.
32 devices in a mesh: samp: 4 (over x, core), win: 8 (over z, y).
Axes of the slice: x: 2, y: 2, z: 4, core: 2. Of those that a mesh axis runs over, the one named last changes fastest.
Arguments:
- atoms: bfloat16 [64, 8192, 128], P('samp', 'win'), may hold values from -6 to 6
- cond: float32 [8, 8192, 128], P('samp', 'win'), may hold values from -6 to 6
- pair: bfloat16 [8, 8192, 16, 128], P('samp', 'win'), may hold values from -6 to 6
- struct_ids: int32 [64], P('samp'), may hold values from 0 to 7, as said below
- cotangent: bfloat16 [64, 8192, 128], P('samp', 'win'), may hold values from -6 to 6
- weights: float32 [17, 128, 128], replicated
- vectors: float32 [7, 128], replicated
- pair_weight: float32 [16, 4], replicated, may hold values from -1.5 to 1.5
- stat_left: float32 [17, 128, 128], P(None, 'win'), as said below
- stat_right: float32 [17, 128, 128], P(None, 'win')
- root_left: float32 [17, 128, 128], P(None, 'win')
- root_right: float32 [17, 128, 128], replicated
- stat_vectors: float32 [7, 128], replicated, may hold values from 47185.92 to 188743.69
- stat_pair: float32 [16, 4], replicated, may hold values from 47185.92 to 188743.69
- ema_weights: float32 [17, 128, 128], P(None, 'win'), may hold values from -0.5 to 0.5
- ema_vectors: float32 [7, 128], replicated, may hold values from -3 to 3
- ema_pair: float32 [16, 4], replicated, may hold values from -1.5 to 1.5
Outputs:
- out: bfloat16 [64, 8192, 128], P('samp', 'win')
- grad_atoms: bfloat16 [64, 8192, 128], P('samp', 'win')
- grad_weights: float32 [17, 128, 128], P(None, 'win')
- grad_vectors: float32 [7, 128], replicated
- grad_pair_weight: float32 [16, 4], replicated
- new_left: float32 [17, 128, 128], P(None, 'win')
- new_right: float32 [17, 128, 128], P(None, 'win')
- new_weights: float32 [17, 128, 128], P(None, 'win')
- new_weights_low: bfloat16 [17, 128, 128], P(None, 'win')
- new_vectors: float32 [7, 128], replicated
- new_pair_weight: float32 [16, 4], replicated
- new_stat_vectors: float32 [7, 128], replicated
- new_stat_pair: float32 [16, 4], replicated
- new_ema_weights: float32 [17, 128, 128], P(None, 'win')
- new_ema_vectors: float32 [7, 128], replicated
- new_ema_pair: float32 [16, 4], replicated
Inputs may be any that keep to these rules, and one draw needn't show every extreme that they name: `struct_ids`: sample n names a structure among the 2 structures that start at n // 16 * 2; every structure is named by exactly 8 samples. `stat_left`: each block of the statistics and of the roots is symmetric.
All inputs are finite; a program needn't handle non-finite values.
Results may differ from a plain program's by a relative error of at most 0.015.
The roundings to bfloat16 on the way count: a program that leaves them out, or rounds other values in their place, can miss the bound.
Values may be sent and summed in bfloat16 or wider, within the bound.
No kernel may reach another device: no remote copies, remote signals or barrier semaphores. Data moves between devices by JAX's collectives and lax.ppermute only.
A program may use at most 576 MiB of HBM per device.

v0:
```python
import math

import jax
import jax.numpy as jnp
from jax import lax
from jax.sharding import PartitionSpec as P

HEADS = 4
FF = 256
QW = 32
HALO = 48
KW = 128


stat_decay = 0.5
ema_decay = 0.8
matrix_rate = 1.0
vector_rate = 0.2


def extended(block, sides, width):
    for axis, dim in sides:
        count = lax.axis_size(axis)
        forward = [(i, i + 1) for i in range(count - 1)]
        backward = [(target, source) for source, target in forward]
        low = lax.ppermute(
            lax.slice_in_dim(block, block.shape[dim] - width, None, axis=dim), axis, forward
        )
        high = lax.ppermute(lax.slice_in_dim(block, 0, width, axis=dim), axis, backward)
        block = jnp.concatenate([low, block, high], axis=dim)
    return block


def passed_along(shard, axis, by):
    devices = lax.axis_size(axis)
    pairs = [(i, i + by) for i in range(devices) if 0 <= i + by < devices]
    return lax.ppermute(shard, axis, pairs)


def layer_stats(values):
    center = values - jnp.mean(values, axis=-1, keepdims=True)
    inverse = lax.rsqrt(jnp.mean(center * center, axis=-1, keepdims=True) + 1e-05)
    return (center * inverse, inverse)


def layer_back(normed, inverse, grad_norm):
    return inverse * (
        grad_norm
        - jnp.mean(grad_norm, axis=-1, keepdims=True)
        - normed * jnp.mean(grad_norm * normed, axis=-1, keepdims=True)
    )


def key_windows(padded, count):
    group_size, _, atom_width = padded.shape
    blocks = padded.reshape(group_size, count + 3, QW, atom_width)
    return jnp.concatenate([blocks[:, offset : offset + count] for offset in range(4)], axis=2)


def window_fold(window_grad, count):
    group_size = window_grad.shape[0]
    atom_width = window_grad.shape[-1]
    parts = window_grad.reshape(group_size, count, 4, QW, atom_width)
    folded = jnp.zeros((group_size, count + 3, QW, atom_width), jnp.float32)
    for offset in range(4):
        folded = folded.at[:, offset : offset + count].add(parts[:, :, offset].astype(jnp.float32))
    return folded.reshape(group_size, (count + 3) * QW, atom_width)


def body(
    atoms,
    cond,
    pair,
    struct_ids,
    cotangent,
    weights,
    vectors,
    pair_weight,
    stat_left,
    stat_right,
    root_left,
    root_right,
    stat_vectors,
    stat_pair,
    ema_weights,
    ema_vectors,
    ema_pair,
):
    high = lax.Precision.HIGHEST
    f32 = jnp.float32
    bf16 = jnp.bfloat16
    samp_dev, atom_dev, atom_width = atoms.shape
    struct_dev = cond.shape[0]
    count = atom_dev // QW
    head_dim = atom_width // HEADS
    factor = 1.0 / math.sqrt(head_dim)
    in_blocks = 2 * FF // atom_width
    out_blocks = FF // atom_width
    win_index = lax.axis_index("win")
    win_count = lax.axis_size("win")
    local_ids = struct_ids - lax.axis_index("samp") * struct_dev
    onehot = (local_ids[:, None] == jnp.arange(struct_dev, dtype=jnp.int32)[None, :]).astype(f32)
    low_weights = weights.astype(bf16)

    def select(table):
        return jnp.einsum("gs,sac->gac", onehot, table, precision=high)

    def gather_back(term):
        return jnp.einsum("gs,gac->sac", onehot, term, precision=high)

    def condition_projection(source, block):
        return jnp.einsum("sac,cd->sad", source, low_weights[block], preferred_element_type=f32)

    def row_proj(source, block):
        return jnp.einsum("gac,cd->gad", source, low_weights[block], preferred_element_type=f32)

    cond_norm, _ = layer_stats(cond)
    cond_one = (cond_norm * vectors[0]).astype(bf16)
    cond_two = (cond_norm * vectors[4]).astype(bf16)
    scale_one = jax.nn.sigmoid(condition_projection(cond_one, 0) + vectors[1])
    shift_one = condition_projection(cond_one, 1)
    gate_one = jax.nn.sigmoid(condition_projection(cond_one, 7) + vectors[3])
    scale_two = jax.nn.sigmoid(condition_projection(cond_two, 8) + vectors[5])
    shift_two = condition_projection(cond_two, 9)
    gate_two = jax.nn.sigmoid(condition_projection(cond_two, 10) + vectors[6])
    pair_f = pair.astype(f32)
    pair_center = pair_f - jnp.mean(pair_f, axis=2, keepdims=True)
    pair_norm = pair_center * lax.rsqrt(
        jnp.mean(pair_center * pair_center, axis=2, keepdims=True) + 1e-05
    )
    bias_table = jnp.einsum("sack,ch->shak", pair_norm, pair_weight, precision=high)
    bias_table = bias_table.reshape(struct_dev, HEADS, count, QW, KW)
    inputs = atoms.astype(f32)
    normed_one, inverse_one = layer_stats(inputs)
    sel_scale_one = select(scale_one)
    ada_one = (sel_scale_one * normed_one + select(shift_one)).astype(bf16)
    queries = (row_proj(ada_one, 2) + vectors[2]).astype(bf16)
    attn_gate = jax.nn.sigmoid(row_proj(ada_one, 5))
    key_rows = row_proj(ada_one, 3).astype(bf16)
    value_rows = row_proj(ada_one, 4).astype(bf16)
    padded = extended(jnp.stack([key_rows, value_rows]), (("win", 2),), HALO)
    key_pad = padded[0]
    value_pad = padded[1]
    key_pos = (
        win_index * atom_dev - HALO + jnp.arange(count)[:, None] * QW + jnp.arange(KW)[None, :]
    )
    key_valid = (key_pos >= 0) & (key_pos < atom_dev * win_count)
    valid_five = key_valid[None, :, None, None, :]
    valid_slot = key_valid[None, :, :, None]
    group_size = max(
        [
            size_try
            for size_try in range(1, samp_dev + 1)
            if samp_dev % size_try == 0 and size_try * atom_dev <= 4096
        ]
    )
    count_of_blocks = samp_dev // group_size

    def split(array):
        return array.reshape((count_of_blocks, group_size) + array.shape[1:])

    def block_scores(query_blk, key_blk, onehot_blk):
        query_heads = query_blk.reshape(group_size, count, QW, HEADS, head_dim)
        key_heads = key_windows(key_blk, count).reshape(group_size, count, KW, HEADS, head_dim)
        bias_sel = jnp.einsum("gs,shwqk->gwhqk", onehot_blk, bias_table, precision=high)
        raw_scores = (
            jnp.einsum("gwqhd,gwkhd->gwhqk", query_heads, key_heads, preferred_element_type=f32)
            * factor
            + bias_sel
        )
        return (jnp.where(valid_five, raw_scores, -1000000000.0), query_heads, key_heads)

    def forward_block(carry_zero, block_items):
        query_blk, key_blk, value_blk, onehot_blk = block_items
        scores, _, _ = block_scores(query_blk, key_blk, onehot_blk)
        row_top = jnp.max(scores, axis=-1, keepdims=True)
        row_exp = jnp.exp(scores - row_top)
        row_total = jnp.sum(row_exp, axis=-1, keepdims=True)
        attn_probs = row_exp / row_total
        value_heads = key_windows(value_blk, count).reshape(group_size, count, KW, HEADS, head_dim)
        mixed = jnp.einsum(
            "gwhqk,gwkhd->gwqhd", attn_probs.astype(bf16), value_heads, preferred_element_type=f32
        )
        return (
            carry_zero,
            (
                mixed.reshape(group_size, atom_dev, atom_width),
                (row_top + jnp.log(row_total))[..., 0],
            ),
        )

    _, (attn_mix, log_total) = lax.scan(
        forward_block,
        jnp.zeros((), f32),
        (split(queries), split(key_pad), split(value_pad), split(onehot)),
    )
    attn_mix = attn_mix.reshape(samp_dev, atom_dev, atom_width)
    mixed_low = (attn_gate * attn_mix).astype(bf16)
    attn_out = row_proj(mixed_low, 6)
    sel_gate_one = select(gate_one)
    hidden_one = inputs + sel_gate_one * attn_out
    normed_two, second_inverse_root = layer_stats(hidden_one)
    sel_scale_two = select(scale_two)
    ada_two = (sel_scale_two * normed_two + select(shift_two)).astype(bf16)
    in_weights = low_weights[11 : 11 + in_blocks]
    out_weights = low_weights[11 + in_blocks :]
    expand = jnp.einsum("gac,bcd->gabd", ada_two, in_weights, preferred_element_type=f32).reshape(
        samp_dev, atom_dev, 2 * FF
    )
    gate_ff = expand[..., :FF]
    up_ff = expand[..., FF:]
    sig_ff = jax.nn.sigmoid(gate_ff)
    hidden_low = (gate_ff * sig_ff * up_ff).astype(bf16)
    hidden_four = hidden_low.reshape(samp_dev, atom_dev, out_blocks, atom_width)
    ff_out = jnp.einsum("gabc,bcd->gad", hidden_four, out_weights, preferred_element_type=f32)
    sel_gate_two = select(gate_two)
    result = hidden_one + sel_gate_two * ff_out
    grad_out = cotangent.astype(f32)
    grad_ff = (grad_out * sel_gate_two).astype(bf16)
    pre_gate_two = (gather_back(grad_out * ff_out) * gate_two * (1.0 - gate_two)).astype(bf16)
    grad_wout = jnp.einsum("gabc,gad->bcd", hidden_four, grad_ff, preferred_element_type=f32)
    grad_hidden = jnp.einsum(
        "gad,bcd->gabc", grad_ff, out_weights, preferred_element_type=f32
    ).reshape(samp_dev, atom_dev, FF)
    grad_gate_ff = grad_hidden * up_ff * sig_ff * (1.0 + gate_ff * (1.0 - sig_ff))
    grad_up_ff = grad_hidden * gate_ff * sig_ff
    grad_expand = jnp.concatenate([grad_gate_ff, grad_up_ff], axis=-1).astype(bf16)
    grad_expand = grad_expand.reshape(samp_dev, atom_dev, in_blocks, atom_width)
    grad_win = jnp.einsum("gac,gabd->bcd", ada_two, grad_expand, preferred_element_type=f32)
    grad_ada_two = jnp.einsum("gabd,bcd->gac", grad_expand, in_weights, preferred_element_type=f32)
    pre_scale_two = (gather_back(grad_ada_two * normed_two) * scale_two * (1.0 - scale_two)).astype(
        bf16
    )
    pre_shift_two = gather_back(grad_ada_two).astype(bf16)
    grad_hidden_one = grad_out + layer_back(
        normed_two, second_inverse_root, grad_ada_two * sel_scale_two
    )
    grad_attn = (grad_hidden_one * sel_gate_one).astype(bf16)
    pre_gate_one = (gather_back(grad_hidden_one * attn_out) * gate_one * (1.0 - gate_one)).astype(
        bf16
    )
    grad_wo = jnp.einsum("gac,gad->cd", mixed_low, grad_attn, preferred_element_type=f32)
    grad_mixed = jnp.einsum("gad,cd->gac", grad_attn, low_weights[6], preferred_element_type=f32)
    grad_mix = (grad_mixed * attn_gate).astype(bf16)
    grad_gate_pre = (grad_mixed * attn_mix * attn_gate * (1.0 - attn_gate)).astype(bf16)

    def backward_block(bias_grad, block_items):
        query_blk, key_blk, value_blk, onehot_blk, grad_blk, total_blk = block_items
        scores, query_heads, key_heads = block_scores(query_blk, key_blk, onehot_blk)
        attn_probs = jnp.exp(scores - total_blk[..., None])
        probs_low = attn_probs.astype(bf16)
        value_heads = key_windows(value_blk, count).reshape(group_size, count, KW, HEADS, head_dim)
        grad_heads = grad_blk.reshape(group_size, count, QW, HEADS, head_dim)
        grad_probs = jnp.einsum(
            "gwqhd,gwkhd->gwhqk", grad_heads, value_heads, preferred_element_type=f32
        )
        grad_scores = (
            attn_probs * (grad_probs - jnp.sum(grad_probs * attn_probs, axis=-1, keepdims=True))
        ).astype(bf16)
        grad_query = (
            jnp.einsum("gwhqk,gwkhd->gwqhd", grad_scores, key_heads, preferred_element_type=f32)
            * factor
        )
        grad_keys = (
            jnp.einsum("gwhqk,gwqhd->gwkhd", grad_scores, query_heads, preferred_element_type=f32)
            * factor
        )
        grad_values = jnp.einsum(
            "gwhqk,gwqhd->gwkhd", probs_low, grad_heads, preferred_element_type=f32
        )
        key_slot = jnp.where(
            valid_slot, grad_keys.reshape(group_size, count, KW, atom_width), 0.0
        ).astype(bf16)
        value_slot = jnp.where(
            valid_slot, grad_values.reshape(group_size, count, KW, atom_width), 0.0
        ).astype(bf16)
        bias_grad = bias_grad + jnp.einsum(
            "gs,gwhqk->shwqk", onehot_blk, grad_scores.astype(f32), precision=high
        )
        return (
            bias_grad,
            (grad_query.reshape(group_size, atom_dev, atom_width), key_slot, value_slot),
        )

    bias_grad, (grad_query_all, key_slots, value_slots) = lax.scan(
        backward_block,
        jnp.zeros((struct_dev, HEADS, count, QW, KW), f32),
        (
            split(queries),
            split(key_pad),
            split(value_pad),
            split(onehot),
            split(grad_mix),
            log_total,
        ),
    )
    grad_query_all = grad_query_all.reshape(samp_dev, atom_dev, atom_width)
    key_slots = key_slots.reshape(samp_dev, count, KW, atom_width)
    value_slots = value_slots.reshape(samp_dev, count, KW, atom_width)
    grad_key_pad = window_fold(key_slots, count)
    grad_value_pad = window_fold(value_slots, count)
    rims_low = jnp.stack([grad_key_pad[:, :HALO], grad_value_pad[:, :HALO]])
    rims_high = jnp.stack(
        [grad_key_pad[:, HALO + atom_dev :], grad_value_pad[:, HALO + atom_dev :]]
    )
    arriving_from_above = passed_along(rims_low.astype(jnp.bfloat16), "win", -1).astype(
        rims_low.dtype
    )
    from_below = passed_along(rims_high.astype(jnp.bfloat16), "win", 1).astype(rims_high.dtype)
    own_grads = jnp.stack(
        [grad_key_pad[:, HALO : HALO + atom_dev], grad_value_pad[:, HALO : HALO + atom_dev]]
    )
    own_grads = own_grads.at[:, :, atom_dev - HALO :].add(arriving_from_above)
    own_grads = own_grads.at[:, :, :HALO].add(from_below)
    grad_kv = jnp.einsum("gac,bgad->bcd", ada_one.astype(f32), own_grads, precision=high)
    kv_back = jnp.einsum("bgad,bcd->gac", own_grads, low_weights[3:5].astype(f32), precision=high)
    grad_query_low = grad_query_all.astype(bf16)
    project_grads = jnp.stack([grad_query_low, grad_gate_pre])
    project_weights = jnp.stack([low_weights[2], low_weights[5]])
    grad_pq = jnp.einsum("gac,bgad->bcd", ada_one, project_grads, preferred_element_type=f32)
    grad_ada_one = (
        jnp.einsum("bgad,bcd->gac", project_grads, project_weights, preferred_element_type=f32)
        + kv_back
    )
    pre_scale_one = (gather_back(grad_ada_one * normed_one) * scale_one * (1.0 - scale_one)).astype(
        bf16
    )
    pre_shift_one = gather_back(grad_ada_one).astype(bf16)
    grad_inputs = grad_hidden_one + layer_back(
        normed_one, inverse_one, grad_ada_one * sel_scale_one
    )
    cond_grads_one = jnp.stack([pre_scale_one, pre_shift_one, pre_gate_one])
    cond_grads_two = jnp.stack([pre_scale_two, pre_shift_two, pre_gate_two])
    cond_weights_one = jnp.stack([low_weights[0], low_weights[1], low_weights[7]])
    cond_weights_two = jnp.stack([low_weights[8], low_weights[9], low_weights[10]])
    grad_cond_one = jnp.einsum(
        "sac,bsad->bcd", cond_one, cond_grads_one, preferred_element_type=f32
    )
    grad_cond_two = jnp.einsum(
        "sac,bsad->bcd", cond_two, cond_grads_two, preferred_element_type=f32
    )
    back_one = jnp.einsum(
        "bsad,bcd->sac", cond_grads_one, cond_weights_one, preferred_element_type=f32
    )
    back_two = jnp.einsum(
        "bsad,bcd->sac", cond_grads_two, cond_weights_two, preferred_element_type=f32
    )
    grad_vec = jnp.stack(
        [
            jnp.sum(back_one * cond_norm, axis=(0, 1)),
            jnp.sum(pre_scale_one.astype(f32), axis=(0, 1)),
            jnp.sum(grad_query_low.astype(f32), axis=(0, 1)),
            jnp.sum(pre_gate_one.astype(f32), axis=(0, 1)),
            jnp.sum(back_two * cond_norm, axis=(0, 1)),
            jnp.sum(pre_scale_two.astype(f32), axis=(0, 1)),
            jnp.sum(pre_gate_two.astype(f32), axis=(0, 1)),
        ]
    )
    grad_pw = jnp.einsum(
        "sack,shak->ch",
        pair_norm,
        bias_grad.reshape(struct_dev, HEADS, atom_dev, KW),
        precision=high,
    )
    grad_w = jnp.concatenate(
        [
            jnp.stack(
                [
                    grad_cond_one[0],
                    grad_cond_one[1],
                    grad_pq[0],
                    grad_kv[0],
                    grad_kv[1],
                    grad_pq[1],
                    grad_wo,
                    grad_cond_one[2],
                    grad_cond_two[0],
                    grad_cond_two[1],
                    grad_cond_two[2],
                ]
            ),
            grad_win,
            grad_wout,
        ],
        axis=0,
    )
    total_w, total_v, total_p = lax.psum((grad_w, grad_vec, grad_pw), ("samp", "win"))
    own_count = stat_left.shape[1]
    row_start = win_index * own_count
    own_rows = lax.dynamic_slice_in_dim(total_w, row_start, own_count, 1)
    own_cols = lax.dynamic_slice_in_dim(total_w, row_start, own_count, 2)
    left_new = stat_decay * stat_left + (1.0 - stat_decay) * jnp.einsum(
        "bic,bjc->bij", own_rows, total_w, precision=high
    )
    right_new = stat_decay * stat_right + (1.0 - stat_decay) * jnp.einsum(
        "bci,bcj->bij", own_cols, total_w, precision=high
    )
    left_part = jnp.einsum("bij,bjk->bik", root_left, total_w, precision=high)
    update_step = jnp.einsum("bik,bkl->bil", left_part, root_right, precision=high)
    weight_rows = lax.dynamic_slice_in_dim(weights, row_start, own_count, 1)
    weights_new = weight_rows - matrix_rate * update_step
    stat_v_new = stat_decay * stat_vectors + (1.0 - stat_decay) * total_v * total_v
    vectors_new = vectors - vector_rate * total_v * lax.rsqrt(stat_v_new)
    stat_p_new = stat_decay * stat_pair + (1.0 - stat_decay) * total_p * total_p
    pair_new = pair_weight - vector_rate * total_p * lax.rsqrt(stat_p_new)
    return (
        result.astype(bf16),
        grad_inputs.astype(bf16),
        own_rows,
        total_v,
        total_p,
        left_new,
        right_new,
        weights_new,
        weights_new.astype(bf16),
        vectors_new,
        pair_new,
        stat_v_new,
        stat_p_new,
        ema_decay * ema_weights + (1.0 - ema_decay) * weights_new,
        ema_decay * ema_vectors + (1.0 - ema_decay) * vectors_new,
        ema_decay * ema_pair + (1.0 - ema_decay) * pair_new,
    )


def solution(mesh):
    placed = (
        P("samp", "win", None),
        P("samp", "win", None),
        P("samp", "win", None, None),
        P("samp"),
        P("samp", "win", None),
        P(),
        P(),
        P(),
        P(None, "win", None),
        P(None, "win", None),
        P(None, "win", None),
        P(),
        P(),
        P(),
        P(None, "win", None),
        P(),
        P(),
    )
    return jax.shard_map(
        body,
        mesh=mesh,
        in_specs=placed,
        out_specs=(
            P("samp", "win", None),
            P("samp", "win", None),
            P(None, "win", None),
            P(),
            P(),
            P(None, "win", None),
            P(None, "win", None),
            P(None, "win", None),
            P(None, "win", None),
            P(),
            P(),
            P(),
            P(),
            P(None, "win", None),
            P(),
            P(),
        ),
        check_vma=False,
    )
```

profile of v0, /device:TPU:0, one launch (start us, length us, event | category | flops | bytes accessed | tf_op | source)
XLA Modules:
  0.0 1927.8 jit_solution(2644594116962246197)
XLA Ops:
  22.6 28.3 %fusion.81 = f32[16,1024]{0,1:T(8,128)S(1)} fusion(f32[16,1024]{0,1:T(8,128)S(1)} %broadcast_multiply_fusion.7, bf16[16,1024,128]{2,1,0:T(8,128)(2,1)S(1)} %copy-done.8), kind=kLoop, calls=%fused_computation.116 | loop fusion | flops 8372224 | bytes 4325376 | tf_op jit(solution)/shard_map/reduce_sum | solution.py:42
  55.4 18.8 fusion.73
  179.7 386.0 %while.42 = (s32[]{:T(128)}, f32[4,4,1024,128]{3,2,1,0:T(8,128)}, f32[4,4,32,4,32]{4,3,2,1,0:T(4,128)}, bf16[4,4,1120,128]{3,2,1,0:T(8,128)(2,1)}, bf16[4,4,1024...) while((s32[]{:T(128)}, f32[4,4,1024,128]{3,2,1,0:T(8,128)}, ...), condition=%wide.region_9.10_spmd.clone, body=%wide.region_6.9_spmd.clone.sunk | while | flops 371195904 | bytes 130099432 | solution.py:192
  191.3 20.4 %fusion.359 = f32[4,4,32,32,128]{4,0,3,2,1:T(4,128)} fusion(f32[2,4,32,32,128]{4,0,3,2,1:T(2,128)} %get-tuple-element.821, f32[4,4,2]{1,2,0:T(2,128)S(1)} %get-tuple-element.820, s32[]{:T(128)} %get-tuple-element.804), kind=kOutput, calls=%fused_computation.26.clone.2 | convolution fusion | flops 50331648 | bytes 12583940 | tf_op jit(solution)/shard_map/while/body/eval_jaxpr/gs,shwqk->gwhqk/dot_general | solution.py:165
  287.6 20.4 %fusion.359 = f32[4,4,32,32,128]{4,0,3,2,1:T(4,128)} fusion(f32[2,4,32,32,128]{4,0,3,2,1:T(2,128)} %get-tuple-element.821, f32[4,4,2]{1,2,0:T(2,128)S(1)} %get-tuple-element.820, s32[]{:T(128)} %get-tuple-element.804), kind=kOutput, calls=%fused_computation.26.clone.2 | convolution fusion | flops 50331648 | bytes 12583940 | tf_op jit(solution)/shard_map/while/body/eval_jaxpr/gs,shwqk->gwhqk/dot_general | solution.py:165
  384.0 20.4 %fusion.359 = f32[4,4,32,32,128]{4,0,3,2,1:T(4,128)} fusion(f32[2,4,32,32,128]{4,0,3,2,1:T(2,128)} %get-tuple-element.821, f32[4,4,2]{1,2,0:T(2,128)S(1)} %get-tuple-element.820, s32[]{:T(128)} %get-tuple-element.804), kind=kOutput, calls=%fused_computation.26.clone.2 | convolution fusion | flops 50331648 | bytes 12583940 | tf_op jit(solution)/shard_map/while/body/eval_jaxpr/gs,shwqk->gwhqk/dot_general | solution.py:165
  480.3 20.4 %fusion.359 = f32[4,4,32,32,128]{4,0,3,2,1:T(4,128)} fusion(f32[2,4,32,32,128]{4,0,3,2,1:T(2,128)} %get-tuple-element.821, f32[4,4,2]{1,2,0:T(2,128)S(1)} %get-tuple-element.820, s32[]{:T(128)} %get-tuple-element.804), kind=kOutput, calls=%fused_computation.26.clone.2 | convolution fusion | flops 50331648 | bytes 12583940 | tf_op jit(solution)/shard_map/while/body/eval_jaxpr/gs,shwqk->gwhqk/dot_general | solution.py:165
  582.5 20.2 %fusion.278 = (f32[16,1024]{0,1:T(8,128)}, f32[16,1024,128]{2,0,1:T(8,128)S(1)}, f32[16,1024,128]{2,0,1:T(8,128)}) fusion(f32[16,1024,128]{2,0,1:T(8,128)S(1)} %fusion.110, bf16[16,1024,128]{2,1,0:T(8,128)(2,1)S(1)} %copy-done.10, f32[2,1024,128]{2,1,0:T(8,128)S(1)} %copy-done.42, s32[16]{0:T(128)S(1)} %copy-done.84), kind=kOutput, calls=%fused_computation.405 | convolution fusion | flops 58703904 | bytes 30474304 | tf_op jit(solution)/shard_map/gs,sac->gac/dot_general | solution.py:106
  604.3 28.3 %multiply_reduce_fusion.2 = f32[16,1024]{0,1:T(8,128)S(1)} fusion(f32[16,1024,128]{2,0,1:T(8,128)S(1)} %get-tuple-element.544, f32[16,1024]{0,1:T(8,128)S(1)} %broadcast_multiply_fusion.6), kind=kLoop, calls=%fused_computation.159 | loop fusion | flops 6275072 | bytes 8519680 | tf_op jit(solution)/shard_map/reduce_sum | solution.py:42
  660.8 26.7 %fusion.59 = (bf16[16,1024,256]{1,2,0:T(8,128)(2,1)}, bf16[16,1024,256]{1,2,0:T(8,128)(2,1)}, bf16[16,1024,256]{1,2,0:T(8,128)(2,1)}) fusion(f32[16,1024,2,128]{1,3,2,0:T(8,128)} %fusion.119, f32[16,1024,512]{1,2,0:T(8,128)} %bitcast.550), kind=kLoop, calls=%fused_computation.86 | loop fusion | flops 67108864 | bytes 75497472 | tf_op jit(solution)/shard_map/convert.27
  726.1 34.4 %fusion.270 = (f32[16,1024]{0,1:T(8,128)}, f32[16,1024]{0,1:T(8,128)}, f32[16,1024,128,1]{2,0,3,1:T(8,128)S(1)}) fusion(f32[16,1024,128]{2,0,1:T(8,128)} %fusion.206, f32[16,1024]{0,1:T(8,128)S(1)} %add_rsqrt_fusion.1, f32[16,1024,128]{2,0,1:T(8,128)} %copy-done.6, f32[16,1024]{0,1:T(8,128)S(1)} %broadcast_multiply_fusion.6, ...), kind=kOutput, calls=%fused_computation.403 | convolution fusion | flops 2160033792 | bytes 43253760 | tf_op jit(solution)/shard_map/gabd,bcd->gac/dot_general | solution.py:230
  783.6 25.9 %multiply_convert_fusion.3 = (bf16[16,1024,128]{2,0,1:T(8,128)(2,1)S(1)}, f32[16,1024,128]{2,0,1:T(8,128)}, bf16[16,1024,128]{2,0,1:T(8,128)(2,1)}, f32[16,1024,128,1]{2,0,3,1:T(8,128)}) fusion(f32[16,1024,128]{2,0,1:T(8,128)} %get-tuple-element.601, f32[16,1024]{0,1:T(8,128)S(1)} %get-tuple-element.606, f32[16,1024,128]{2,0,1:T(8,128)} %copy-done.6, ...), kind=kOutput, calls=%fused_computation.156 | convolution fusion | flops 1103101952 | bytes 81854464 | tf_op jit(solution)/shard_map/gabc,bcd->gad/dot_general | solution.py:215
  820.6 664.3 %while.43 = (s32[]{:T(128)}, f32[2,4,32,32,128]{4,0,3,1,2:T(2,128)}, bf16[4,4,1024,128]{2,3,1,0:T(8,128)(2,1)}, bf16[4,4,32,128,128]{4,3,2,1,0:T(8,128)(2,1)}, b...) while((s32[]{:T(128)}, ...), condition=%wide.region_16.17_spmd.clone.clone.clone, body=%wide.region_14.16_spmd.clone.clone.clone.sunk | while | flops 837828608 | bytes 328945280 | solution.py:285
  831.6 20.4 %fusion.379 = f32[4,4,32,32,128]{4,0,3,2,1:T(4,128)} fusion(f32[2,4,32,32,128]{4,0,3,2,1:T(2,128)} %get-tuple-element.862, f32[4,4,2]{1,2,0:T(2,128)S(1)} %get-tuple-element.861, s32[]{:T(128)} %get-tuple-element.839), kind=kOutput, calls=%fused_computation.70.clone.1 | convolution fusion | flops 50331648 | bytes 12583940 | tf_op jit(solution)/shard_map/while/body/eval_jaxpr/gs,shwqk->gwhqk/dot_general | solution.py:165
  995.1 20.4 %fusion.379 = f32[4,4,32,32,128]{4,0,3,2,1:T(4,128)} fusion(f32[2,4,32,32,128]{4,0,3,2,1:T(2,128)} %get-tuple-element.862, f32[4,4,2]{1,2,0:T(2,128)S(1)} %get-tuple-element.861, s32[]{:T(128)} %get-tuple-element.839), kind=kOutput, calls=%fused_computation.70.clone.1 | convolution fusion | flops 50331648 | bytes 12583940 | tf_op jit(solution)/shard_map/while/body/eval_jaxpr/gs,shwqk->gwhqk/dot_general | solution.py:165
  1159.0 20.4 %fusion.379 = f32[4,4,32,32,128]{4,0,3,2,1:T(4,128)} fusion(f32[2,4,32,32,128]{4,0,3,2,1:T(2,128)} %get-tuple-element.862, f32[4,4,2]{1,2,0:T(2,128)S(1)} %get-tuple-element.861, s32[]{:T(128)} %get-tuple-element.839), kind=kOutput, calls=%fused_computation.70.clone.1 | convolution fusion | flops 50331648 | bytes 12583940 | tf_op jit(solution)/shard_map/while/body/eval_jaxpr/gs,shwqk->gwhqk/dot_general | solution.py:165
  1323.2 20.4 %fusion.379 = f32[4,4,32,32,128]{4,0,3,2,1:T(4,128)} fusion(f32[2,4,32,32,128]{4,0,3,2,1:T(2,128)} %get-tuple-element.862, f32[4,4,2]{1,2,0:T(2,128)S(1)} %get-tuple-element.861, s32[]{:T(128)} %get-tuple-element.839), kind=kOutput, calls=%fused_computation.70.clone.1 | convolution fusion | flops 50331648 | bytes 12583940 | tf_op jit(solution)/shard_map/while/body/eval_jaxpr/gs,shwqk->gwhqk/dot_general | solution.py:165
  1614.2 23.0 %fusion.191 = f32[16,4]{0,1:T(4,128)S(1)} fusion(f32[2,4,1024,128]{3,2,1,0:T(8,128)} %bitcast.593, bf16[2,1024,16,128]{3,2,1,0:T(8,128)(2,1)S(1)} %bitcast.555, f32[2,1024,128]{2,1,0:T(8,128)S(1)} %copy-done.51, f32[2,1024,128]{2,1,0:T(8,128)S(1)} %copy-done.35), kind=kOutput, calls=%fused_computation.254 | convolution fusion | flops 213909504 | bytes 14680320 | tf_op jit(solution)/shard_map/sack,shak->ch/dot_general | solution.py:359
  1674.2 37.8 %fusion.271 = (f32[16,1024]{0,1:T(8,128)}, f32[16,1024]{0,1:T(8,128)}, f32[16,1024,128]{2,0,1:T(8,128)}, f32[16,1024,128]{2,0,1:T(8,128)}) fusion(f32[16,1024]{0,1:T(8,128)} %copy-done.36, f32[16,1024]{0,1:T(8,128)S(1)} %copy-done.31, bf16[16,1024,128]{2,1,0:T(8,128)(2,1)S(1)} %copy-done.11, f32[16,1024,128]{2,0,1:T(8,128)S(1)} %bitcast.565, ...), kind=kOutput, calls=%fused_computation.404 | convolution fusion | flops 6459195392 | bytes 55312384 | tf_op jit(solution)/shard_map/bgad,bcd->gac/dot_general | solution.py:316
  1712.0 16.4 fusion.79
  1734.1 17.7 fusion.182
  1773.4 17.1 fusion.78
  1794.6 41.2 %all-reduce.2 = (f32[7,128]{1,0:T(8,128)S(1)}, f32[16,4]{0,1:T(4,128)S(1)}) all-reduce(f32[7,128]{1,0:T(8,128)S(1)} %stack.141, f32[16,4]{0,1:T(4,128)S(1)} %fusion.191), channel_id=1, replica_groups=mesh['samp'=4,'win'=8] {'samp','win'}, use_global_device_ids=true, to_apply=%region_27.28 | all-reduce | flops 960 | bytes 7680 | tf_op jit(solution)/shard_map/psum | solution.py:387
  1837.1 67.9 %all-reduce.5.cloned.1.call-done = f32[17,128,128]{1,2,0:T(8,128)} async-done(((f32[17,128,128]{1,2,0:T(8,128)}), f32[17,128,128]{1,2,0:T(8,128)}) %all-reduce.5.cloned.1.call-update) | async-done | bytes 1114128 | tf_op jit(solution)/shard_map/psum | solution.py:387
  (634 shorter events, 1333.9 us)
Async XLA Ops:
  7.2 1903.6 %copy-start = (f32[17,128,128]{2,1,0:T(8,128)S(1)}, f32[17,128,128]{2,1,0:T(8,128)}, u32[]{:S(2)}) copy-start(f32[17,128,128]{2,1,0:T(8,128)} %param.52) | copy-start | bytes 3342340
  7.2 1897.8 %all-reduce.5.cloned.1.call-start = ((), (), s32[]{:S(2)}) async-start(), calls=%async_computation | async-start | bytes 2228224 | tf_op jit(solution)/shard_map/psum | solution.py:387
  17.0 34.1 %copy-start.104 = (s32[16]{0:T(128)S(1)}, s32[16]{0:T(128)}, u32[]{:S(2)}) copy-start(s32[16]{0:T(128)} %param.44) | copy-start | bytes 196
  17.4 37.9 %copy-start.40 = (f32[2,1024,128]{2,1,0:T(8,128)}, f32[2,1024,128]{2,1,0:T(8,128)S(1)}, u32[]{:S(2)}) copy-start(f32[2,1024,128]{2,1,0:T(8,128)S(1)} %fusion.151) | copy-start | bytes 3145732
  22.6 51.6 %copy-start.30 = (f32[16,1024]{0,1:T(8,128)}, f32[16,1024]{0,1:T(8,128)S(1)}, u32[]{:S(2)}) copy-start(f32[16,1024]{0,1:T(8,128)S(1)} %broadcast_multiply_fusion.7) | copy-start | bytes 196612
  51.1 114.1 %copy-start.83 = (s32[16]{0:T(128)}, s32[16]{0:T(128)S(1)}, u32[]{:S(2)}) copy-start(s32[16]{0:T(128)S(1)} %broadcast_subtract_fusion) | copy-start | bytes 196
  79.5 93.5 %collective-permute-start = (bf16[2,16,48,128]{3,2,1,0:T(8,128)(2,1)}, bf16[2,16,48,128]{3,2,1,0:T(8,128)(2,1)}, u32[]{:S(2)}, u32[]{:S(2)}) collective-permute-start(bf16[2,16,48,128]{3,2,1,0:T(8,128)(2,1)} %get-tuple-element.579), channel_id=1, source_target_pairs={{0,1},{1,2},{2,3},{3,4},{4,5},{5,6},{6,7},{8,9},{9,10},{10,11},{11... | collective-permute-start | bytes 1179656 | tf_op jit(solution)/shard_map/ppermute | solution.py:26
  85.2 87.9 %collective-permute-start.1 = (bf16[2,16,48,128]{3,2,1,0:T(8,128)(2,1)}, bf16[2,16,48,128]{3,2,1,0:T(8,128)(2,1)}, u32[]{:S(2)}, u32[]{:S(2)}) collective-permute-start(bf16[2,16,48,128]{3,2,1,0:T(8,128)(2,1)} %get-tuple-element.580), channel_id=1, source_target_pairs={{1,0},{2,1},{3,2},{4,3},{5,4},{6,5},{7,6},{9,8},{10,9},{11,10},{12... | collective-permute-start | bytes 1179656 | tf_op jit(solution)/shard_map/ppermute | solution.py:29
  579.9 52.8 %slice-start.4 = ((s8[8388608]{0:T(1024)(128)(4,1)}), s8[4194304]{0:T(1024)(128)(4,1)S(1)}, s32[]{:S(2)}) async-start(s8[8388608]{0:T(1024)(128)(4,1)} %bitcast.551), calls=%async_computation.5 | async-start | bytes 8388608
  582.5 50.2 %slice-start.5 = ((s8[8388608]{0:T(1024)(128)(4,1)}), s8[4194304]{0:T(1024)(128)(4,1)S(1)}, s32[]{:S(2)}) async-start(s8[8388608]{0:T(1024)(128)(4,1)} %bitcast.551), calls=%async_computation.6 | async-start | bytes 8388608
  712.1 48.4 %slice-start.2 = ((s8[8388608]{0:T(1024)(128)(4,1)}), s8[4194304]{0:T(1024)(128)(4,1)S(1)}, s32[]{:S(2)}) async-start(s8[8388608]{0:T(1024)(128)(4,1)} %bitcast.546), calls=%async_computation.3 | async-start | bytes 8388608
  726.1 34.4 %slice-start.3 = ((s8[8388608]{0:T(1024)(128)(4,1)}), s8[4194304]{0:T(1024)(128)(4,1)S(1)}, s32[]{:S(2)}) async-start(s8[8388608]{0:T(1024)(128)(4,1)} %bitcast.546), calls=%async_computation.4 | async-start | bytes 8388608
  1575.0 96.9 %collective-permute-start.3 = (bf16[2,16,48,128]{3,2,1,0:T(8,128)(2,1)}, bf16[2,16,48,128]{3,2,1,0:T(8,128)(2,1)}, u32[]{:S(2)}, u32[]{:S(2)}) collective-permute-start(bf16[2,16,48,128]{3,2,1,0:T(8,128)(2,1)} %pad_maximum_fusion.17), channel_id=1, source_target_pairs={{0,1},{1,2},{2,3},{3,4},{4,5},{5,6},{6,7},{8,9},{9,10},{10,11},{11... | collective-permute-start | bytes 1179656 | tf_op jit(solution)/shard_map/ppermute | solution.py:37
  1581.1 84.4 %collective-permute-start.2 = (bf16[2,16,48,128]{3,2,1,0:T(8,128)(2,1)}, bf16[2,16,48,128]{3,2,1,0:T(8,128)(2,1)}, u32[]{:S(2)}, u32[]{:S(2)}) collective-permute-start(bf16[2,16,48,128]{3,2,1,0:T(8,128)(2,1)} %pad_maximum_fusion.16), channel_id=1, source_target_pairs={{1,0},{2,1},{3,2},{4,3},{5,4},{6,5},{7,6},{9,8},{10,9},{11,10},{12... | collective-permute-start | bytes 1179656 | tf_op jit(solution)/shard_map/ppermute | solution.py:37
  1611.4 48.7 %copy-start.66 = (bf16[2,1024,128]{2,1,0:T(8,128)(2,1)}, bf16[2,1024,128]{2,1,0:T(8,128)(2,1)S(1)}, u32[]{:S(2)}) copy-start(bf16[2,1024,128]{2,1,0:T(8,128)(2,1)S(1)} %copy.446) | copy-start | bytes 1572868
  1790.5 45.4 %copy-start.95 = (f32[16,4]{0,1:T(4,128)S(1)}, f32[16,4]{0,1:T(4,128)}, u32[]{:S(2)}) copy-start(f32[16,4]{0,1:T(4,128)} %param.48) | copy-start | bytes 772
  1790.5 45.4 %copy-start.100 = (f32[16,4]{0,1:T(4,128)S(1)}, f32[16,4]{0,1:T(4,128)}, u32[]{:S(2)}) copy-start(f32[16,4]{0,1:T(4,128)} %param.57) | copy-start | bytes 772
  1790.5 45.3 %copy-start.101 = (f32[16,4]{0,1:T(4,128)S(1)}, f32[16,4]{0,1:T(4,128)}, u32[]{:S(2)}) copy-start(f32[16,4]{0,1:T(4,128)} %param.54) | copy-start | bytes 772
  1790.5 45.9 %copy-start.93 = (f32[7,128]{1,0:T(8,128)S(1)}, f32[7,128]{1,0:T(8,128)}, u32[]{:S(2)}) copy-start(f32[7,128]{1,0:T(8,128)} %param.47) | copy-start | bytes 10756
  1790.5 45.9 %copy-start.96 = (f32[7,128]{1,0:T(8,128)S(1)}, f32[7,128]{1,0:T(8,128)}, u32[]{:S(2)}) copy-start(f32[7,128]{1,0:T(8,128)} %param.56) | copy-start | bytes 10756
  1790.5 45.9 %copy-start.97 = (f32[7,128]{1,0:T(8,128)S(1)}, f32[7,128]{1,0:T(8,128)}, u32[]{:S(2)}) copy-start(f32[7,128]{1,0:T(8,128)} %param.53) | copy-start | bytes 10756
  1791.5 122.0 %copy-start.78 = (f32[17,16,128]{2,1,0:T(8,128)S(1)}, f32[17,16,128]{2,1,0:T(8,128)}, u32[]{:S(2)}) copy-start(f32[17,16,128]{2,1,0:T(8,128)} %param.49) | copy-start | bytes 417796
  1835.8 84.9 %copy-start.98 = (f32[7,128]{1,0:T(8,128)}, f32[7,128]{1,0:T(8,128)S(1)}, u32[]{:S(2)}) copy-start(f32[7,128]{1,0:T(8,128)S(1)} %get-tuple-element.524) | copy-start | bytes 10756
  1835.8 84.9 %copy-start.102 = (f32[16,4]{0,1:T(4,128)}, f32[16,4]{0,1:T(4,128)S(1)}, u32[]{:S(2)}) copy-start(f32[16,4]{0,1:T(4,128)S(1)} %get-tuple-element.525) | copy-start | bytes 772
  (132 other events, 1359.9 us)
Sparse Core Ops, SparseCore 0:
  1772.3 132.6 all-reduce.4
where the time goes:
time: 1950 us; the launch traced here: 1930 us
  matrix products  838 us (43%)
  local copies, waits for them, and re-layouts  558 us (29%)
  other arithmetic  382 us (20%)
  waiting for transfers between devices  68 us (3%)
  blocking collectives  41.2 us (2%)
    dot_general x8, matrix products, block_scores(): jnp.einsum('gs,shwqk->gwhqk', onehot_blk, bias_table, precision=high)  163 us
    concatenate x16, local copies, waits for them, and re-layouts, key_windows(): jnp.concatenate([blocks[:, offset:offset + count] for offset in range(4)]...  102 us
    dot_general x8, matrix products, block_scores(): jnp.einsum('gwqhd,gwkhd->gwhqk', query_heads, key_heads, preferred_elemen...  97.4 us
    dynamic_update_slice x12, local copies, waits for them, and re-layouts, body(): lax.scan(backward_block, jnp.zeros((struct_dev, HEADS, count, QW, KW), f3...  94.9 us
    dynamic_update_slice x16, local copies, waits for them, and re-layouts, body(): lax.scan(forward_block, jnp.zeros((), f32), (split(queries), split(key_pa...  76.1 us
    psum x1, waiting for transfers between devices, body(): lax.psum((grad_w, grad_vec, grad_pw), ('samp', 'win'))  67.9 us
    dot_general x6, matrix products, select(): return jnp.einsum('gs,sac->gac', onehot, table, precision=high)  67.7 us
    reduce_sum x3, other arithmetic, layer_stats(): jnp.mean(center * center, axis=-1, keepdims=True) + 1e-05  58.4 us
  transfers between devices with their start and end apart: 5, of which 1 were waited for; matrix products, arithmetic and copies ran while one was open for 10% of the time, Pallas kernels for 0%

commit v1 on v0

v1 whole, which is shorter than its diff:
```python
import functools
import math

import jax
import jax.numpy as jnp
from jax import lax
from jax.experimental import pallas as pl
from jax.experimental.pallas import tpu as pltpu
from jax.sharding import PartitionSpec as P

HEADS = 4
FF = 256
QW = 32
HALO = 48
KW = 128
C = 128
PAIR = 16
NBLK = 17
GROUP = 4

stat_decay = 0.5
ema_decay = 0.8
matrix_rate = 1.0
vector_rate = 0.2

F32 = jnp.float32
BF16 = jnp.bfloat16
LOG2E = math.log2(math.e)
FACTOR = 1.0 / math.sqrt(C // HEADS)
INVALID = -1000000000.0
VMEM_LIMIT = 60 * 1024 * 1024


def dot(left, right):
    return lax.dot_general(left, right, (((1,), (0,)), ((), ())), preferred_element_type=F32)


def dot_nt(left, right):
    return lax.dot_general(left, right, (((1,), (1,)), ((), ())), preferred_element_type=F32)


def dot_tn(left, right):
    return lax.dot_general(left, right, (((0,), (0,)), ((), ())), preferred_element_type=F32)


def layer_stats(values):
    center = values - jnp.mean(values, axis=-1, keepdims=True)
    inverse = lax.rsqrt(jnp.mean(center * center, axis=-1, keepdims=True) + 1e-05)
    return (center * inverse, inverse)


def layer_back(normed, inverse, grad_norm):
    return inverse * (
        grad_norm
        - jnp.mean(grad_norm, axis=-1, keepdims=True)
        - normed * jnp.mean(grad_norm * normed, axis=-1, keepdims=True)
    )


def rows_sum(values):
    return jnp.sum(values, axis=0, keepdims=True)


def normed_channels(scratch, start):
    channels = [scratch[pl.ds(start + c, 8, stride=PAIR), :] for c in range(PAIR)]
    mean = sum(channels[1:], channels[0]) * (1.0 / PAIR)
    center = [channel - mean for channel in channels]
    squares = [part * part for part in center]
    spread = sum(squares[1:], squares[0]) * (1.0 / PAIR)
    return center, lax.rsqrt(spread + 1e-05)


def bias_kernel(base_ref, pair_ref, pw_ref, bias_ref, flat, tile):
    group = pl.program_id(1)
    flat[...] = pair_ref[0].astype(F32).reshape(flat.shape)
    for w in range(GROUP):
        for part in range(QW // 8):
            center, inverse = normed_channels(flat, (w * QW + part * 8) * PAIR)
            for h in range(HEADS):
                terms = [center[c] * pw_ref[c, h] for c in range(PAIR)]
                total = sum(terms[1:], terms[0]) * inverse
                tile[w, h * QW + part * 8 : h * QW + part * 8 + 8, :] = total
    for w in range(GROUP):
        start = base_ref[0] + (group * GROUP + w) * QW - HALO
        position = start + lax.broadcasted_iota(jnp.int32, (KW, C), 0)
        valid = (position >= 0) & (position < base_ref[1])
        bias_ref[0, w] = jnp.where(valid, tile[w].T * LOG2E, INVALID * LOG2E)


def bias_table(base, pair, pair_weight):
    structs, atoms = pair.shape[:2]
    rows = GROUP * QW
    return pl.pallas_call(
        bias_kernel,
        grid_spec=pltpu.PrefetchScalarGridSpec(
            num_scalar_prefetch=1,
            grid=(structs, atoms // rows),
            in_specs=[
                pl.BlockSpec((1, rows, PAIR, KW), lambda s, i, _: (s, i, 0, 0)),
                pl.BlockSpec(memory_space=pltpu.SMEM),
            ],
            out_specs=pl.BlockSpec((1, GROUP, KW, C), lambda s, i, _: (s, i, 0, 0)),
            scratch_shapes=[
                pltpu.VMEM((rows * PAIR, KW), F32),
                pltpu.VMEM((GROUP, C, KW), F32),
            ],
        ),
        out_shape=jax.ShapeDtypeStruct((structs, atoms // QW, KW, C), F32),
        compiler_params=pltpu.CompilerParams(vmem_limit_bytes=VMEM_LIMIT),
        cost_estimate=pl.CostEstimate(flops=10**8, bytes_accessed=13 * 2**20, transcendentals=0),
        name="pair_bias",
    )(base, pair, pair_weight)


def pair_grad_kernel(pair_ref, dbias_ref, out_ref, flat, tile):
    first = (pl.program_id(0) == 0) & (pl.program_id(1) == 0)

    @pl.when(first)
    def _():
        out_ref[...] = jnp.zeros_like(out_ref)

    flat[...] = pair_ref[0].astype(F32).reshape(flat.shape)
    for w in range(GROUP):
        tile[w] = dbias_ref[0, w].T
    for w in range(GROUP):
        for part in range(QW // 8):
            center, inverse = normed_channels(flat, (w * QW + part * 8) * PAIR)
            for h in range(HEADS):
                grad = tile[w, h * QW + part * 8 : h * QW + part * 8 + 8, :] * inverse
                for c in range(PAIR):
                    out_ref[c * HEADS + h] += center[c] * grad


def pair_grad(pair, dbias):
    structs, atoms = pair.shape[:2]
    rows = GROUP * QW
    return pl.pallas_call(
        pair_grad_kernel,
        grid=(structs, atoms // rows),
        in_specs=[
            pl.BlockSpec((1, rows, PAIR, KW), lambda s, i: (s, i, 0, 0)),
            pl.BlockSpec((1, GROUP, KW, C), lambda s, i: (s, i, 0, 0)),
        ],
        out_specs=pl.BlockSpec((PAIR * HEADS, 8, KW), lambda s, i: (0, 0, 0)),
        scratch_shapes=[
            pltpu.VMEM((rows * PAIR, KW), F32),
            pltpu.VMEM((GROUP, C, KW), F32),
        ],
        out_shape=jax.ShapeDtypeStruct((PAIR * HEADS, 8, KW), F32),
        compiler_params=pltpu.CompilerParams(vmem_limit_bytes=VMEM_LIMIT),
        cost_estimate=pl.CostEstimate(flops=10**8, bytes_accessed=13 * 2**20, transcendentals=0),
        name="pair_grad",
    )(pair, dbias)


def main_kernel(
    ids_ref,
    x_ref,
    xlo_ref,
    xhi_ref,
    g_ref,
    bias_ref,
    cond_ref,
    clo_ref,
    chi_ref,
    w_ref,
    vec_ref,
    out_ref,
    grad_ref,
    gxb_ref,
    rlo_ref,
    rhi_ref,
    dbias_ref,
    gw_ref,
    dvec_ref,
    accb_ref,
    tabb_ref,
    wq,
    w6,
    win,
    wo,
    wc1,
    wc2,
    mask,
    t_s1,
    t_h1,
    t_hs,
    t_hh,
    t_g1,
    t_s2,
    t_h2,
    t_g2,
    a_s1,
    a_h1,
    a_g1,
    a_s2,
    a_h2,
    a_g2,
    k_scr,
    v_scr,
    q_scr,
    gate_scr,
    ada_scr,
    n1_scr,
    inv_scr,
    o_scr,
    p_scr,
    do_scr,
    dd_scr,
    d4_scr,
    dk_scr,
    dv_scr,
    dx_scr,
):
    step = pl.program_id(0)
    structs, atoms, _ = cond_ref.shape
    windows = atoms // QW
    tile = min(256, atoms)
    tiles = atoms // tile
    s = ids_ref[step]

    def cond_rows(source):
        normed, _ = layer_stats(source)
        one = (normed * vec_ref[0:1]).astype(BF16)
        two = (normed * vec_ref[4:5]).astype(BF16)
        return normed, one, two

    @pl.when(step == 0)
    def _():
        def low(b):
            return w_ref[b].astype(BF16)

        for at, b in enumerate((2, 5, 3, 4)):
            wq[:, at * C : at * C + C] = low(b)
        w6[...] = low(6)
        for at in range(4):
            win[:, at * C : at * C + C] = low(11 + at)
        for at in range(2):
            wo[at * C : at * C + C, :] = low(15 + at)
        for at, b in enumerate((0, 1, 7)):
            wc1[:, at * C : at * C + C] = low(b)
        for at, b in enumerate((8, 9, 10)):
            wc2[:, at * C : at * C + C] = low(b)
        rows_head = lax.broadcasted_iota(jnp.int32, (C, C), 0) // QW
        lane_head = lax.broadcasted_iota(jnp.int32, (C, C), 1) // (C // HEADS)
        mask[...] = jnp.where(rows_head == lane_head, 1.0, 0.0).astype(BF16)
        for acc in (a_s1, a_h1, a_g1, a_s2, a_h2, a_g2, gw_ref, dvec_ref):
            acc[...] = jnp.zeros_like(acc)
        dbias_ref[...] = jnp.zeros_like(dbias_ref)
        for st in range(structs):

            def table(i, carry):
                rows = pl.ds(pl.multiple_of(i * tile, tile), tile)
                _, one, two = cond_rows(cond_ref[st, rows])
                first = dot(one, wc1[...])
                t_s1[st, rows] = jax.nn.sigmoid(first[:, :C] + vec_ref[1:2])
                t_h1[st, rows] = first[:, C : 2 * C]
                t_g1[st, rows] = jax.nn.sigmoid(first[:, 2 * C :] + vec_ref[3:4])
                second = dot(two, wc2[...])
                t_s2[st, rows] = jax.nn.sigmoid(second[:, :C] + vec_ref[5:6])
                t_h2[st, rows] = second[:, C : 2 * C]
                t_g2[st, rows] = jax.nn.sigmoid(second[:, 2 * C :] + vec_ref[6:7])
                return carry

            lax.fori_loop(0, tiles, table, 0)
            _, one, _ = cond_rows(jnp.concatenate([clo_ref[st], chi_ref[st]], axis=0))
            first = dot(one, wc1[:, : 2 * C])
            t_hs[st] = jax.nn.sigmoid(first[:, :C] + vec_ref[1:2])
            t_hh[st] = first[:, C:]
            tabb_ref[0, st, :HALO] = t_s1[st, :HALO]
            tabb_ref[0, st, HALO:] = t_s1[st, atoms - HALO :]
            tabb_ref[1, st, :HALO] = t_h1[st, :HALO]
            tabb_ref[1, st, HALO:] = t_h1[st, atoms - HALO :]

    def project(i, carry):
        start = pl.multiple_of(i * tile, tile)
        rows = pl.ds(start, tile)
        normed, inverse = layer_stats(x_ref[0, rows].astype(F32))
        n1_scr[rows] = normed
        inv_scr[rows] = jnp.broadcast_to(inverse, (tile, C))
        ada = (t_s1[s, rows] * normed + t_h1[s, rows]).astype(BF16)
        ada_scr[rows] = ada
        out = dot(ada, wq[...])
        q_scr[rows] = (out[:, :C] + vec_ref[2:3]).astype(BF16)
        gate_scr[rows] = jax.nn.sigmoid(out[:, C : 2 * C])
        pad = pl.ds(pl.multiple_of(start + HALO, 16), tile)
        k_scr[pad] = out[:, 2 * C : 3 * C].astype(BF16)
        v_scr[pad] = out[:, 3 * C :].astype(BF16)
        return carry

    lax.fori_loop(0, tiles, project, 0)
    halo = jnp.concatenate([xlo_ref[0], xhi_ref[0]], axis=0).astype(F32)
    normed, _ = layer_stats(halo)
    out = dot((t_hs[s] * normed + t_hh[s]).astype(BF16), wq[:, 2 * C :])
    k_scr[:HALO] = out[:HALO, :C].astype(BF16)
    v_scr[:HALO] = out[:HALO, C:].astype(BF16)
    k_scr[HALO + atoms :] = out[HALO:, :C].astype(BF16)
    v_scr[HALO + atoms :] = out[HALO:, C:].astype(BF16)

    lane_head = lax.broadcasted_iota(jnp.int32, (QW, C), 1) // (C // HEADS)

    def spread(rows):
        return jnp.concatenate([rows] * HEADS, axis=0) * mask[...]

    def gathered(full):
        parts = [full[h * QW : h * QW + QW] for h in range(HEADS)]
        last = parts[HEADS - 1]
        for h in range(HEADS - 2, -1, -1):
            last = jnp.where(lane_head == h, parts[h], last)
        return last

    def attend(i, carry):
        spans = []
        scores = []
        for u in range(GROUP):
            w = i * GROUP + u
            start = pl.multiple_of(w * QW, QW)
            spans.append((w, start))
            queries = spread(q_scr[pl.ds(start, QW)])
            scores.append(dot_nt(k_scr[pl.ds(start, KW)], queries))
        probs = []
        for u in range(GROUP):
            value = scores[u] * (FACTOR * LOG2E) + bias_ref[s, spans[u][0]]
            exps = jnp.exp2(value - jnp.max(value, axis=0, keepdims=True))
            prob = (exps * (1.0 / rows_sum(exps))).astype(BF16)
            p_scr[spans[u][0]] = prob
            probs.append(prob)
        for u in range(GROUP):
            start = spans[u][1]
            o_scr[pl.ds(start, QW)] = gathered(dot_tn(probs[u], v_scr[pl.ds(start, KW)]))
        return carry

    lax.fori_loop(0, windows // GROUP, attend, 0)

    def middle(i, carry):
        rows = pl.ds(pl.multiple_of(i * tile, tile), tile)
        gate = gate_scr[rows]
        mixed = o_scr[rows]
        y = (gate * mixed).astype(BF16)
        attn = dot(y, w6[...])
        gate_one = t_g1[s, rows]
        x1 = x_ref[0, rows].astype(F32) + gate_one * attn
        normed, inverse = layer_stats(x1)
        scale_two = t_s2[s, rows]
        ada = (scale_two * normed + t_h2[s, rows]).astype(BF16)
        expand = dot(ada, win[...])
        a = expand[:, :FF]
        b = expand[:, FF:]
        sig = jax.nn.sigmoid(a)
        silu = a * sig
        hid = (silu * b).astype(BF16)
        ff = dot(hid, wo[...])
        gate_two = t_g2[s, rows]
        out_ref[0, rows] = (x1 + gate_two * ff).astype(BF16)
        g = g_ref[0, rows].astype(F32)
        a_g2[s, rows] += g * ff
        dff = (g * gate_two).astype(BF16)
        dwo = dot_tn(dff, hid)
        gw_ref[15] += dwo[:, :C]
        gw_ref[16] += dwo[:, C:]
        dhid = dot_nt(dff, wo[...])
        da = (dhid * b * (sig + silu * (1.0 - sig))).astype(BF16)
        db = (dhid * silu).astype(BF16)
        dab = jnp.concatenate([da, db], axis=1)
        dwin = dot_tn(ada, dab)
        for at in range(4):
            gw_ref[11 + at] += dwin[:, at * C : at * C + C]
        dada = dot_nt(dab, win[...])
        a_s2[s, rows] += dada * normed
        a_h2[s, rows] += dada
        dx1 = g + layer_back(normed, inverse, dada * scale_two)
        dx_scr[rows] = dx1
        a_g1[s, rows] += dx1 * attn
        dattn = (dx1 * gate_one).astype(BF16)
        gw_ref[6] += dot_tn(y, dattn)
        dy = dot_nt(dattn, w6[...])
        do = (dy * gate).astype(BF16)
        do_scr[rows] = do
        dd_scr[rows] = (do.astype(F32) * mixed * -1.0).astype(BF16)
        d4_scr[rows, C : 2 * C] = (dy * mixed * gate * (1.0 - gate)).astype(BF16)
        return carry

    lax.fori_loop(0, tiles, middle, 0)

    dk_scr[...] = jnp.zeros_like(dk_scr)
    dv_scr[...] = jnp.zeros_like(dv_scr)
    ones = jnp.ones((KW, C), BF16)

    def attend_back(i, carry):
        items = []
        for u in range(GROUP):
            w = i * GROUP + u
            start = pl.multiple_of(w * QW, QW)
            dox = spread(do_scr[pl.ds(start, QW)])
            ddx = spread(dd_scr[pl.ds(start, QW)])
            values = jnp.concatenate([v_scr[pl.ds(start, KW)], ones], axis=1)
            diff = dot_nt(values, jnp.concatenate([dox, ddx], axis=1))
            items.append((w, start, dox, diff))
        grads = []
        for w, start, dox, diff in items:
            ds = p_scr[w] * diff.astype(BF16)
            dbias_ref[s, w] += ds.astype(F32)
            grads.append(ds)
        for u in range(GROUP):
            w, start, dox, _ = items[u]
            keys = pl.ds(start, KW)
            dq = gathered(dot_tn(grads[u], k_scr[keys])) * FACTOR
            dvec_ref[2] += jnp.sum(dq.reshape(QW // 8, 8, C), axis=0)
            d4_scr[pl.ds(start, QW), :C] = dq.astype(BF16)
            dk_scr[keys] += dot(grads[u], spread(q_scr[pl.ds(start, QW)]))
            dv_scr[keys] += dot(p_scr[w], dox)
        return carry

    lax.fori_loop(0, windows // GROUP, attend_back, 0)

    def finish(i, carry):
        start = pl.multiple_of(i * tile, tile)
        rows = pl.ds(start, tile)
        pad = pl.ds(pl.multiple_of(start + HALO, 16), tile)
        d4_scr[rows, 2 * C : 3 * C] = (dk_scr[pad] * FACTOR).astype(BF16)
        d4_scr[rows, 3 * C :] = dv_scr[pad].astype(BF16)
        d4 = d4_scr[rows]
        dwq = dot_tn(ada_scr[rows], d4)
        for at, b in enumerate((2, 5, 3, 4)):
            gw_ref[b] += dwq[:, at * C : at * C + C]
        dada = dot_nt(d4, wq[...])
        normed = n1_scr[rows]
        a_s1[s, rows] += dada * normed
        a_h1[s, rows] += dada
        grad = dx_scr[rows] + layer_back(normed, inv_scr[rows], dada * t_s1[s, rows])
        dx_scr[rows] = grad
        grad_ref[0, rows] = grad.astype(BF16)
        return carry

    lax.fori_loop(0, tiles, finish, 0)
    gxb_ref[0, :HALO] = dx_scr[:HALO]
    gxb_ref[0, HALO:] = dx_scr[atoms - HALO :]
    rlo_ref[0, 0] = (dk_scr[:HALO] * FACTOR).astype(BF16)
    rlo_ref[0, 1] = dv_scr[:HALO].astype(BF16)
    rhi_ref[0, 0] = (dk_scr[HALO + atoms :] * FACTOR).astype(BF16)
    rhi_ref[0, 1] = dv_scr[HALO + atoms :].astype(BF16)

    @pl.when(step == pl.num_programs(0) - 1)
    def _():
        for b in (15, 16):
            gw_ref[b] = gw_ref[b].T
        for st in range(structs):
            accb_ref[0, st, :HALO] = a_s1[st, :HALO]
            accb_ref[0, st, HALO:] = a_s1[st, atoms - HALO :]
            accb_ref[1, st, :HALO] = a_h1[st, :HALO]
            accb_ref[1, st, HALO:] = a_h1[st, atoms - HALO :]
            for acc in (a_s1, a_h1):
                acc[st, :HALO] = jnp.zeros((HALO, C), F32)
                acc[st, atoms - HALO :] = jnp.zeros((HALO, C), F32)

            def conditioning(i, carry):
                rows = pl.ds(pl.multiple_of(i * tile, tile), tile)
                normed, one, two = cond_rows(cond_ref[st, rows])

                def pre(acc, gate):
                    return (acc[st, rows] * gate[st, rows] * (1.0 - gate[st, rows])).astype(BF16)

                first = [pre(a_s1, t_s1), a_h1[st, rows].astype(BF16), pre(a_g1, t_g1)]
                second = [pre(a_s2, t_s2), a_h2[st, rows].astype(BF16), pre(a_g2, t_g2)]
                for at, part in ((1, first[0]), (3, first[2]), (5, second[0]), (6, second[2])):
                    dvec_ref[at] += jnp.sum(part.astype(F32).reshape(tile // 8, 8, C), axis=0)
                for at, source, parts, weight, blocks in (
                    (0, one, first, wc1, (0, 1, 7)),
                    (4, two, second, wc2, (8, 9, 10)),
                ):
                    joined = jnp.concatenate(parts, axis=1)
                    grads = dot_tn(source, joined)
                    for j, b in enumerate(blocks):
                        gw_ref[b] += grads[:, j * C : j * C + C]
                    back = dot_nt(joined, weight[...]) * normed
                    dvec_ref[at] += jnp.sum(back.reshape(tile // 8, 8, C), axis=0)
                return carry

            lax.fori_loop(0, tiles, conditioning, 0)


def main_call(ids, atoms, xlo, xhi, cotangent, bias, cond, clo, chi, weights, vectors):
    samples, rows, _ = atoms.shape
    structs = cond.shape[0]
    windows = rows // QW
    padded = rows + 2 * HALO

    def per_sample(*shape):
        zeros = (0,) * len(shape)
        return pl.BlockSpec((1,) + shape, lambda i, _: (i,) + zeros)

    def whole(*shape):
        zeros = (0,) * len(shape)
        return pl.BlockSpec(shape, lambda i, _: zeros, pipeline_mode=pl.Buffered(1))

    def table(count=rows):
        return pltpu.VMEM((structs, count, C), F32)

    shape = jax.ShapeDtypeStruct
    return pl.pallas_call(
        main_kernel,
        grid_spec=pltpu.PrefetchScalarGridSpec(
            num_scalar_prefetch=1,
            grid=(samples,),
            in_specs=[
                per_sample(rows, C),
                per_sample(HALO, C),
                per_sample(HALO, C),
                per_sample(rows, C),
                whole(structs, windows, KW, C),
                whole(structs, rows, C),
                whole(structs, HALO, C),
                whole(structs, HALO, C),
                whole(NBLK, C, C),
                whole(7, C),
            ],
            out_specs=[
                per_sample(rows, C),
                per_sample(rows, C),
                per_sample(2 * HALO, C),
                per_sample(2, HALO, C),
                per_sample(2, HALO, C),
                whole(structs, windows, KW, C),
                whole(NBLK, C, C),
                whole(7, 8, C),
                whole(2, structs, 2 * HALO, C),
                whole(2, structs, 2 * HALO, C),
            ],
            scratch_shapes=[
                pltpu.VMEM((C, 4 * C), BF16),
                pltpu.VMEM((C, C), BF16),
                pltpu.VMEM((C, 2 * FF), BF16),
                pltpu.VMEM((FF, C), BF16),
                pltpu.VMEM((C, 3 * C), BF16),
                pltpu.VMEM((C, 3 * C), BF16),
                pltpu.VMEM((C, C), BF16),
                table(),
                table(),
                table(2 * HALO),
                table(2 * HALO),
                table(),
                table(),
                table(),
                table(),
                table(),
                table(),
                table(),
                table(),
                table(),
                table(),
                pltpu.VMEM((padded, C), BF16),
                pltpu.VMEM((padded, C), BF16),
                pltpu.VMEM((rows, C), BF16),
                pltpu.VMEM((rows, C), F32),
                pltpu.VMEM((rows, C), BF16),
                pltpu.VMEM((rows, C), F32),
                pltpu.VMEM((rows, C), F32),
                pltpu.VMEM((rows, C), F32),
                pltpu.VMEM((windows, KW, C), BF16),
                pltpu.VMEM((rows, C), BF16),
                pltpu.VMEM((rows, C), BF16),
                pltpu.VMEM((rows, 4 * C), BF16),
                pltpu.VMEM((padded, C), F32),
                pltpu.VMEM((padded, C), F32),
                pltpu.VMEM((rows, C), F32),
            ],
        ),
        out_shape=[
            shape((samples, rows, C), BF16),
            shape((samples, rows, C), BF16),
            shape((samples, 2 * HALO, C), F32),
            shape((samples, 2, HALO, C), BF16),
            shape((samples, 2, HALO, C), BF16),
            shape((structs, windows, KW, C), F32),
            shape((NBLK, C, C), F32),
            shape((7, 8, C), F32),
            shape((2, structs, 2 * HALO, C), F32),
            shape((2, structs, 2 * HALO, C), F32),
        ],
        compiler_params=pltpu.CompilerParams(vmem_limit_bytes=VMEM_LIMIT),
        name="block",
    )(ids, atoms, xlo, xhi, cotangent, bias, cond, clo, chi, weights, vectors)


def rim_kernel(
    ids_ref,
    below_ref,
    above_ref,
    xlo_ref,
    xhi_ref,
    gxb_ref,
    tab_ref,
    acc_ref,
    cond_ref,
    w_ref,
    vec_ref,
    gw_ref,
    dvec_ref,
    grad_ref,
    gwo_ref,
    dveco_ref,
    sums,
    dw,
):
    samples = xlo_ref.shape[0]
    structs = cond_ref.shape[0]
    sums[...] = acc_ref[...]
    dw[...] = jnp.zeros_like(dw)
    weight = jnp.concatenate([w_ref[3], w_ref[4]], axis=1).astype(BF16)

    def one(i, carry):
        s = ids_ref[i]
        x = jnp.concatenate([xlo_ref[i], xhi_ref[i]], axis=0).astype(F32)
        normed, inverse = layer_stats(x)
        scale = tab_ref[0, s]
        ada = (scale * normed + tab_ref[1, s]).astype(BF16)
        dkv = jnp.concatenate(
            [
                jnp.concatenate([below_ref[i, 0], above_ref[i, 0]], axis=0),
                jnp.concatenate([below_ref[i, 1], above_ref[i, 1]], axis=0),
            ],
            axis=1,
        )
        dw[...] += dot_tn(ada, dkv)
        dada = dot_nt(dkv, weight)
        sums[0, s] += dada * normed
        sums[1, s] += dada
        grad_ref[i] = (gxb_ref[i] + layer_back(normed, inverse, dada * scale)).astype(BF16)
        return carry

    lax.fori_loop(0, samples, one, 0)
    gwo_ref[...] = gw_ref[...]
    gwo_ref[3] += dw[:, :C]
    gwo_ref[4] += dw[:, C:]
    dveco_ref[...] = dvec_ref[...]
    weight = jnp.concatenate([w_ref[0], w_ref[1]], axis=1).astype(BF16)
    for st in range(structs):
        normed, _ = layer_stats(cond_ref[st])
        source = (normed * vec_ref[0:1]).astype(BF16)
        scale = tab_ref[0, st]
        pre_scale = (sums[0, st] * scale * (1.0 - scale)).astype(BF16)
        pre_shift = sums[1, st].astype(BF16)
        joined = jnp.concatenate([pre_scale, pre_shift], axis=1)
        grads = dot_tn(source, joined)
        gwo_ref[0] += grads[:, :C]
        gwo_ref[1] += grads[:, C:]
        back = dot_nt(joined, weight) * normed
        dveco_ref[0] += jnp.sum(back.reshape(2 * HALO // 8, 8, C), axis=0)
        dveco_ref[1] += jnp.sum(pre_scale.astype(F32).reshape(2 * HALO // 8, 8, C), axis=0)


def rim_call(ids, below, above, xlo, xhi, gxb, tab, acc, cond, weights, vectors, gw, dvec):
    samples = xlo.shape[0]
    structs = cond.shape[0]
    full = pl.BlockSpec(memory_space=pltpu.VMEM)
    shape = jax.ShapeDtypeStruct
    return pl.pallas_call(
        rim_kernel,
        in_specs=[pl.BlockSpec(memory_space=pltpu.SMEM)] + [full] * 12,
        out_specs=[full] * 3,
        out_shape=[
            shape((samples, 2 * HALO, C), BF16),
            shape((NBLK, C, C), F32),
            shape((7, 8, C), F32),
        ],
        scratch_shapes=[
            pltpu.VMEM((2, structs, 2 * HALO, C), F32),
            pltpu.VMEM((C, 2 * C), F32),
        ],
        compiler_params=pltpu.CompilerParams(vmem_limit_bytes=VMEM_LIMIT),
        name="rims",
    )(ids, below, above, xlo, xhi, gxb, tab, acc, cond, weights, vectors, gw, dvec)


def passed(shard, by):
    devices = lax.axis_size("win")
    pairs = [(i, i + by) for i in range(devices) if 0 <= i + by < devices]
    return lax.ppermute(shard, "win", pairs)


def body(
    atoms,
    cond,
    pair,
    struct_ids,
    cotangent,
    weights,
    vectors,
    pair_weight,
    stat_left,
    stat_right,
    root_left,
    root_right,
    stat_vectors,
    stat_pair,
    ema_weights,
    ema_vectors,
    ema_pair,
):
    high = lax.Precision.HIGHEST
    rows = atoms.shape[1]
    struct_dev = cond.shape[0]
    win_index = lax.axis_index("win")
    win_count = lax.axis_size("win")
    ids = struct_ids - lax.axis_index("samp") * struct_dev
    x_first, x_last = atoms[:, :HALO], atoms[:, rows - HALO :]
    c_first, c_last = cond[:, :HALO], cond[:, rows - HALO :]
    xlo, xhi = passed(x_last, 1), passed(x_first, -1)
    clo, chi = passed(c_last, 1), passed(c_first, -1)
    base = jnp.stack([win_index * rows, jnp.int32(rows * win_count)]).astype(jnp.int32)
    bias = bias_table(base, pair, pair_weight)
    (result, grad_atoms, gxb, rim_low, rim_high, dbias, gw, dvec, accb, tabb) = main_call(
        ids, atoms, xlo, xhi, cotangent, bias, cond, clo, chi, weights, vectors
    )
    above = passed(rim_low, -1)
    below = passed(rim_high, 1)
    dpair = pair_grad(pair, dbias)
    cond_rim = jnp.concatenate([c_first, c_last], axis=1)
    grad_rim, gw, dvec = rim_call(
        ids, below, above, x_first, x_last, gxb, tabb, accb, cond_rim, weights, vectors, gw, dvec
    )
    grad_atoms = grad_atoms.at[:, :HALO].set(grad_rim[:, :HALO])
    grad_atoms = grad_atoms.at[:, rows - HALO :].set(grad_rim[:, HALO:])
    total_w, total_v, total_p = lax.psum(
        (gw, jnp.sum(dvec, axis=1), jnp.sum(dpair, axis=(1, 2)).reshape(PAIR, HEADS)),
        ("samp", "win"),
    )
    own_count = stat_left.shape[1]
    row_start = win_index * own_count
    own_rows = lax.dynamic_slice_in_dim(total_w, row_start, own_count, 1)
    own_cols = lax.dynamic_slice_in_dim(total_w, row_start, own_count, 2)
    left_new = stat_decay * stat_left + (1.0 - stat_decay) * jnp.einsum(
        "bic,bjc->bij", own_rows, total_w, precision=high
    )
    right_new = stat_decay * stat_right + (1.0 - stat_decay) * jnp.einsum(
        "bci,bcj->bij", own_cols, total_w, precision=high
    )
    left_part = jnp.einsum("bij,bjk->bik", root_left, total_w, precision=high)
    update_step = jnp.einsum("bik,bkl->bil", left_part, root_right, precision=high)
    weight_rows = lax.dynamic_slice_in_dim(weights, row_start, own_count, 1)
    weights_new = weight_rows - matrix_rate * update_step
    stat_v_new = stat_decay * stat_vectors + (1.0 - stat_decay) * total_v * total_v
    vectors_new = vectors - vector_rate * total_v * lax.rsqrt(stat_v_new)
    stat_p_new = stat_decay * stat_pair + (1.0 - stat_decay) * total_p * total_p
    pair_new = pair_weight - vector_rate * total_p * lax.rsqrt(stat_p_new)
    return (
        result,
        grad_atoms,
        own_rows,
        total_v,
        total_p,
        left_new,
        right_new,
        weights_new,
        weights_new.astype(BF16),
        vectors_new,
        pair_new,
        stat_v_new,
        stat_p_new,
        ema_decay * ema_weights + (1.0 - ema_decay) * weights_new,
        ema_decay * ema_vectors + (1.0 - ema_decay) * vectors_new,
        ema_decay * ema_pair + (1.0 - ema_decay) * pair_new,
    )


def solution(mesh):
    placed = (
        P("samp", "win", None),
        P("samp", "win", None),
        P("samp", "win", None, None),
        P("samp"),
        P("samp", "win", None),
        P(),
        P(),
        P(),
        P(None, "win", None),
        P(None, "win", None),
        P(None, "win", None),
        P(),
        P(),
        P(),
        P(None, "win", None),
        P(),
        P(),
    )
    return jax.shard_map(
        body,
        mesh=mesh,
        in_specs=placed,
        out_specs=(
            P("samp", "win", None),
            P("samp", "win", None),
            P(None, "win", None),
            P(),
            P(),
            P(None, "win", None),
            P(None, "win", None),
            P(None, "win", None),
            P(None, "win", None),
            P(),
            P(),
            P(),
            P(),
            P(None, "win", None),
            P(),
            P(),
        ),
        check_vma=False,
    )
```

time: 1950 us -> 509 us (0.26); the launches traced: 1930 us -> 507 us
  matrix products: 838 us -> 10.5 us
  local copies, waits for them, and re-layouts: 558 us -> 7.92 us
  other arithmetic: 382 us -> 5.12 us
  Pallas kernels: 0 us -> 321 us
    dot_general x81 -> x0, matrix products: 824 us -> none  [the longest x8 163 us: block_scores(): jnp.einsum('gs,shwqk->gwhqk', onehot_blk, bias_table, precision=high)]
    pallas_call x0 -> x4, Pallas kernels: none -> 321 us  [the longest x1 275 us: main_call(): pl.pallas_call(main_kernel, grid_spec=pltpu.PrefetchScalarGridSpec(num_sc...]
    dynamic_update_slice x28 -> x0, local copies, waits for them, and re-layouts: 171 us -> none  [the longest x12 94.9 us: body(): lax.scan(backward_block, jnp.zeros((struct_dev, HEADS, count, QW, KW), f3...]
    concatenate x18 -> x0, local copies, waits for them, and re-layouts: 126 us -> none  [the longest x16 102 us: key_windows(): jnp.concatenate([blocks[:, offset:offset + count] for offset in range(4)]...]
    reduce_sum x16 -> x2, other arithmetic: 114 us -> 1.52 us  [the longest x1 1.5 us: body(): jnp.sum(dpair, axis=(1, 2)).reshape(PAIR, HEADS)]
    convert_element_type x13 -> x0, other arithmetic: 102 us -> none  [the longest x4 42.6 us: backward_block(): value_slot = jnp.where(valid_slot, grad_values.reshape(group_size, count,...]
    reshape x17 -> x2, local copies, waits for them, and re-layouts: 90.4 us -> 0.16 us  [body(): jnp.sum(dpair, axis=(1, 2)).reshape(PAIR, HEADS)]
    concatenate x18 -> x1, other arithmetic: 53.9 us -> 0.65 us  [body(): cond_rim = jnp.concatenate([c_first, c_last], axis=1)]
  transfers between devices with their start and end apart: 5 -> 7, of which waited for: 1 -> 1; matrix products, arithmetic and copies ran while one was open for 10% -> 2% of each run, Pallas kernels for 0% -> 7%
where the time goes in v1:
time: 509 us; the launch traced here: 507 us
  Pallas kernels  321 us (63%)
  waiting for transfers between devices  86.6 us (17%)
  blocking collectives  42.1 us (8%)
  starting transfers between devices  19.7 us (4%)
  between operations  14.4 us (3%)
  matrix products  10.5 us (2%)
  local copies, waits for them, and re-layouts  7.92 us (2%)
  other arithmetic  5.12 us (1%)
    pallas_call x1, Pallas kernels, main_call(): pl.pallas_call(main_kernel, grid_spec=pltpu.PrefetchScalarGridSpec(num_sc...  275 us
    psum x1, waiting for transfers between devices, body(): lax.psum((gw, jnp.sum(dvec, axis=1), jnp.sum(dpair, axis=(1, 2)).reshape(...  86.5 us
    psum x1, blocking collectives, body(): lax.psum((gw, jnp.sum(dvec, axis=1), jnp.sum(dpair, axis=(1, 2)).reshape(...  42.1 us
    ppermute x6, starting transfers between devices, passed(): return lax.ppermute(shard, 'win', pairs)  19.7 us
    pallas_call x1, Pallas kernels, bias_table(): pl.pallas_call(bias_kernel, grid_spec=pltpu.PrefetchScalarGridSpec(num_sc...  17.8 us
    pallas_call x1, Pallas kernels, pair_grad(): pl.pallas_call(pair_grad_kernel, grid=(structs, atoms // rows), in_specs=...  17.1 us
    pallas_call x1, Pallas kernels, rim_call(): pl.pallas_call(rim_kernel, in_specs=[pl.BlockSpec(memory_space=pltpu.SMEM...  11.4 us
  transfers between devices with their start and end apart: 7, of which 1 were waited for; matrix products, arithmetic and copies ran while one was open for 2% of the time, Pallas kernels for 7%

profile of v1, /device:TPU:0, one launch (start us, length us, event | category | flops | bytes accessed | tf_op | source)
XLA Modules:
  0.0 507.4 jit_solution(7375458884553897142)
XLA Ops:
  7.2 0.9 fusion.9
  8.2 1.3 collective-permute-start.3
  9.4 5.5 %collective-permute-start.2 = (f32[2,48,128]{2,1,0:T(8,128)S(1)}, f32[2,48,128]{2,1,0:T(8,128)S(1)}, u32[]{:S(2)}, u32[]{:S(2)}) collective-permute-start(f32[2,48,128]{2,1,0:T(8,128)S(1)} %get-tuple-element.109), channel_id=1, source_target_pairs={{0,1},{1,2},{2,3},{3,4},{4,5},{5,6},{6,7},{8,9},{9,10},{10,11},{11... | collective-permute-start | bytes 147464 | tf_op jit(solution)/shard_map/ppermute | solution.py:678
  15.0 1.1 fusion.8
  16.0 1.3 collective-permute-start.1
  17.3 5.5 %collective-permute-start = (bf16[16,48,128]{2,1,0:T(8,128)(2,1)S(1)}, bf16[16,48,128]{2,1,0:T(8,128)(2,1)S(1)}, u32[]{:S(2)}, u32[]{:S(2)}) collective-permute-start(bf16[16,48,128]{2,1,0:T(8,128)(2,1)S(1)} %get-tuple-element.107.xhi_ref), channel_id=1, source_target_pairs={{0,1},{1,2},{2,3},{3,4},{4,5},{5,6},{6,7},{8,9},{9,10},{10,11},{11... | collective-permute-start | bytes 589832 | tf_op jit(solution)/shard_map/ppermute | solution.py:678
  22.8 1.2 broadcast_subtract_fusion.ids_ref
  24.6 1.4 copy.51.pw_ref
  25.9 17.8 %pair_bias.1.bias_ref = f32[2,32,128,128]{3,2,1,0:T(8,128)} custom-call(s32[2]{0:T(128)} %pad_add_fusion.base_ref, bf16[2,1024,16,128]{3,2,1,0:T(8,128)(2,1)} %pair_ref.3, f32[16,4]{1,0:T(8,128)} %copy.51.pw_ref), custom_call_target="tpu_custom_call" | custom-call | flops 100000000 | bytes 13631488 | tf_op jit(solution)/shard_map/pair_bias/pallas_call | solution.py:93
  45.1 274.8 %block.1 = (bf16[16,1024,128]{2,1,0:T(8,128)(2,1)}, bf16[16,1024,128]{2,1,0:T(8,128)(2,1)}, f32[16,96,128]{2,1,0:T(8,128)}, bf16[16,2,48,128]{3,2,1,0:T(8,128)(2...) custom-call(s32[16]{0:T(128)} %broadcast_subtract_fusion.ids_ref, ...), custom_call_target="tpu_custom_call" | custom-call | tf_op jit(solution)/shard_map/block/pallas_call | solution.py:500
  319.9 4.8 collective-permute-start.4
  324.8 1.3 collective-permute-start.5
  326.7 17.1 %pair_grad.1 = f32[64,8,128]{2,1,0:T(8,128)} custom-call(bf16[2,1024,16,128]{3,2,1,0:T(8,128)(2,1)} %pair_ref.3, f32[2,32,128,128]{3,2,1,0:T(8,128)} %get-tuple-element.65.dbias_ref), custom_call_target="tpu_custom_call" | custom-call | flops 100000000 | bytes 13631488 | tf_op jit(solution)/shard_map/pair_grad/pallas_call | solution.py:137
  343.9 1.5 reduce_sum.19
  345.6 0.8 copy-done.5
  346.5 11.4 %rims.1 = (bf16[16,96,128]{2,1,0:T(8,128)(2,1)}, f32[17,128,128]{2,1,0:T(8,128)}, f32[7,8,128]{2,1,0:T(8,128)}) custom-call(s32[16]{0:T(128)} %broadcast_subtract_fusion.ids_ref, bf16[16,2,48,128]{3,2,1,0:T(8,128)(2,1)} %copy-done.5, bf16[16,2,48,128]{3,2,1,0:T(8,128)(2,1)} %copy-done.6, bf16[16,48,128]{2,1,0:T(8,128)(2,1)} %copy-done.2, ...), custom_call_target="tpu_custom_call" | custom-call | tf_op jit(solution)/shard_map/rims/pallas_call | solution.py:657
  358.6 42.1 %all-reduce = (f32[7,128]{1,0:T(8,128)S(1)}, f32[16,4]{0,1:T(4,128)S(1)}) all-reduce(f32[7,128]{1,0:T(8,128)S(1)} %reduce_sum.18, f32[16,4]{0,1:T(4,128)S(1)} %copy.52), channel_id=1, replica_groups=mesh['samp'=4,'win'=8] {'samp','win'}, use_global_device_ids=true, to_apply=%region_2.0 | all-reduce | flops 960 | bytes 7680 | tf_op jit(solution)/shard_map/psum | solution.py:724
  402.0 0.7 slice_dynamic-update-slice_fusion.1
  402.7 0.7 slice_dynamic-update-slice_fusion
  403.4 86.5 %all-reduce.3.cloned.1.call-done = f32[17,128,128]{2,1,0:T(8,128)} async-done(((f32[17,128,128]{2,1,0:T(8,128)}), f32[17,128,128]{2,1,0:T(8,128)}) %all-reduce.3.cloned.1.call-update) | async-done | bytes 1114128 | tf_op jit(solution)/shard_map/psum | solution.py:724
  489.9 2.3 fusion.10
  492.3 2.8 multiply_add_fusion
  495.1 2.9 fusion
  498.0 2.5 fusion.1
  (65 shorter events, 4.9 us)
Async XLA Ops:
  7.2 485.0 %copy-start = (f32[17,128,128]{2,1,0:T(8,128)S(1)}, f32[17,128,128]{2,1,0:T(8,128)}, u32[]{:S(2)}) copy-start(f32[17,128,128]{2,1,0:T(8,128)} %param.32) | copy-start | bytes 3342340
  7.2 482.7 %all-reduce.3.cloned.1.call-start = ((), (), s32[]{:S(2)}) async-start(), calls=%async_computation | async-start | bytes 2228224 | tf_op jit(solution)/shard_map/psum | solution.py:724
  8.2 35.5 %collective-permute-start.3 = (f32[2,48,128]{2,1,0:T(8,128)S(1)}, f32[2,48,128]{2,1,0:T(8,128)S(1)}, u32[]{:S(2)}, u32[]{:S(2)}) collective-permute-start(f32[2,48,128]{2,1,0:T(8,128)S(1)} %get-tuple-element.108), channel_id=1, source_target_pairs={{1,0},{2,1},{3,2},{4,3},{5,4},{6,5},{7,6},{9,8},{10,9},{11,10},{12... | collective-permute-start | bytes 147464 | tf_op jit(solution)/shard_map/ppermute | solution.py:678
  9.4 34.3 %collective-permute-start.2 = (f32[2,48,128]{2,1,0:T(8,128)S(1)}, f32[2,48,128]{2,1,0:T(8,128)S(1)}, u32[]{:S(2)}, u32[]{:S(2)}) collective-permute-start(f32[2,48,128]{2,1,0:T(8,128)S(1)} %get-tuple-element.109), channel_id=1, source_target_pairs={{0,1},{1,2},{2,3},{3,4},{4,5},{5,6},{6,7},{8,9},{9,10},{10,11},{11... | collective-permute-start | bytes 147464 | tf_op jit(solution)/shard_map/ppermute | solution.py:678
  16.0 27.7 %copy-start.2 = (bf16[16,48,128]{2,1,0:T(8,128)(2,1)}, bf16[16,48,128]{2,1,0:T(8,128)(2,1)S(1)}, u32[]{:S(2)}) copy-start(bf16[16,48,128]{2,1,0:T(8,128)(2,1)S(1)} %get-tuple-element.106.xlo_ref) | copy-start | bytes 589828
  16.0 27.7 %copy-start.3 = (bf16[16,48,128]{2,1,0:T(8,128)(2,1)}, bf16[16,48,128]{2,1,0:T(8,128)(2,1)S(1)}, u32[]{:S(2)}) copy-start(bf16[16,48,128]{2,1,0:T(8,128)(2,1)S(1)} %get-tuple-element.107.xhi_ref) | copy-start | bytes 589828
  16.0 27.7 %collective-permute-start.1 = (bf16[16,48,128]{2,1,0:T(8,128)(2,1)S(1)}, bf16[16,48,128]{2,1,0:T(8,128)(2,1)S(1)}, u32[]{:S(2)}, u32[]{:S(2)}) collective-permute-start(bf16[16,48,128]{2,1,0:T(8,128)(2,1)S(1)} %get-tuple-element.106.xlo_ref), channel_id=1, source_target_pairs={{1,0},{2,1},{3,2},{4,3},{5,4},{6,5},{7,6},{9,8},{10,9},{11,10},{12... | collective-permute-start | bytes 589832 | tf_op jit(solution)/shard_map/ppermute | solution.py:678
  17.3 26.4 %collective-permute-start = (bf16[16,48,128]{2,1,0:T(8,128)(2,1)S(1)}, bf16[16,48,128]{2,1,0:T(8,128)(2,1)S(1)}, u32[]{:S(2)}, u32[]{:S(2)}) collective-permute-start(bf16[16,48,128]{2,1,0:T(8,128)(2,1)S(1)} %get-tuple-element.107.xhi_ref), channel_id=1, source_target_pairs={{0,1},{1,2},{2,3},{3,4},{4,5},{5,6},{6,7},{8,9},{9,10},{10,11},{11... | collective-permute-start | bytes 589832 | tf_op jit(solution)/shard_map/ppermute | solution.py:678
  319.9 25.6 %collective-permute-start.4 = (bf16[16,2,48,128]{3,2,1,0:T(8,128)(2,1)}, bf16[16,2,48,128]{3,2,1,0:T(8,128)(2,1)S(1)}, u32[]{:S(2)}, u32[]{:S(2)}) collective-permute-start(bf16[16,2,48,128]{3,2,1,0:T(8,128)(2,1)} %get-tuple-element.55), channel_id=1, source_target_pairs={{0,1},{1,2},{2,3},{3,4},{4,5},{5,6},{6,7},{8,9},{9,10},{10,11},{11... | collective-permute-start | bytes 1179656 | tf_op jit(solution)/shard_map/ppermute | solution.py:678
  324.8 20.8 %collective-permute-start.5 = (bf16[16,2,48,128]{3,2,1,0:T(8,128)(2,1)}, bf16[16,2,48,128]{3,2,1,0:T(8,128)(2,1)S(1)}, u32[]{:S(2)}, u32[]{:S(2)}) collective-permute-start(bf16[16,2,48,128]{3,2,1,0:T(8,128)(2,1)} %get-tuple-element.56), channel_id=1, source_target_pairs={{1,0},{2,1},{3,2},{4,3},{5,4},{6,5},{7,6},{9,8},{10,9},{11,10},{12... | collective-permute-start | bytes 1179656 | tf_op jit(solution)/shard_map/ppermute | solution.py:678
  357.8 42.9 %copy-start.16 = (f32[7,128]{1,0:T(8,128)S(1)}, f32[7,128]{1,0:T(8,128)}, u32[]{:S(2)}) copy-start(f32[7,128]{1,0:T(8,128)} %vec_ref.3) | copy-start | bytes 10756
  357.8 42.9 %copy-start.19 = (f32[7,128]{1,0:T(8,128)S(1)}, f32[7,128]{1,0:T(8,128)}, u32[]{:S(2)}) copy-start(f32[7,128]{1,0:T(8,128)} %param.36) | copy-start | bytes 10756
  357.8 42.9 %copy-start.20 = (f32[7,128]{1,0:T(8,128)S(1)}, f32[7,128]{1,0:T(8,128)}, u32[]{:S(2)}) copy-start(f32[7,128]{1,0:T(8,128)} %param.33) | copy-start | bytes 10756
  357.8 43.5 %copy-start.18 = (f32[16,4]{0,1:T(4,128)S(1)}, f32[16,4]{0,1:T(4,128)}, u32[]{:S(2)}) copy-start(f32[16,4]{0,1:T(4,128)} %param.28) | copy-start | bytes 772
  357.9 43.5 %copy-start.22 = (f32[16,4]{0,1:T(4,128)S(1)}, f32[16,4]{0,1:T(4,128)}, u32[]{:S(2)}) copy-start(f32[16,4]{0,1:T(4,128)} %param.37) | copy-start | bytes 772
  357.9 43.5 %copy-start.23 = (f32[16,4]{0,1:T(4,128)S(1)}, f32[16,4]{0,1:T(4,128)}, u32[]{:S(2)}) copy-start(f32[16,4]{0,1:T(4,128)} %param.34) | copy-start | bytes 772
  357.9 44.1 %copy-start.7 = (bf16[16,96,128]{2,1,0:T(8,128)(2,1)S(1)}, bf16[16,96,128]{2,1,0:T(8,128)(2,1)}, u32[]{:S(2)}) copy-start(bf16[16,96,128]{2,1,0:T(8,128)(2,1)} %get-tuple-element.62) | copy-start | bytes 1179652
  357.9 132.0 %copy-start.12 = (f32[17,16,128]{2,1,0:T(8,128)S(1)}, f32[17,16,128]{2,1,0:T(8,128)}, u32[]{:S(2)}) copy-start(f32[17,16,128]{2,1,0:T(8,128)} %param.31) | copy-start | bytes 417796
  400.7 91.5 %copy-start.21 = (f32[7,128]{1,0:T(8,128)}, f32[7,128]{1,0:T(8,128)S(1)}, u32[]{:S(2)}) copy-start(f32[7,128]{1,0:T(8,128)S(1)} %get-tuple-element.98) | copy-start | bytes 10756
  400.7 91.5 %copy-start.24 = (f32[16,4]{0,1:T(4,128)}, f32[16,4]{0,1:T(4,128)S(1)}, u32[]{:S(2)}) copy-start(f32[16,4]{0,1:T(4,128)S(1)} %get-tuple-element.99) | copy-start | bytes 772
  400.7 91.5 %copy-start.13 = (f32[17,16,128]{2,1,0:T(8,128)S(1)}, f32[17,16,128]{2,1,0:T(8,128)}, u32[]{:S(2)}) copy-start(f32[17,16,128]{2,1,0:T(8,128)} %param.35) | copy-start | bytes 417796
  492.3 2.8 copy-start.10
  495.0 3.0 copy-start.11
  495.1 5.4 %copy-start.4 = (f32[17,16,128]{2,1,0:T(8,128)}, f32[17,16,128]{2,1,0:T(8,128)S(1)}, u32[]{:S(2)}) copy-start(f32[17,16,128]{2,1,0:T(8,128)S(1)} %constant_dynamic-slice_fusion) | copy-start | bytes 417796
  (8 other events, 7.8 us)
Sparse Core Ops, SparseCore 0:
  358.1 131.8 all-reduce.2

commit v2 on v1

v2 whole, which is shorter than its diff:
```python
import functools
import math

import jax
import jax.numpy as jnp
from jax import lax
from jax.experimental import pallas as pl
from jax.experimental.pallas import tpu as pltpu
from jax.sharding import PartitionSpec as P

HEADS = 4
FF = 256
QW = 32
HALO = 48
KW = 128
C = 128
PAIR = 16
NBLK = 17
UNROLL = 8
PACK = 2
TILE = 512

stat_decay = 0.5
ema_decay = 0.8
matrix_rate = 1.0
vector_rate = 0.2

F32 = jnp.float32
BF16 = jnp.bfloat16
LOG2E = math.log2(math.e)
FACTOR = 1.0 / math.sqrt(C // HEADS)
INVALID = -1000000000.0
VMEM_LIMIT = 60 * 1024 * 1024
VEC_AT = NBLK * C
PW_AT = VEC_AT + 8
PACKED = 2240


def dot(left, right):
    return lax.dot_general(left, right, (((1,), (0,)), ((), ())), preferred_element_type=F32)


def dot_nt(left, right):
    return lax.dot_general(left, right, (((1,), (1,)), ((), ())), preferred_element_type=F32)


def dot_tn(left, right):
    return lax.dot_general(left, right, (((0,), (0,)), ((), ())), preferred_element_type=F32)


def layer_stats(values):
    center = values - jnp.mean(values, axis=-1, keepdims=True)
    inverse = lax.rsqrt(jnp.mean(center * center, axis=-1, keepdims=True) + 1e-05)
    return (center * inverse, inverse)


def layer_back(normed, inverse, grad_norm):
    return inverse * (
        grad_norm
        - jnp.mean(grad_norm, axis=-1, keepdims=True)
        - normed * jnp.mean(grad_norm * normed, axis=-1, keepdims=True)
    )


def pipeline(stages):
    waiting = list(stages)
    active = []
    while waiting or active:
        if waiting:
            active.append(waiting.pop(0))
        active = [item for item in active if next(item, active) is None]
        yield


def together(streams):
    count = len(streams[0])
    for at in range(count + len(streams) - 1):
        pipes = []
        for behind, phases in enumerate(streams):
            if 0 <= at - behind < count:
                depth, stages = phases[at - behind]
                pipes.append([pipeline(stages), depth + len(stages), 0])
        longest = max(length for _, length, _ in pipes)
        for tick in range(1, longest + 1):
            for item in pipes:
                while item[2] * longest < tick * item[1]:
                    item[2] += 1
                    next(item[0], None)
        for pipe, _, _ in pipes:
            for _ in pipe:
                pass


def rows_sum(values):
    return jnp.sum(values, axis=0, keepdims=True)


def bias_kernel(pair_ref, pw_ref, bias_ref, root_ref, expand):
    group = pl.program_id(1)
    per_step = bias_ref.shape[1]
    atoms = pl.num_programs(1) * per_step * QW

    @pl.when((pl.program_id(0) == 0) & (group == 0))
    def _():
        rows = lax.broadcasted_iota(jnp.int32, (QW * PAIR, C), 0) // PAIR
        lanes = lax.broadcasted_iota(jnp.int32, (QW * PAIR, C), 1) % QW
        same = rows == lanes
        weight = pw_ref[...] - jnp.mean(pw_ref[...], axis=0, keepdims=True)
        full = jnp.where(same, jnp.concatenate([weight] * QW, axis=0), 0.0)
        high = full.astype(BF16)
        expand[:, :C] = high
        expand[:, C : 2 * C] = (full - high.astype(F32)).astype(BF16)
        expand[:, 2 * C :] = jnp.where(same, 1.0 / PAIR, 0.0).astype(BF16)

    def one(w):
        low = pair_ref[0, w * QW : w * QW + QW].reshape(QW * PAIR, KW)
        wide = low.astype(F32)
        square = wide * wide
        high = square.astype(BF16)
        rest = (square - high.astype(F32)).astype(BF16)
        yield
        out = dot_tn(low, expand[...])
        second = dot_tn(high, expand[:, 2 * C :]) + dot_tn(rest, expand[:, 2 * C :])
        yield
        mean = out[:, 2 * C :]
        root = lax.rsqrt(jnp.maximum(second - mean * mean, 0.0) + 1e-05)
        value = (out[:, :C] + out[:, C : 2 * C]) * (root * LOG2E)
        start = lax.axis_index("win") * atoms + (group * per_step + w) * QW - HALO
        position = start + lax.broadcasted_iota(jnp.int32, (KW, C), 0)
        valid = (position >= 0) & (position < lax.axis_size("win") * atoms)
        bias_ref[0, w] = jnp.where(valid, value, INVALID * LOG2E)
        root_ref[0, w] = root.astype(BF16)

    for _ in pipeline([one(w) for w in range(per_step)]):
        pass


def bias_table(pair, wide_weight):
    structs, atoms = pair.shape[:2]
    count = min(8, atoms // QW)
    rows = count * QW
    return pl.pallas_call(
        bias_kernel,
        grid=(structs, atoms // rows),
        in_specs=[
            pl.BlockSpec((1, rows, PAIR, KW), lambda s, i: (s, i, 0, 0)),
            pl.BlockSpec((PAIR, C), lambda s, i: (0, 0)),
        ],
        out_specs=[
            pl.BlockSpec((1, count, KW, C), lambda s, i: (s, i, 0, 0)),
            pl.BlockSpec((1, count, KW, C), lambda s, i: (s, i, 0, 0)),
        ],
        scratch_shapes=[pltpu.VMEM((QW * PAIR, 3 * C), BF16)],
        out_shape=[
            jax.ShapeDtypeStruct((structs, atoms // QW, KW, C), F32),
            jax.ShapeDtypeStruct((structs, atoms // QW, KW, C), BF16),
        ],
        compiler_params=pltpu.CompilerParams(vmem_limit_bytes=VMEM_LIMIT),
        cost_estimate=pl.CostEstimate(flops=10**9, bytes_accessed=15 * 2**20, transcendentals=0),
        name="pair_bias",
    )(pair, wide_weight)


def pair_grad_kernel(pair_ref, dbias_ref, root_ref, out_ref, total):
    step = pl.program_id(0) * pl.num_programs(1) + pl.program_id(1)

    @pl.when(step == 0)
    def _():
        total[...] = jnp.zeros_like(total)

    parts = []
    for w in range(dbias_ref.shape[1]):
        low = pair_ref[0, w * QW : w * QW + QW].reshape(QW * PAIR, KW)
        grad = (dbias_ref[0, w] * root_ref[0, w].astype(F32)).astype(BF16)
        parts.append((low, grad))
    for at in range(0, len(parts), 2):
        pair_of = parts[at : at + 2]
        left = jnp.concatenate([low for low, _ in pair_of], axis=1)
        right = jnp.concatenate([grad for _, grad in pair_of], axis=0)
        total[...] += dot(left, right)

    @pl.when(step == pl.num_programs(0) * pl.num_programs(1) - 1)
    def _():
        lanes = lax.broadcasted_iota(jnp.int32, (PAIR, C), 1) % QW
        acc = jnp.zeros((PAIR, C), F32)
        for q in range(QW):
            acc = acc + jnp.where(lanes == q, total[q * PAIR : q * PAIR + PAIR], 0.0)
        out_ref[...] = acc - jnp.mean(acc, axis=0, keepdims=True)


def pair_grad(pair, dbias, root):
    structs, atoms = pair.shape[:2]
    count = min(8, atoms // QW)
    rows = count * QW
    table = pl.BlockSpec((1, count, KW, C), lambda s, i: (s, i, 0, 0))
    return pl.pallas_call(
        pair_grad_kernel,
        grid=(structs, atoms // rows),
        in_specs=[
            pl.BlockSpec((1, rows, PAIR, KW), lambda s, i: (s, i, 0, 0)),
            table,
            table,
        ],
        out_specs=pl.BlockSpec((PAIR, C), lambda s, i: (0, 0)),
        scratch_shapes=[pltpu.VMEM((QW * PAIR, C), F32)],
        out_shape=jax.ShapeDtypeStruct((PAIR, C), F32),
        compiler_params=pltpu.CompilerParams(vmem_limit_bytes=VMEM_LIMIT),
        cost_estimate=pl.CostEstimate(flops=10**9, bytes_accessed=15 * 2**20, transcendentals=0),
        name="pair_grad",
    )(pair, dbias, root)


def main_kernel(
    ids_ref,
    x_ref,
    xlo_ref,
    xhi_ref,
    g_ref,
    bias_ref,
    cond_ref,
    clo_ref,
    chi_ref,
    w_ref,
    vec_ref,
    out_ref,
    grad_ref,
    gxb_ref,
    rlo_ref,
    rhi_ref,
    dbias_ref,
    gw_ref,
    dvec_ref,
    accb_ref,
    tabb_ref,
    wq,
    w6,
    win,
    wo,
    wqt,
    w6t,
    wint,
    wot,
    wc1,
    wc2,
    mask,
    t_s1,
    t_h1,
    t_hs,
    t_hh,
    t_g1,
    t_s2,
    t_h2,
    t_g2,
    a_s1,
    a_h1,
    a_g1,
    a_s2,
    a_h2,
    a_g2,
    k_scr,
    v_scr,
    q_scr,
    gate_scr,
    ada_scr,
    n1_scr,
    inv_scr,
    o_scr,
    p_scr,
    do_scr,
    dd_scr,
    d4_scr,
    dk_scr,
    dv_scr,
    dx_scr,
):
    step = pl.program_id(0)
    structs, atoms, _ = cond_ref.shape
    windows = atoms // QW
    tile = min(TILE, atoms)
    tiles = atoms // tile
    s = [lax.rem(ids_ref[step * PACK + b], structs) for b in range(PACK)]

    def cond_rows(source):
        normed, _ = layer_stats(source)
        one = (normed * vec_ref[0:1]).astype(BF16)
        two = (normed * vec_ref[4:5]).astype(BF16)
        return normed, one, two

    def joined(ref, st):
        return ref[st].astype(F32) + ref[structs + st].astype(F32)

    @pl.when(step == 0)
    def _():
        def low(b):
            return w_ref[b].astype(BF16)

        for at, b in enumerate((2, 5, 3, 4)):
            wq[:, at * C : at * C + C] = low(b)
        w6[...] = low(6)
        for at in range(4):
            win[:, at * C : at * C + C] = low(11 + at)
        for at in range(2):
            wo[at * C : at * C + C, :] = low(15 + at)
        for source, turned in ((wq, wqt), (w6, w6t), (win, wint), (wo, wot)):
            turned[...] = source[...].T
        for at, b in enumerate((0, 1, 7)):
            wc1[:, at * C : at * C + C] = low(b)
        for at, b in enumerate((8, 9, 10)):
            wc2[:, at * C : at * C + C] = low(b)
        rows_head = lax.broadcasted_iota(jnp.int32, (C, C), 0) // QW
        lane_head = lax.broadcasted_iota(jnp.int32, (C, C), 1) // (C // HEADS)
        mask[...] = jnp.where(rows_head == lane_head, 1.0, 0.0).astype(BF16)
        for acc in (a_s1, a_h1, a_g1, a_s2, a_h2, a_g2, gw_ref, dvec_ref):
            acc[...] = jnp.zeros_like(acc)
        dbias_ref[...] = jnp.zeros_like(dbias_ref)
        for st in range(structs):

            def table(i, carry):
                rows = pl.ds(pl.multiple_of(i * tile, tile), tile)
                _, one, two = cond_rows(cond_ref[st, rows])
                first = dot(one, wc1[...])
                t_s1[st, rows] = jax.nn.sigmoid(first[:, :C] + vec_ref[1:2])
                t_h1[st, rows] = first[:, C : 2 * C]
                t_g1[st, rows] = jax.nn.sigmoid(first[:, 2 * C :] + vec_ref[3:4])
                second = dot(two, wc2[...])
                t_s2[st, rows] = jax.nn.sigmoid(second[:, :C] + vec_ref[5:6])
                t_h2[st, rows] = second[:, C : 2 * C]
                t_g2[st, rows] = jax.nn.sigmoid(second[:, 2 * C :] + vec_ref[6:7])
                return carry

            lax.fori_loop(0, tiles, table, 0)
            _, one, _ = cond_rows(jnp.concatenate([joined(clo_ref, st), joined(chi_ref, st)], axis=0))
            first = dot(one, wc1[:, : 2 * C])
            t_hs[st] = jax.nn.sigmoid(first[:, :C] + vec_ref[1:2])
            t_hh[st] = first[:, C:]
            tabb_ref[0, st, :HALO] = t_s1[st, :HALO]
            tabb_ref[0, st, HALO:] = t_s1[st, atoms - HALO :]
            tabb_ref[1, st, :HALO] = t_h1[st, :HALO]
            tabb_ref[1, st, HALO:] = t_h1[st, atoms - HALO :]

    def project(b, i):
        start = i * tile
        rows = pl.ds(start, tile)
        pad = pl.ds(start + HALO, tile)
        normed, inverse = layer_stats(x_ref[b, rows].astype(F32))
        n1_scr[b, rows] = normed
        inv_scr[b, rows] = jnp.broadcast_to(inverse, (tile, C))
        ada = (t_s1[s[b], rows] * normed + t_h1[s[b], rows]).astype(BF16)
        ada_scr[b, rows] = ada
        yield
        out = dot(ada, wq[...])
        yield
        q_scr[b, rows] = (out[:, :C] + vec_ref[2:3]).astype(BF16)
        gate_scr[b, rows] = jax.nn.sigmoid(out[:, C : 2 * C])
        k_scr[b, pad] = out[:, 2 * C : 3 * C].astype(BF16)
        v_scr[b, pad] = out[:, 3 * C :].astype(BF16)

    def project_halo(b):
        halo = jnp.concatenate([xlo_ref[b], xhi_ref[b]], axis=0).astype(F32)
        normed, _ = layer_stats(halo)
        ada = (t_hs[s[b]] * normed + t_hh[s[b]]).astype(BF16)
        yield
        out = dot(ada, wq[:, 2 * C :])
        yield
        k_scr[b, :HALO] = out[:HALO, :C].astype(BF16)
        v_scr[b, :HALO] = out[:HALO, C:].astype(BF16)
        k_scr[b, HALO + atoms :] = out[HALO:, :C].astype(BF16)
        v_scr[b, HALO + atoms :] = out[HALO:, C:].astype(BF16)

    lane_head = lax.broadcasted_iota(jnp.int32, (QW, C), 1) // (C // HEADS)

    def spread(rows):
        return jnp.concatenate([rows] * HEADS, axis=0) * mask[...]

    def gathered(full):
        parts = [full[h * QW : h * QW + QW] for h in range(HEADS)]
        last = parts[HEADS - 1]
        for h in range(HEADS - 2, -1, -1):
            last = jnp.where(lane_head == h, parts[h], last)
        return last

    def attend(b, group):
        scores = []
        for w in group:
            queries = spread(q_scr[b, w * QW : w * QW + QW])
            scores.append(dot(k_scr[b, w * QW : w * QW + KW], queries.T))
        yield
        probs = []
        for u, w in enumerate(group):
            value = scores[u] * (FACTOR * LOG2E) + bias_ref[s[b], w]
            exps = jnp.exp2(value - jnp.max(value, axis=0, keepdims=True))
            prob = (exps * (1.0 / rows_sum(exps))).astype(BF16)
            p_scr[b, w] = prob
            probs.append(prob)
        yield
        fulls = [dot_tn(probs[u], v_scr[b, w * QW : w * QW + KW]) for u, w in enumerate(group)]
        yield
        for u, w in enumerate(group):
            o_scr[b, w * QW : w * QW + QW] = gathered(fulls[u])

    def middle(b, i):
        rows = pl.ds(i * tile, tile)
        gate = gate_scr[b, rows]
        mixed = o_scr[b, rows]
        y = (gate * mixed).astype(BF16)
        yield
        attn = dot(y, w6[...])
        yield
        gate_one = t_g1[s[b], rows]
        x1 = x_ref[b, rows].astype(F32) + gate_one * attn
        normed, inverse = layer_stats(x1)
        scale_two = t_s2[s[b], rows]
        ada = (scale_two * normed + t_h2[s[b], rows]).astype(BF16)
        yield
        expand = dot(ada, win[...])
        yield
        a = expand[:, :FF]
        up = expand[:, FF:]
        sig = jax.nn.sigmoid(a)
        silu = a * sig
        hid = (silu * up).astype(BF16)
        yield
        ff = dot(hid, wo[...])
        gate_two = t_g2[s[b], rows]
        g = g_ref[b, rows].astype(F32)
        dff = (g * gate_two).astype(BF16)
        dhid = dot(dff, wot[...])
        yield
        out_ref[b, rows] = (x1 + gate_two * ff).astype(BF16)
        a_g2[s[b], rows] += g * ff
        da = (dhid * up * (sig + silu * (1.0 - sig))).astype(BF16)
        db = (dhid * silu).astype(BF16)
        dab = jnp.concatenate([da, db], axis=1)
        yield
        dada = dot(dab, wint[...])
        yield
        a_s2[s[b], rows] += dada * normed
        a_h2[s[b], rows] += dada
        dx1 = g + layer_back(normed, inverse, dada * scale_two)
        dx_scr[b, rows] = dx1
        a_g1[s[b], rows] += dx1 * attn
        dattn = (dx1 * gate_one).astype(BF16)
        yield
        dy = dot(dattn, w6t[...])
        dwo = dot_tn(dff, hid)
        dwin = dot_tn(ada, dab)
        dw6 = dot_tn(y, dattn)
        yield
        do = (dy * gate).astype(BF16)
        do_scr[b, rows] = do
        dd_scr[b, rows] = (do.astype(F32) * mixed * -1.0).astype(BF16)
        d4_scr[b, rows, C : 2 * C] = (dy * mixed * gate * (1.0 - gate)).astype(BF16)
        gw_ref[15] += dwo[:, :C]
        gw_ref[16] += dwo[:, C:]
        for at in range(4):
            gw_ref[11 + at] += dwin[:, at * C : at * C + C]
        gw_ref[6] += dw6

    dk_scr[...] = jnp.zeros_like(dk_scr)
    dv_scr[...] = jnp.zeros_like(dv_scr)
    ones = jnp.ones((KW, C), BF16)

    def attend_back(b, group):
        diffs = []
        spreads = []
        for w in group:
            dox = spread(do_scr[b, w * QW : w * QW + QW])
            ddx = spread(dd_scr[b, w * QW : w * QW + QW])
            values = jnp.concatenate([v_scr[b, w * QW : w * QW + KW], ones], axis=1)
            diffs.append(dot(values, jnp.concatenate([dox.T, ddx.T], axis=0)))
            spreads.append(dox)
        yield
        grads = []
        for u, w in enumerate(group):
            ds = p_scr[b, w] * diffs[u].astype(BF16)
            dbias_ref[s[b], w] += ds.astype(F32)
            grads.append(ds)
        yield
        fulls = []
        dks = []
        dvs = []
        for u, w in enumerate(group):
            fulls.append(dot_tn(grads[u], k_scr[b, w * QW : w * QW + KW]))
            dks.append(dot(grads[u], spread(q_scr[b, w * QW : w * QW + QW])))
            dvs.append(dot(p_scr[b, w], spreads[u]))
        yield
        for u, w in enumerate(group):
            dq = gathered(fulls[u]) * FACTOR
            dvec_ref[2] += jnp.sum(dq.reshape(QW // 8, 8, C), axis=0)
            d4_scr[b, w * QW : w * QW + QW, :C] = dq.astype(BF16)
            dk_scr[b, w * QW : w * QW + KW] += dks[u]
            dv_scr[b, w * QW : w * QW + KW] += dvs[u]

    def finish(b, i):
        start = i * tile
        rows = pl.ds(start, tile)
        pad = pl.ds(start + HALO, tile)
        d4_scr[b, rows, 2 * C : 3 * C] = (dk_scr[b, pad] * FACTOR).astype(BF16)
        d4_scr[b, rows, 3 * C :] = dv_scr[b, pad].astype(BF16)
        yield
        d4 = d4_scr[b, rows]
        dwq = dot_tn(ada_scr[b, rows], d4)
        dada = dot(d4, wqt[...])
        yield
        for at, block in enumerate((2, 5, 3, 4)):
            gw_ref[block] += dwq[:, at * C : at * C + C]
        normed = n1_scr[b, rows]
        a_s1[s[b], rows] += dada * normed
        a_h1[s[b], rows] += dada
        grad = dx_scr[b, rows] + layer_back(normed, inv_scr[b, rows], dada * t_s1[s[b], rows])
        dx_scr[b, rows] = grad
        grad_ref[b, rows] = grad.astype(BF16)

    groups = [tuple(range(at, at + UNROLL)) for at in range(0, windows, UNROLL)]

    def phases(b):
        return [
            (3, [project_halo(b)] + [project(b, i) for i in range(tiles)]),
            (4, [attend(b, group) for group in groups]),
            (11, [middle(b, i) for i in range(tiles)]),
            (4, [attend_back(b, group) for group in groups]),
            (3, [finish(b, i) for i in range(tiles)]),
        ]

    together([phases(b) for b in range(PACK)])
    for b in range(PACK):
        gxb_ref[b, :HALO] = dx_scr[b, :HALO]
        gxb_ref[b, HALO:] = dx_scr[b, atoms - HALO :]
        for ref, span in ((rlo_ref, slice(0, HALO)), (rhi_ref, slice(HALO + atoms, None))):
            ref[b, :, :C] = (dk_scr[b, span] * FACTOR).astype(BF16)
            ref[b, :, C:] = dv_scr[b, span].astype(BF16)

    @pl.when(step == pl.num_programs(0) - 1)
    def _():
        for b in (15, 16):
            gw_ref[b] = gw_ref[b].T
        for st in range(structs):
            accb_ref[0, st, :HALO] = a_s1[st, :HALO]
            accb_ref[0, st, HALO:] = a_s1[st, atoms - HALO :]
            accb_ref[1, st, :HALO] = a_h1[st, :HALO]
            accb_ref[1, st, HALO:] = a_h1[st, atoms - HALO :]
            for acc in (a_s1, a_h1):
                acc[st, :HALO] = jnp.zeros((HALO, C), F32)
                acc[st, atoms - HALO :] = jnp.zeros((HALO, C), F32)

            def conditioning(i, carry):
                rows = pl.ds(pl.multiple_of(i * tile, tile), tile)
                normed, one, two = cond_rows(cond_ref[st, rows])

                def pre(acc, gate):
                    return (acc[st, rows] * gate[st, rows] * (1.0 - gate[st, rows])).astype(BF16)

                first = [pre(a_s1, t_s1), a_h1[st, rows].astype(BF16), pre(a_g1, t_g1)]
                second = [pre(a_s2, t_s2), a_h2[st, rows].astype(BF16), pre(a_g2, t_g2)]
                for at, part in ((1, first[0]), (3, first[2]), (5, second[0]), (6, second[2])):
                    dvec_ref[at] += jnp.sum(part.astype(F32).reshape(tile // 8, 8, C), axis=0)
                for at, source, parts, weight, blocks in (
                    (0, one, first, wc1, (0, 1, 7)),
                    (4, two, second, wc2, (8, 9, 10)),
                ):
                    joined = jnp.concatenate(parts, axis=1)
                    grads = dot_tn(source, joined)
                    for j, b in enumerate(blocks):
                        gw_ref[b] += grads[:, j * C : j * C + C]
                    back = dot_nt(joined, weight[...]) * normed
                    dvec_ref[at] += jnp.sum(back.reshape(tile // 8, 8, C), axis=0)
                return carry

            lax.fori_loop(0, tiles, conditioning, 0)


def main_call(ids, atoms, low_msg, high_msg, cotangent, bias, cond, weights, vectors):
    samples, rows, _ = atoms.shape
    structs = cond.shape[0]
    windows = rows // QW
    padded = rows + 2 * HALO

    def per_sample(*shape):
        zeros = (0,) * len(shape)
        return pl.BlockSpec((PACK,) + shape, lambda i, _: (i,) + zeros)

    def whole(*shape):
        zeros = (0,) * len(shape)
        return pl.BlockSpec(shape, lambda i, _: zeros, pipeline_mode=pl.Buffered(1))

    def table(count=rows):
        return pltpu.VMEM((structs, count, C), F32)

    cond_part = pl.BlockSpec((2 * structs, HALO, C), lambda i, _: (samples // (2 * structs), 0, 0))
    shape = jax.ShapeDtypeStruct
    return pl.pallas_call(
        main_kernel,
        grid_spec=pltpu.PrefetchScalarGridSpec(
            num_scalar_prefetch=1,
            grid=(samples // PACK,),
            in_specs=[
                per_sample(rows, C),
                per_sample(HALO, C),
                per_sample(HALO, C),
                per_sample(rows, C),
                whole(structs, windows, KW, C),
                whole(structs, rows, C),
                cond_part,
                cond_part,
                whole(NBLK, C, C),
                whole(7, C),
            ],
            out_specs=[
                per_sample(rows, C),
                per_sample(rows, C),
                per_sample(2 * HALO, C),
                per_sample(HALO, 2 * C),
                per_sample(HALO, 2 * C),
                whole(structs, windows, KW, C),
                whole(NBLK, C, C),
                whole(7, 8, C),
                whole(2, structs, 2 * HALO, C),
                whole(2, structs, 2 * HALO, C),
            ],
            scratch_shapes=[
                pltpu.VMEM((C, 4 * C), BF16),
                pltpu.VMEM((C, C), BF16),
                pltpu.VMEM((C, 2 * FF), BF16),
                pltpu.VMEM((FF, C), BF16),
                pltpu.VMEM((4 * C, C), BF16),
                pltpu.VMEM((C, C), BF16),
                pltpu.VMEM((2 * FF, C), BF16),
                pltpu.VMEM((C, FF), BF16),
                pltpu.VMEM((C, 3 * C), BF16),
                pltpu.VMEM((C, 3 * C), BF16),
                pltpu.VMEM((C, C), BF16),
                table(),
                table(),
                table(2 * HALO),
                table(2 * HALO),
                table(),
                table(),
                table(),
                table(),
                table(),
                table(),
                table(),
                table(),
                table(),
                table(),
                pltpu.VMEM((PACK, padded, C), BF16),
                pltpu.VMEM((PACK, padded, C), BF16),
                pltpu.VMEM((PACK, rows, C), BF16),
                pltpu.VMEM((PACK, rows, C), F32),
                pltpu.VMEM((PACK, rows, C), BF16),
                pltpu.VMEM((PACK, rows, C), F32),
                pltpu.VMEM((PACK, rows, C), F32),
                pltpu.VMEM((PACK, rows, C), F32),
                pltpu.VMEM((PACK, windows, KW, C), BF16),
                pltpu.VMEM((PACK, rows, C), BF16),
                pltpu.VMEM((PACK, rows, C), BF16),
                pltpu.VMEM((PACK, rows, 4 * C), BF16),
                pltpu.VMEM((PACK, padded, C), F32),
                pltpu.VMEM((PACK, padded, C), F32),
                pltpu.VMEM((PACK, rows, C), F32),
            ],
        ),
        out_shape=[
            shape((samples, rows, C), BF16),
            shape((samples, rows, C), BF16),
            shape((samples, 2 * HALO, C), F32),
            shape((samples, HALO, 2 * C), BF16),
            shape((samples, HALO, 2 * C), BF16),
            shape((structs, windows, KW, C), F32),
            shape((NBLK, C, C), F32),
            shape((7, 8, C), F32),
            shape((2, structs, 2 * HALO, C), F32),
            shape((2, structs, 2 * HALO, C), F32),
        ],
        compiler_params=pltpu.CompilerParams(vmem_limit_bytes=VMEM_LIMIT),
        name="block",
    )(ids, atoms, low_msg, high_msg, cotangent, bias, cond, low_msg, high_msg, weights, vectors)


def rim_kernel(
    ids_ref,
    below_ref,
    above_ref,
    first_ref,
    last_ref,
    gxb_ref,
    tab_ref,
    acc_ref,
    w_ref,
    vec_ref,
    gw_ref,
    dvec_ref,
    dpair_ref,
    grad_ref,
    packed_ref,
    sums,
    dw,
):
    samples = below_ref.shape[0]
    structs = tab_ref.shape[1]
    sums[...] = acc_ref[...]
    dw[...] = jnp.zeros_like(dw)
    weight = jnp.concatenate([w_ref[3], w_ref[4]], axis=1).astype(BF16).T
    vecs = VEC_AT
    packed_ref[:vecs] = gw_ref[...].reshape(NBLK * C, C)
    packed_ref[vecs : vecs + 8] = jnp.concatenate(
        [jnp.sum(dvec_ref[at], axis=0, keepdims=True) for at in range(7)] + [jnp.zeros((1, C), F32)],
        axis=0,
    )
    packed_ref[PW_AT : PW_AT + PAIR] = dpair_ref[...]
    packed_ref[PW_AT + PAIR :] = jnp.zeros((PACKED - PW_AT - PAIR, C), F32)

    def one(i):
        s = lax.rem(ids_ref[i], structs)
        x = jnp.concatenate([first_ref[i], last_ref[i]], axis=0).astype(F32)
        normed, inverse = layer_stats(x)
        scale = tab_ref[0, s]
        ada = (scale * normed + tab_ref[1, s]).astype(BF16)
        dkv = jnp.concatenate([below_ref[i], above_ref[i]], axis=0)
        dada = dot(dkv, weight)
        yield
        part = dot_tn(ada, dkv)
        grad_norm = dada * scale
        grad = gxb_ref[i] + layer_back(normed, inverse, grad_norm)
        yield
        dw[...] += part
        sums[0, s] += dada * normed
        sums[1, s] += dada
        grad_ref[i] = grad.astype(BF16)

    for _ in pipeline([one(i) for i in range(samples)]):
        pass
    packed_ref[3 * C : 4 * C] += dw[:, :C]
    packed_ref[4 * C : 5 * C] += dw[:, C:]
    weight = jnp.concatenate([w_ref[0], w_ref[1]], axis=1).astype(BF16)
    for st in range(structs):
        at = samples + st
        cond = jnp.concatenate([first_ref[at], last_ref[at]], axis=0).astype(F32)
        at = samples + structs + st
        cond = cond + jnp.concatenate([first_ref[at], last_ref[at]], axis=0).astype(F32)
        normed, _ = layer_stats(cond)
        source = (normed * vec_ref[0:1]).astype(BF16)
        scale = tab_ref[0, st]
        pre_scale = (sums[0, st] * scale * (1.0 - scale)).astype(BF16)
        pre_shift = sums[1, st].astype(BF16)
        joined = jnp.concatenate([pre_scale, pre_shift], axis=1)
        grads = dot_tn(source, joined)
        packed_ref[:C] += grads[:, :C]
        packed_ref[C : 2 * C] += grads[:, C:]
        back = dot_nt(joined, weight) * normed
        packed_ref[vecs : vecs + 1] += rows_sum(back)
        packed_ref[vecs + 1 : vecs + 2] += rows_sum(pre_scale.astype(F32))


def rim_call(ids, below, above, first, last, gxb, tab, acc, weights, vectors, gw, dvec, dpair):
    samples = below.shape[0]
    structs = tab.shape[1]
    full = pl.BlockSpec(memory_space=pltpu.VMEM)
    shape = jax.ShapeDtypeStruct
    return pl.pallas_call(
        rim_kernel,
        in_specs=[pl.BlockSpec(memory_space=pltpu.SMEM)] + [full] * 12,
        out_specs=[full] * 2,
        out_shape=[
            shape((samples, 2 * HALO, C), BF16),
            shape((PACKED, C), F32),
        ],
        scratch_shapes=[
            pltpu.VMEM((2, structs, 2 * HALO, C), F32),
            pltpu.VMEM((C, 2 * C), F32),
        ],
        compiler_params=pltpu.CompilerParams(vmem_limit_bytes=VMEM_LIMIT),
        name="rims",
    )(ids, below, above, first, last, gxb, tab, acc, weights, vectors, gw, dvec, dpair)


def split_low(values):
    high = values.astype(BF16)
    return high, (values - high.astype(F32)).astype(BF16)


def update_kernel(
    total_ref,
    sl_ref,
    sr_ref,
    rl_ref,
    rr_ref,
    w_ref,
    ew_ref,
    vec_ref,
    sv_ref,
    ev_ref,
    pw_ref,
    sp_ref,
    ep_ref,
    rows_ref,
    tv_ref,
    tp_ref,
    left_ref,
    right_ref,
    neww_ref,
    low_ref,
    newv_ref,
    newp_ref,
    nsv_ref,
    nsp_ref,
    neww_ema_ref,
    newv_ema_ref,
    newp_ema_ref,
    turned,
):
    count = sl_ref.shape[1]
    own = pl.ds(lax.axis_index("win") * count, count)

    def product(parts, right):
        high, low = split_low(right)
        lefts = [split_low(part) for part in parts]
        tall = jnp.concatenate([a for a, _ in lefts] + [b for _, b in lefts], axis=0)
        size = tall.shape[0] // 2
        first = dot(tall, high)
        return first[:size] + first[size:] + dot(tall[:size], low)

    def one(b):
        block = total_ref[b * C : b * C + C]
        turned[b] = block.T
        pad = jnp.zeros((16 - count, C), F32) if count < 16 else None

        def rows(values):
            return values if pad is None else jnp.concatenate([values, pad], axis=0)

        own_rows = total_ref[pl.ds(b * C + lax.axis_index("win") * count, count)]
        rows_ref[b] = own_rows
        yield
        own_cols = turned[b, own]
        both = product([rows(own_cols), rows(rl_ref[b])], block)
        left = product([rows(own_rows)], turned[b])
        size = max(count, 16)
        yield
        step = product([both[size:]], rr_ref[b])
        right_ref[b] = stat_decay * sr_ref[b] + (1.0 - stat_decay) * both[:count]
        left_ref[b] = stat_decay * sl_ref[b] + (1.0 - stat_decay) * left[:count]
        yield
        new = w_ref[b, own] - matrix_rate * step[:count]
        neww_ref[b] = new
        low_ref[b] = new.astype(BF16)
        neww_ema_ref[b] = ema_decay * ew_ref[b] + (1.0 - ema_decay) * new

    for _ in pipeline([one(b) for b in range(NBLK)]):
        pass
    sums = total_ref[PW_AT : PW_AT + PAIR]
    pair_total = jnp.concatenate(
        [jnp.sum(sums[:, h * QW : h * QW + QW], axis=1, keepdims=True) for h in range(HEADS)], axis=1
    )
    for total, param, stat, ema, out, new_ref, stat_ref, ema_ref in (
        (total_ref[VEC_AT : VEC_AT + 7], vec_ref, sv_ref, ev_ref, tv_ref, newv_ref, nsv_ref, newv_ema_ref),
        (pair_total, pw_ref, sp_ref, ep_ref, tp_ref, newp_ref, nsp_ref, newp_ema_ref),
    ):
        out[...] = total
        new_stat = stat_decay * stat[...] + (1.0 - stat_decay) * total * total
        stat_ref[...] = new_stat
        new = param[...] - vector_rate * total * lax.rsqrt(new_stat)
        new_ref[...] = new
        ema_ref[...] = ema_decay * ema[...] + (1.0 - ema_decay) * new


def update_call(*args):
    rows = args[1].shape
    vec = args[7].shape
    pw = args[10].shape
    full = pl.BlockSpec(memory_space=pltpu.VMEM)

    def shape(dims, kind=F32):
        return jax.ShapeDtypeStruct(dims, kind)

    return pl.pallas_call(
        update_kernel,
        in_specs=[full] * len(args),
        out_specs=[full] * 14,
        out_shape=[
            shape(rows),
            shape(vec),
            shape(pw),
            shape(rows),
            shape(rows),
            shape(rows),
            shape(rows, BF16),
            shape(vec),
            shape(pw),
            shape(vec),
            shape(pw),
            shape(rows),
            shape(vec),
            shape(pw),
        ],
        scratch_shapes=[pltpu.VMEM((NBLK, C, C), F32)],
        compiler_params=pltpu.CompilerParams(vmem_limit_bytes=VMEM_LIMIT),
        name="update",
    )(*args)


def passed(shard, by):
    devices = lax.axis_size("win")
    pairs = [(i, i + by) for i in range(devices) if 0 <= i + by < devices]
    return lax.ppermute(shard, "win", pairs)


def rounded(values):
    return lax.reduce_precision(values, exponent_bits=8, mantissa_bits=7)


def partner(values, axis, bit):
    devices = lax.axis_size(axis)
    return lax.ppermute(values, axis, [(i, i ^ bit) for i in range(devices)])


def bits(axis):
    devices = lax.axis_size(axis)
    return [(axis, 1 << at) for at in range((devices - 1).bit_length())]


def summed(values):
    halvings = bits("samp")
    for at, (axis, bit) in enumerate(halvings):
        side = (lax.axis_index(axis) // bit) % 2
        half = values.shape[0] // 2
        send = lax.dynamic_slice_in_dim(values, (1 - side) * half, half)
        keep = lax.dynamic_slice_in_dim(values, side * half, half)
        wire = F32 if at == 0 else BF16
        values = keep + partner(send.astype(wire), axis, bit).astype(F32)
    for axis, bit in bits("win"):
        values = rounded(values)
        values = values + partner(values.astype(BF16), axis, bit).astype(F32)
    values = values.astype(BF16)
    for axis, bit in reversed(halvings):
        side = (lax.axis_index(axis) // bit) % 2
        other = partner(values, axis, bit)
        values = jnp.where(
            side == 0,
            jnp.concatenate([values, other]),
            jnp.concatenate([other, values]),
        )
    return values.astype(F32)


def body(
    atoms,
    cond,
    pair,
    struct_ids,
    cotangent,
    weights,
    vectors,
    pair_weight,
    stat_left,
    stat_right,
    root_left,
    root_right,
    stat_vectors,
    stat_pair,
    ema_weights,
    ema_vectors,
    ema_pair,
):
    rows = atoms.shape[1]
    messages = []
    for span in (slice(0, HALO), slice(rows - HALO, rows)):
        high = rounded(cond[:, span])
        rest = cond[:, span] - high
        parts = [atoms[:, span], high.astype(BF16), rest.astype(BF16)]
        messages.append(jnp.concatenate(parts, axis=0))
    first, last = messages
    low_msg, high_msg = passed(last, 1), passed(first, -1)
    bias, root = bias_table(pair, jnp.repeat(pair_weight, QW, axis=1))
    (result, grad_atoms, gxb, rim_low, rim_high, dbias, gw, dvec, accb, tabb) = main_call(
        struct_ids, atoms, low_msg, high_msg, cotangent, bias, cond, weights, vectors
    )
    above = passed(rim_low, -1)
    below = passed(rim_high, 1)
    dpair = pair_grad(pair, dbias, root)
    grad_rim, packed = rim_call(
        struct_ids, below, above, first, last, gxb, tabb, accb, weights, vectors, gw, dvec, dpair
    )
    grad_atoms = grad_atoms.at[:, :HALO].set(grad_rim[:, :HALO])
    grad_atoms = grad_atoms.at[:, rows - HALO :].set(grad_rim[:, HALO:])
    updated = update_call(
        summed(packed),
        stat_left,
        stat_right,
        root_left,
        root_right,
        weights,
        ema_weights,
        vectors,
        stat_vectors,
        ema_vectors,
        pair_weight,
        stat_pair,
        ema_pair,
    )
    return (result, grad_atoms, *updated)


def solution(mesh):
    placed = (
        P("samp", "win", None),
        P("samp", "win", None),
        P("samp", "win", None, None),
        P("samp"),
        P("samp", "win", None),
        P(),
        P(),
        P(),
        P(None, "win", None),
        P(None, "win", None),
        P(None, "win", None),
        P(),
        P(),
        P(),
        P(None, "win", None),
        P(),
        P(),
    )
    return jax.shard_map(
        body,
        mesh=mesh,
        in_specs=placed,
        out_specs=(
            P("samp", "win", None),
            P("samp", "win", None),
            P(None, "win", None),
            P(),
            P(),
            P(None, "win", None),
            P(None, "win", None),
            P(None, "win", None),
            P(None, "win", None),
            P(),
            P(),
            P(),
            P(),
            P(None, "win", None),
            P(),
            P(),
        ),
        check_vma=False,
    )
```

time: 509 us -> 209 us (0.41)
  Pallas kernels: 321 us -> 140 us
  waiting for transfers between devices: 86.6 us -> 25.8 us
  blocking collectives: 42.1 us -> 0 us
  between operations: 14.4 us -> 0.93 us
  matrix products: 10.5 us -> 0 us
  local copies, waits for them, and re-layouts: 7.92 us -> 13.6 us
    pallas_call x1, Pallas kernels: 275 us -> 106 us  [main_call(): pl.pallas_call(main_kernel, grid_spec=pltpu.PrefetchScalarGridSpec(num_sc...]
    psum x1 -> x0, waiting for transfers between devices: 86.5 us -> none  [body(): lax.psum((gw, jnp.sum(dvec, axis=1), jnp.sum(dpair, axis=(1, 2)).reshape(...]
    psum x1 -> x0, blocking collectives: 42.1 us -> none  [body(): lax.psum((gw, jnp.sum(dvec, axis=1), jnp.sum(dpair, axis=(1, 2)).reshape(...]
    ppermute x0 -> x7, waiting for transfers between devices: none -> 19.8 us  [partner(): return lax.ppermute(values, axis, [(i, i ^ bit) for i in range(devices)])]
    ppermute x0 -> x7, starting transfers between devices: none -> 10.7 us  [partner(): return lax.ppermute(values, axis, [(i, i ^ bit) for i in range(devices)])]
    dot_general x4 -> x0, matrix products: 10.5 us -> none  [the longest x1 2.92 us: body(): jnp.einsum('bci,bcj->bij', own_cols, total_w, precision=high)]
    pallas_call x1, Pallas kernels: 17.1 us -> 9.17 us  [pair_grad(): pl.pallas_call(pair_grad_kernel, grid=(structs, atoms // rows), in_specs=...]
    ppermute x6 -> x4, starting transfers between devices: 19.7 us -> 12.9 us  [passed(): return lax.ppermute(shard, 'win', pairs)]
  transfers between devices with their start and end apart: 7 -> 11, of which waited for: 1 -> 8; matrix products, arithmetic and copies ran while one was open for 2% -> 2% of each run, Pallas kernels for 7% -> 11%
where the time goes in v2:
time: 209 us; the launch traced here: 208 us
  Pallas kernels  140 us (67%)
  waiting for transfers between devices  25.8 us (12%)
  starting transfers between devices  23.6 us (11%)
  local copies, waits for them, and re-layouts  13.6 us (7%)
  other arithmetic  3.58 us (2%)
    pallas_call x1, Pallas kernels, main_call(): pl.pallas_call(main_kernel, grid_spec=pltpu.PrefetchScalarGridSpec(num_sc...  106 us
    ppermute x7, waiting for transfers between devices, partner(): return lax.ppermute(values, axis, [(i, i ^ bit) for i in range(devices)])  19.8 us
    pallas_call x1, Pallas kernels, bias_table(): pl.pallas_call(bias_kernel, grid=(structs, atoms // rows), in_specs=[pl.B...  13.7 us
    ppermute x4, starting transfers between devices, passed(): return lax.ppermute(shard, 'win', pairs)  12.9 us
    ppermute x7, starting transfers between devices, partner(): return lax.ppermute(values, axis, [(i, i ^ bit) for i in range(devices)])  10.7 us
    unnamed x27, local copies, waits for them, and re-layouts  9.18 us
    pallas_call x1, Pallas kernels, pair_grad(): pl.pallas_call(pair_grad_kernel, grid=(structs, atoms // rows), in_specs=...  9.17 us
    ppermute x4, waiting for transfers between devices, passed(): return lax.ppermute(shard, 'win', pairs)  6.02 us
  transfers between devices with their start and end apart: 11, of which 8 were waited for; matrix products, arithmetic and copies ran while one was open for 2% of the time, Pallas kernels for 11%

profile of v2, /device:TPU:0, one launch (start us, length us, event | category | flops | bytes accessed | tf_op | source)
XLA Modules:
  0.0 207.9 jit_solution(7457964106838415171)
XLA Ops:
  4.0 5.5 %collective-permute-start = (bf16[20,48,128]{2,1,0:T(8,128)(2,1)S(1)}, bf16[20,48,128]{2,1,0:T(8,128)(2,1)S(1)}, u32[]{:S(2)}, u32[]{:S(2)}) collective-permute-start(bf16[20,48,128]{2,1,0:T(8,128)(2,1)S(1)} %pad_maximum_fusion.last_ref), channel_id=1, source_target_pairs={{0,1},{1,2},{2,3},{3,4},{4,5},{5,6},{6,7},{8,9},{9,10},{10,11},{11... | collective-permute-start | bytes 737288 | tf_op jit(solution)/shard_map/ppermute | solution.py:904
  11.0 13.7 %pair_bias.1 = (f32[2,32,128,128]{3,2,1,0:T(8,128)}, bf16[2,32,128,128]{3,2,1,0:T(8,128)(2,1)}) custom-call(bf16[2,1024,16,128]{3,2,1,0:T(8,128)(2,1)} %pair_ref.3, f32[16,128]{1,0:T(8,128)} %reshape.95.pw_ref), custom_call_target="tpu_custom_call" | custom-call | flops 1000000000 | bytes 15728640 | tf_op jit(solution)/shard_map/pair_bias/pallas_call | solution.py:142
  25.6 105.9 %block.1 = (bf16[16,1024,128]{2,1,0:T(8,128)(2,1)}, bf16[16,1024,128]{2,1,0:T(8,128)(2,1)}, f32[16,96,128]{2,1,0:T(8,128)}, bf16[16,48,256]{2,1,0:T(8,128)(2,1)}...) custom-call(s32[16]{0:T(128)} %ids_ref.3, ...), custom_call_target="tpu_custom_call" | custom-call | tf_op jit(solution)/shard_map/block/pallas_call | solution.py:591
  131.4 4.8 %collective-permute-start.2 = (bf16[16,48,256]{2,1,0:T(8,128)(2,1)}, bf16[16,48,256]{2,1,0:T(8,128)(2,1)S(1)}, u32[]{:S(2)}, u32[]{:S(2)}) collective-permute-start(bf16[16,48,256]{2,1,0:T(8,128)(2,1)} %get-tuple-element.71), channel_id=1, source_target_pairs={{0,1},{1,2},{2,3},{3,4},{4,5},{5,6},{6,7},{8,9},{9,10},{10,11},{11... | collective-permute-start | bytes 1179656 | tf_op jit(solution)/shard_map/ppermute | solution.py:904
  136.3 1.3 collective-permute-start.3
  137.6 9.2 %pair_grad.1.dpair_ref = f32[16,128]{1,0:T(8,128)} custom-call(bf16[2,1024,16,128]{3,2,1,0:T(8,128)(2,1)} %pair_ref.3, f32[2,32,128,128]{3,2,1,0:T(8,128)} %get-tuple-element.78.dbias_ref, bf16[2,32,128,128]{3,2,1,0:T(8,128)(2,1)} %get-tuple-element.79.root_ref), custom_call_target="tpu_custom_call" | custom-call | flops 1000000000 | bytes 15728640 | tf_op jit(solution)/shard_map/pair_grad/pallas_call | solution.py:196
  146.8 6.0 %collective-permute-done.2.below_ref = bf16[16,48,256]{2,1,0:T(8,128)(2,1)S(1)} collective-permute-done((bf16[16,48,256]{2,1,0:T(8,128)(2,1)}, bf16[16,48,256]{2,1,0:T(8,128)(2,1)S(1)}, u32[]{:S(2)}, u32[]{:S(2)}) %collective-permute-start.2) | collective-permute-done | bytes 393248 | tf_op jit(solution)/shard_map/ppermute | solution.py:904
  153.7 5.9 %rims.1 = (bf16[16,96,128]{2,1,0:T(8,128)(2,1)}, f32[2240,128]{1,0:T(8,128)}) custom-call(s32[16]{0:T(128)} %ids_ref.3, bf16[16,48,256]{2,1,0:T(8,128)(2,1)} %copy-done.4, bf16[16,48,256]{2,1,0:T(8,128)(2,1)} %copy-done.5, bf16[20,48,128]{2,1,0:T(8,128)(2,1)} %copy-done, bf16[20,48,128]{2,1,0:T(8,128)(2,1)} %copy-done.1, ...), custom_call_target="tpu_custom_call" | custom-call | tf_op jit(solution)/shard_map/rims/pallas_call | solution.py:760
  160.8 1.9 collective-permute-done.4
  163.9 1.5 collective-permute-start.5
  165.4 4.3 %collective-permute-done.5 = bf16[560,128]{1,0:T(8,128)(2,1)S(1)} collective-permute-done((bf16[560,128]{1,0:T(8,128)(2,1)S(1)}, bf16[560,128]{1,0:T(8,128)(2,1)S(1)}, u32[]{:S(2)}, u32[]{:S(2)}) %collective-permute-start.5) | collective-permute-done | bytes 143392 | tf_op jit(solution)/shard_map/ppermute | solution.py:913
  169.8 2.4 %collective-permute-start.6 = (bf16[560,128]{1,0:T(8,128)(2,1)S(1)}, bf16[560,128]{1,0:T(8,128)(2,1)S(1)}, u32[]{:S(2)}, u32[]{:S(2)}) collective-permute-start(bf16[560,128]{1,0:T(8,128)(2,1)S(1)} %fusion.5), channel_id=1, source_target_pairs={{0,1},{1,0},{2,3},{3,2},{4,5},{5,4},{6,7},{7,6},{8,9},{9,8},{10,11... | collective-permute-start | bytes 430088 | tf_op jit(solution)/shard_map/ppermute | solution.py:913
  172.2 3.2 %collective-permute-done.6 = bf16[560,128]{1,0:T(8,128)(2,1)S(1)} collective-permute-done((bf16[560,128]{1,0:T(8,128)(2,1)S(1)}, bf16[560,128]{1,0:T(8,128)(2,1)S(1)}, u32[]{:S(2)}, u32[]{:S(2)}) %collective-permute-start.6) | collective-permute-done | bytes 143392 | tf_op jit(solution)/shard_map/ppermute | solution.py:913
  175.5 1.8 collective-permute-start.7
  177.4 3.3 %collective-permute-done.7 = bf16[560,128]{1,0:T(8,128)(2,1)S(1)} collective-permute-done((bf16[560,128]{1,0:T(8,128)(2,1)S(1)}, bf16[560,128]{1,0:T(8,128)(2,1)S(1)}, u32[]{:S(2)}, u32[]{:S(2)}) %collective-permute-start.7) | collective-permute-done | bytes 143392 | tf_op jit(solution)/shard_map/ppermute | solution.py:913
  180.8 3.2 %collective-permute-start.8 = (bf16[560,128]{1,0:T(8,128)(2,1)S(1)}, bf16[560,128]{1,0:T(8,128)(2,1)S(1)}, u32[]{:S(2)}, u32[]{:S(2)}) collective-permute-start(bf16[560,128]{1,0:T(8,128)(2,1)S(1)} %fusion.2), channel_id=1, source_target_pairs={{0,4},{1,5},{2,6},{3,7},{4,0},{5,1},{6,2},{7,3},{8,12},{9,13},{10,... | collective-permute-start | bytes 430088 | tf_op jit(solution)/shard_map/ppermute | solution.py:913
  184.0 4.6 %collective-permute-done.8 = bf16[560,128]{1,0:T(8,128)(2,1)S(1)} collective-permute-done((bf16[560,128]{1,0:T(8,128)(2,1)S(1)}, bf16[560,128]{1,0:T(8,128)(2,1)S(1)}, u32[]{:S(2)}, u32[]{:S(2)}) %collective-permute-start.8) | collective-permute-done | bytes 143392 | tf_op jit(solution)/shard_map/ppermute | solution.py:913
  188.7 1.5 collective-permute-start.9
  191.6 2.3 %collective-permute-done.9 = bf16[560,128]{1,0:T(8,128)(2,1)S(1)} collective-permute-done((bf16[560,128]{1,0:T(8,128)(2,1)S(1)}, bf16[560,128]{1,0:T(8,128)(2,1)S(1)}, u32[]{:S(2)}, u32[]{:S(2)}) %collective-permute-start.9) | collective-permute-done | bytes 143392 | tf_op jit(solution)/shard_map/ppermute | solution.py:913
  196.8 5.7 %update.1 = (f32[17,16,128]{2,1,0:T(8,128)}, f32[7,128]{1,0:T(8,128)}, f32[16,4]{1,0:T(8,128)}, f32[17,16,128]{2,1,0:T(8,128)}, f32[17,16,128]{2,1,0:T(8,128)}, ...) custom-call(f32[2240,128]{1,0:T(8,128)} %fusion.total_ref, ...), custom_call_target="tpu_custom_call" | custom-call | tf_op jit(solution)/shard_map/update/pallas_call | solution.py:875
  202.5 1.3 copy.37
  203.8 1.3 copy.38
  205.2 1.3 copy.39
  206.5 1.3 copy.40
  (47 shorter events, 13.3 us)
Async XLA Ops:
  2.6 22.1 %copy-start = (bf16[20,48,128]{2,1,0:T(8,128)(2,1)}, bf16[20,48,128]{2,1,0:T(8,128)(2,1)S(1)}, u32[]{:S(2)}) copy-start(bf16[20,48,128]{2,1,0:T(8,128)(2,1)S(1)} %pad_maximum_fusion.1.first_ref) | copy-start | bytes 737284
  2.6 22.2 %collective-permute-start.1 = (bf16[20,48,128]{2,1,0:T(8,128)(2,1)S(1)}, bf16[20,48,128]{2,1,0:T(8,128)(2,1)S(1)}, u32[]{:S(2)}, u32[]{:S(2)}) collective-permute-start(bf16[20,48,128]{2,1,0:T(8,128)(2,1)S(1)} %pad_maximum_fusion.1.first_ref), channel_id=1, source_target_pairs={{1,0},{2,1},{3,2},{4,3},{5,4},{6,5},{7,6},{9,8},{10,9},{11,10},{12... | collective-permute-start | bytes 737288 | tf_op jit(solution)/shard_map/ppermute | solution.py:904
  4.0 20.8 %copy-start.1 = (bf16[20,48,128]{2,1,0:T(8,128)(2,1)}, bf16[20,48,128]{2,1,0:T(8,128)(2,1)S(1)}, u32[]{:S(2)}) copy-start(bf16[20,48,128]{2,1,0:T(8,128)(2,1)S(1)} %pad_maximum_fusion.last_ref) | copy-start | bytes 737284
  4.0 20.8 %collective-permute-start = (bf16[20,48,128]{2,1,0:T(8,128)(2,1)S(1)}, bf16[20,48,128]{2,1,0:T(8,128)(2,1)S(1)}, u32[]{:S(2)}, u32[]{:S(2)}) collective-permute-start(bf16[20,48,128]{2,1,0:T(8,128)(2,1)S(1)} %pad_maximum_fusion.last_ref), channel_id=1, source_target_pairs={{0,1},{1,2},{2,3},{3,4},{4,5},{5,6},{6,7},{8,9},{9,10},{10,11},{11... | collective-permute-start | bytes 737288 | tf_op jit(solution)/shard_map/ppermute | solution.py:904
  10.2 14.5 %copy-start.7 = (f32[16,4]{1,0:T(8,128)}, f32[16,4]{1,0:T(8,128)S(1)}, u32[]{:S(2)}) copy-start(f32[16,4]{1,0:T(8,128)S(1)} %copy.33.pw_ref) | copy-start | bytes 772
  24.8 0.7 copy-start.2
  24.8 0.8 copy-start.3
  131.4 21.3 %collective-permute-start.2 = (bf16[16,48,256]{2,1,0:T(8,128)(2,1)}, bf16[16,48,256]{2,1,0:T(8,128)(2,1)S(1)}, u32[]{:S(2)}, u32[]{:S(2)}) collective-permute-start(bf16[16,48,256]{2,1,0:T(8,128)(2,1)} %get-tuple-element.71), channel_id=1, source_target_pairs={{0,1},{1,2},{2,3},{3,4},{4,5},{5,6},{6,7},{8,9},{9,10},{10,11},{11... | collective-permute-start | bytes 1179656 | tf_op jit(solution)/shard_map/ppermute | solution.py:904
  136.3 16.5 %collective-permute-start.3 = (bf16[16,48,256]{2,1,0:T(8,128)(2,1)}, bf16[16,48,256]{2,1,0:T(8,128)(2,1)S(1)}, u32[]{:S(2)}, u32[]{:S(2)}) collective-permute-start(bf16[16,48,256]{2,1,0:T(8,128)(2,1)} %get-tuple-element.72), channel_id=1, source_target_pairs={{1,0},{2,1},{3,2},{4,3},{5,4},{6,5},{7,6},{9,8},{10,9},{11,10},{12... | collective-permute-start | bytes 1179656 | tf_op jit(solution)/shard_map/ppermute | solution.py:904
  152.8 0.8 copy-start.4
  152.8 0.9 copy-start.5
  160.7 2.0 collective-permute-start.4
  163.8 26.4 %copy-start.8 = (f32[16,4]{0,1:T(4,128)S(1)}, f32[16,4]{0,1:T(4,128)}, u32[]{:S(2)}) copy-start(f32[16,4]{0,1:T(4,128)} %param.34) | copy-start | bytes 772
  163.8 27.1 %copy-start.9 = (f32[16,4]{0,1:T(4,128)S(1)}, f32[16,4]{0,1:T(4,128)}, u32[]{:S(2)}) copy-start(f32[16,4]{0,1:T(4,128)} %param.37) | copy-start | bytes 772
  163.9 30.2 %copy-start.6 = (bf16[16,96,128]{2,1,0:T(8,128)(2,1)S(1)}, bf16[16,96,128]{2,1,0:T(8,128)(2,1)}, u32[]{:S(2)}) copy-start(bf16[16,96,128]{2,1,0:T(8,128)(2,1)} %get-tuple-element.80) | copy-start | bytes 1179652
  163.9 5.9 %collective-permute-start.5 = (bf16[560,128]{1,0:T(8,128)(2,1)S(1)}, bf16[560,128]{1,0:T(8,128)(2,1)S(1)}, u32[]{:S(2)}, u32[]{:S(2)}) collective-permute-start(bf16[560,128]{1,0:T(8,128)(2,1)S(1)} %dynamic-slice_convert_fusion), channel_id=1, source_target_pairs={{0,16},{8,24},{16,0},{24,8},{1,17},{9,25},{17,1},{25,9},{2,18},{10... | collective-permute-start | bytes 430088 | tf_op jit(solution)/shard_map/ppermute | solution.py:913
  169.8 5.7 %collective-permute-start.6 = (bf16[560,128]{1,0:T(8,128)(2,1)S(1)}, bf16[560,128]{1,0:T(8,128)(2,1)S(1)}, u32[]{:S(2)}, u32[]{:S(2)}) collective-permute-start(bf16[560,128]{1,0:T(8,128)(2,1)S(1)} %fusion.5), channel_id=1, source_target_pairs={{0,1},{1,0},{2,3},{3,2},{4,5},{5,4},{6,7},{7,6},{8,9},{9,8},{10,11... | collective-permute-start | bytes 430088 | tf_op jit(solution)/shard_map/ppermute | solution.py:913
  175.5 5.2 %collective-permute-start.7 = (bf16[560,128]{1,0:T(8,128)(2,1)S(1)}, bf16[560,128]{1,0:T(8,128)(2,1)S(1)}, u32[]{:S(2)}, u32[]{:S(2)}) collective-permute-start(bf16[560,128]{1,0:T(8,128)(2,1)S(1)} %fusion.1), channel_id=1, source_target_pairs={{0,2},{1,3},{2,0},{3,1},{4,6},{5,7},{6,4},{7,5},{8,10},{9,11},{10,... | collective-permute-start | bytes 430088 | tf_op jit(solution)/shard_map/ppermute | solution.py:913
  180.8 7.8 %collective-permute-start.8 = (bf16[560,128]{1,0:T(8,128)(2,1)S(1)}, bf16[560,128]{1,0:T(8,128)(2,1)S(1)}, u32[]{:S(2)}, u32[]{:S(2)}) collective-permute-start(bf16[560,128]{1,0:T(8,128)(2,1)S(1)} %fusion.2), channel_id=1, source_target_pairs={{0,4},{1,5},{2,6},{3,7},{4,0},{5,1},{6,2},{7,3},{8,12},{9,13},{10,... | collective-permute-start | bytes 430088 | tf_op jit(solution)/shard_map/ppermute | solution.py:913
  188.7 5.2 %collective-permute-start.9 = (bf16[560,128]{1,0:T(8,128)(2,1)S(1)}, bf16[560,128]{1,0:T(8,128)(2,1)S(1)}, u32[]{:S(2)}, u32[]{:S(2)}) collective-permute-start(bf16[560,128]{1,0:T(8,128)(2,1)S(1)} %add_convert_fusion), channel_id=1, source_target_pairs={{0,16},{8,24},{16,0},{24,8},{1,17},{9,25},{17,1},{25,9},{2,18},{10... | collective-permute-start | bytes 430088 | tf_op jit(solution)/shard_map/ppermute | solution.py:913
  194.0 1.6 collective-permute-start.10

commit v3 on v2

--- a/solution.py
+++ b/solution.py
@@ -16,8 +16,9 @@
 C = 128
 PAIR = 16
 NBLK = 17
-UNROLL = 8
+UNROLL = 16
 PACK = 2
+SLOTS = 3
 TILE = 512
 
 stat_decay = 0.5
@@ -31,9 +32,6 @@
 FACTOR = 1.0 / math.sqrt(C // HEADS)
 INVALID = -1000000000.0
 VMEM_LIMIT = 60 * 1024 * 1024
-VEC_AT = NBLK * C
-PW_AT = VEC_AT + 8
-PACKED = 2240
 
 
 def dot(left, right):
@@ -95,36 +93,46 @@
     return jnp.sum(values, axis=0, keepdims=True)
 
 
-def bias_kernel(pair_ref, pw_ref, bias_ref, root_ref, expand):
+def bias_kernel(pair_ref, pw_ref, bias_ref, root_ref, expand, flat):
     group = pl.program_id(1)
     per_step = bias_ref.shape[1]
     atoms = pl.num_programs(1) * per_step * QW
+    span = QW * PAIR
 
     @pl.when((pl.program_id(0) == 0) & (group == 0))
     def _():
-        rows = lax.broadcasted_iota(jnp.int32, (QW * PAIR, C), 0) // PAIR
-        lanes = lax.broadcasted_iota(jnp.int32, (QW * PAIR, C), 1) % QW
-        same = rows == lanes
-        weight = pw_ref[...] - jnp.mean(pw_ref[...], axis=0, keepdims=True)
-        full = jnp.where(same, jnp.concatenate([weight] * QW, axis=0), 0.0)
+        rows = lax.broadcasted_iota(jnp.int32, (span, C), 0) // PAIR
+        lanes = lax.broadcasted_iota(jnp.int32, (span, C), 1) % QW
+        wide = lax.dot_general(
+            pw_ref[...],
+            head_lanes(),
+            (((0,), (0,)), ((), ())),
+            precision=lax.Precision.HIGHEST,
+            preferred_element_type=F32,
+        )
+        weight = wide - jnp.mean(wide, axis=0, keepdims=True)
+        full = jnp.where(rows == lanes, jnp.concatenate([weight] * QW, axis=0), 0.0)
         high = full.astype(BF16)
         expand[:, :C] = high
-        expand[:, C : 2 * C] = (full - high.astype(F32)).astype(BF16)
-        expand[:, 2 * C :] = jnp.where(same, 1.0 / PAIR, 0.0).astype(BF16)
+        expand[:, C:] = (full - high.astype(F32)).astype(BF16)
 
     def one(w):
-        low = pair_ref[0, w * QW : w * QW + QW].reshape(QW * PAIR, KW)
-        wide = low.astype(F32)
-        square = wide * wide
-        high = square.astype(BF16)
-        rest = (square - high.astype(F32)).astype(BF16)
+        low = pair_ref[0, w * QW : w * QW + QW].reshape(span, KW)
+        flat[w * span : w * span + span] = low.astype(F32)
         yield
         out = dot_tn(low, expand[...])
-        second = dot_tn(high, expand[:, 2 * C :]) + dot_tn(rest, expand[:, 2 * C :])
-        yield
-        mean = out[:, 2 * C :]
-        root = lax.rsqrt(jnp.maximum(second - mean * mean, 0.0) + 1e-05)
-        value = (out[:, :C] + out[:, C : 2 * C]) * (root * LOG2E)
+        roots = []
+        for part in range(QW // 8):
+            start = w * span + part * 8 * PAIR
+            channels = [flat[pl.ds(start + c, 8, stride=PAIR), :] for c in range(PAIR)]
+            mean = sum(channels[1:], channels[0]) * (1.0 / PAIR)
+            center = [channel - mean for channel in channels]
+            squares = [value * value for value in center]
+            spread = sum(squares[1:], squares[0]) * (1.0 / PAIR)
+            roots.append(lax.rsqrt(spread + 1e-05))
+        yield
+        root = jnp.concatenate(roots * HEADS, axis=0).T
+        value = (out[:, :C] + out[:, C:]) * (root * LOG2E)
         start = lax.axis_index("win") * atoms + (group * per_step + w) * QW - HALO
         position = start + lax.broadcasted_iota(jnp.int32, (KW, C), 0)
         valid = (position >= 0) & (position < lax.axis_size("win") * atoms)
@@ -135,22 +143,29 @@
         pass
 
 
-def bias_table(pair, wide_weight):
+def head_lanes():
+    rows = lax.broadcasted_iota(jnp.int32, (HEADS, C), 0)
+    lanes = lax.broadcasted_iota(jnp.int32, (HEADS, C), 1) // QW
+    return jnp.where(rows == lanes, 1.0, 0.0)
+
+
+def bias_table(pair, turned_weight):
     structs, atoms = pair.shape[:2]
     count = min(8, atoms // QW)
     rows = count * QW
+    table = pl.BlockSpec((1, count, KW, C), lambda s, i: (s, i, 0, 0))
     return pl.pallas_call(
         bias_kernel,
         grid=(structs, atoms // rows),
         in_specs=[
             pl.BlockSpec((1, rows, PAIR, KW), lambda s, i: (s, i, 0, 0)),
-            pl.BlockSpec((PAIR, C), lambda s, i: (0, 0)),
+            pl.BlockSpec((HEADS, PAIR), lambda s, i: (0, 0)),
         ],
-        out_specs=[
-            pl.BlockSpec((1, count, KW, C), lambda s, i: (s, i, 0, 0)),
-            pl.BlockSpec((1, count, KW, C), lambda s, i: (s, i, 0, 0)),
+        out_specs=[table, table],
+        scratch_shapes=[
+            pltpu.VMEM((QW * PAIR, 2 * C), BF16),
+            pltpu.VMEM((rows * PAIR, KW), F32),
         ],
-        scratch_shapes=[pltpu.VMEM((QW * PAIR, 3 * C), BF16)],
         out_shape=[
             jax.ShapeDtypeStruct((structs, atoms // QW, KW, C), F32),
             jax.ShapeDtypeStruct((structs, atoms // QW, KW, C), BF16),
@@ -158,56 +173,7 @@
         compiler_params=pltpu.CompilerParams(vmem_limit_bytes=VMEM_LIMIT),
         cost_estimate=pl.CostEstimate(flops=10**9, bytes_accessed=15 * 2**20, transcendentals=0),
         name="pair_bias",
-    )(pair, wide_weight)
-
-
-def pair_grad_kernel(pair_ref, dbias_ref, root_ref, out_ref, total):
-    step = pl.program_id(0) * pl.num_programs(1) + pl.program_id(1)
-
-    @pl.when(step == 0)
-    def _():
-        total[...] = jnp.zeros_like(total)
-
-    parts = []
-    for w in range(dbias_ref.shape[1]):
-        low = pair_ref[0, w * QW : w * QW + QW].reshape(QW * PAIR, KW)
-        grad = (dbias_ref[0, w] * root_ref[0, w].astype(F32)).astype(BF16)
-        parts.append((low, grad))
-    for at in range(0, len(parts), 2):
-        pair_of = parts[at : at + 2]
-        left = jnp.concatenate([low for low, _ in pair_of], axis=1)
-        right = jnp.concatenate([grad for _, grad in pair_of], axis=0)
-        total[...] += dot(left, right)
-
-    @pl.when(step == pl.num_programs(0) * pl.num_programs(1) - 1)
-    def _():
-        lanes = lax.broadcasted_iota(jnp.int32, (PAIR, C), 1) % QW
-        acc = jnp.zeros((PAIR, C), F32)
-        for q in range(QW):
-            acc = acc + jnp.where(lanes == q, total[q * PAIR : q * PAIR + PAIR], 0.0)
-        out_ref[...] = acc - jnp.mean(acc, axis=0, keepdims=True)
-
-
-def pair_grad(pair, dbias, root):
-    structs, atoms = pair.shape[:2]
-    count = min(8, atoms // QW)
-    rows = count * QW
-    table = pl.BlockSpec((1, count, KW, C), lambda s, i: (s, i, 0, 0))
-    return pl.pallas_call(
-        pair_grad_kernel,
-        grid=(structs, atoms // rows),
-        in_specs=[
-            pl.BlockSpec((1, rows, PAIR, KW), lambda s, i: (s, i, 0, 0)),
-            table,
-            table,
-        ],
-        out_specs=pl.BlockSpec((PAIR, C), lambda s, i: (0, 0)),
-        scratch_shapes=[pltpu.VMEM((QW * PAIR, C), F32)],
-        out_shape=jax.ShapeDtypeStruct((PAIR, C), F32),
-        compiler_params=pltpu.CompilerParams(vmem_limit_bytes=VMEM_LIMIT),
-        cost_estimate=pl.CostEstimate(flops=10**9, bytes_accessed=15 * 2**20, transcendentals=0),
-        name="pair_grad",
-    )(pair, dbias, root)
+    )(pair, turned_weight)
 
 
 def main_kernel(
@@ -217,6 +183,8 @@
     xhi_ref,
     g_ref,
     bias_ref,
+    root_ref,
+    pair_ref,
     cond_ref,
     clo_ref,
     chi_ref,
@@ -224,14 +192,15 @@
     vec_ref,
     out_ref,
     grad_ref,
-    gxb_ref,
     rlo_ref,
     rhi_ref,
+    packed_ref,
+    small_ref,
     dbias_ref,
-    gw_ref,
     dvec_ref,
-    accb_ref,
-    tabb_ref,
+    pair_scr,
+    pair_sem,
+    pair_total,
     wq,
     w6,
     win,
@@ -257,6 +226,11 @@
     a_s2,
     a_h2,
     a_g2,
+    a_hs,
+    a_hh,
+    nh_scr,
+    ih_scr,
+    ah_scr,
     k_scr,
     v_scr,
     q_scr,
@@ -276,6 +250,7 @@
     step = pl.program_id(0)
     structs, atoms, _ = cond_ref.shape
     windows = atoms // QW
+    unroll = min(UNROLL, windows)
     tile = min(TILE, atoms)
     tiles = atoms // tile
     s = [lax.rem(ids_ref[step * PACK + b], structs) for b in range(PACK)]
@@ -286,11 +261,28 @@
         two = (normed * vec_ref[4:5]).astype(BF16)
         return normed, one, two
 
+    def block(at):
+        return packed_ref.at[at * C : at * C + C]
+
     def joined(ref, st):
         return ref[st].astype(F32) + ref[structs + st].astype(F32)
 
+    chunk = min(8, windows)
+    chunks = structs * windows // chunk
+
+    def pair_copy(at):
+        st, first = divmod(at * chunk, windows)
+        return pltpu.make_async_copy(
+            pair_ref.at[st, pl.ds(first * QW, chunk * QW)],
+            pair_scr.at[at % SLOTS],
+            pair_sem.at[at % SLOTS],
+        )
+
     @pl.when(step == 0)
     def _():
+        for at in range(min(SLOTS, chunks)):
+            pair_copy(at).start()
+
         def low(b):
             return w_ref[b].astype(BF16)
 
@@ -310,9 +302,10 @@
         rows_head = lax.broadcasted_iota(jnp.int32, (C, C), 0) // QW
         lane_head = lax.broadcasted_iota(jnp.int32, (C, C), 1) // (C // HEADS)
         mask[...] = jnp.where(rows_head == lane_head, 1.0, 0.0).astype(BF16)
-        for acc in (a_s1, a_h1, a_g1, a_s2, a_h2, a_g2, gw_ref, dvec_ref):
+        for acc in (a_s1, a_h1, a_g1, a_s2, a_h2, a_g2, a_hs, a_hh, packed_ref, dvec_ref):
             acc[...] = jnp.zeros_like(acc)
         dbias_ref[...] = jnp.zeros_like(dbias_ref)
+        pair_total[...] = jnp.zeros_like(pair_total)
         for st in range(structs):
 
             def table(i, carry):
@@ -333,10 +326,6 @@
             first = dot(one, wc1[:, : 2 * C])
             t_hs[st] = jax.nn.sigmoid(first[:, :C] + vec_ref[1:2])
             t_hh[st] = first[:, C:]
-            tabb_ref[0, st, :HALO] = t_s1[st, :HALO]
-            tabb_ref[0, st, HALO:] = t_s1[st, atoms - HALO :]
-            tabb_ref[1, st, :HALO] = t_h1[st, :HALO]
-            tabb_ref[1, st, HALO:] = t_h1[st, atoms - HALO :]
 
     def project(b, i):
         start = i * tile
@@ -357,8 +346,11 @@
 
     def project_halo(b):
         halo = jnp.concatenate([xlo_ref[b], xhi_ref[b]], axis=0).astype(F32)
-        normed, _ = layer_stats(halo)
+        normed, inverse = layer_stats(halo)
         ada = (t_hs[s[b]] * normed + t_hh[s[b]]).astype(BF16)
+        nh_scr[b] = normed
+        ih_scr[b] = jnp.broadcast_to(inverse, (2 * HALO, C))
+        ah_scr[b] = ada
         yield
         out = dot(ada, wq[:, 2 * C :])
         yield
@@ -450,11 +442,11 @@
         do_scr[b, rows] = do
         dd_scr[b, rows] = (do.astype(F32) * mixed * -1.0).astype(BF16)
         d4_scr[b, rows, C : 2 * C] = (dy * mixed * gate * (1.0 - gate)).astype(BF16)
-        gw_ref[15] += dwo[:, :C]
-        gw_ref[16] += dwo[:, C:]
+        block(15)[...] += dwo[:, :C]
+        block(16)[...] += dwo[:, C:]
         for at in range(4):
-            gw_ref[11 + at] += dwin[:, at * C : at * C + C]
-        gw_ref[6] += dw6
+            block(11 + at)[...] += dwin[:, at * C : at * C + C]
+        block(6)[...] += dw6
 
     dk_scr[...] = jnp.zeros_like(dk_scr)
     dv_scr[...] = jnp.zeros_like(dv_scr)
@@ -472,9 +464,9 @@
         yield
         grads = []
         for u, w in enumerate(group):
-            ds = p_scr[b, w] * diffs[u].astype(BF16)
-            dbias_ref[s[b], w] += ds.astype(F32)
-            grads.append(ds)
+            ds = p_scr[b, w].astype(F32) * diffs[u]
+            dbias_ref[s[b], w] += ds
+            grads.append(ds.astype(BF16))
         yield
         fulls = []
         dks = []
@@ -502,8 +494,8 @@
         dwq = dot_tn(ada_scr[b, rows], d4)
         dada = dot(d4, wqt[...])
         yield
-        for at, block in enumerate((2, 5, 3, 4)):
-            gw_ref[block] += dwq[:, at * C : at * C + C]
+        for at, which in enumerate((2, 5, 3, 4)):
+            block(which)[...] += dwq[:, at * C : at * C + C]
         normed = n1_scr[b, rows]
         a_s1[s[b], rows] += dada * normed
         a_h1[s[b], rows] += dada
@@ -511,7 +503,25 @@
         dx_scr[b, rows] = grad
         grad_ref[b, rows] = grad.astype(BF16)
 
-    groups = [tuple(range(at, at + UNROLL)) for at in range(0, windows, UNROLL)]
+    def finish_halo(b):
+        spans = (slice(0, HALO), slice(HALO + atoms, None))
+        dk = jnp.concatenate([dk_scr[b, span] for span in spans], axis=0) * FACTOR
+        dv = jnp.concatenate([dv_scr[b, span] for span in spans], axis=0)
+        dkv = jnp.concatenate([dk.astype(BF16), dv.astype(BF16)], axis=1)
+        yield
+        dw = dot_tn(ah_scr[b], dkv)
+        dada = dot(dkv, wqt[2 * C :])
+        yield
+        block(3)[...] += dw[:, :C]
+        block(4)[...] += dw[:, C:]
+        normed = nh_scr[b]
+        a_hs[s[b]] += dada * normed
+        a_hh[s[b]] += dada
+        rim = layer_back(normed, ih_scr[b], dada * t_hs[s[b]]).astype(BF16)
+        rlo_ref[b] = rim[:HALO]
+        rhi_ref[b] = rim[HALO:]
+
+    groups = [tuple(range(at, at + unroll)) for at in range(0, windows, unroll)]
 
     def phases(b):
         return [
@@ -519,57 +529,90 @@
             (4, [attend(b, group) for group in groups]),
             (11, [middle(b, i) for i in range(tiles)]),
             (4, [attend_back(b, group) for group in groups]),
-            (3, [finish(b, i) for i in range(tiles)]),
+            (3, [finish_halo(b)] + [finish(b, i) for i in range(tiles)]),
         ]
 
     together([phases(b) for b in range(PACK)])
-    for b in range(PACK):
-        gxb_ref[b, :HALO] = dx_scr[b, :HALO]
-        gxb_ref[b, HALO:] = dx_scr[b, atoms - HALO :]
-        for ref, span in ((rlo_ref, slice(0, HALO)), (rhi_ref, slice(HALO + atoms, None))):
-            ref[b, :, :C] = (dk_scr[b, span] * FACTOR).astype(BF16)
-            ref[b, :, C:] = dv_scr[b, span].astype(BF16)
 
     @pl.when(step == pl.num_programs(0) - 1)
     def _():
-        for b in (15, 16):
-            gw_ref[b] = gw_ref[b].T
-        for st in range(structs):
-            accb_ref[0, st, :HALO] = a_s1[st, :HALO]
-            accb_ref[0, st, HALO:] = a_s1[st, atoms - HALO :]
-            accb_ref[1, st, :HALO] = a_h1[st, :HALO]
-            accb_ref[1, st, HALO:] = a_h1[st, atoms - HALO :]
-            for acc in (a_s1, a_h1):
-                acc[st, :HALO] = jnp.zeros((HALO, C), F32)
-                acc[st, atoms - HALO :] = jnp.zeros((HALO, C), F32)
-
-            def conditioning(i, carry):
-                rows = pl.ds(pl.multiple_of(i * tile, tile), tile)
-                normed, one, two = cond_rows(cond_ref[st, rows])
-
-                def pre(acc, gate):
-                    return (acc[st, rows] * gate[st, rows] * (1.0 - gate[st, rows])).astype(BF16)
-
-                first = [pre(a_s1, t_s1), a_h1[st, rows].astype(BF16), pre(a_g1, t_g1)]
-                second = [pre(a_s2, t_s2), a_h2[st, rows].astype(BF16), pre(a_g2, t_g2)]
-                for at, part in ((1, first[0]), (3, first[2]), (5, second[0]), (6, second[2])):
-                    dvec_ref[at] += jnp.sum(part.astype(F32).reshape(tile // 8, 8, C), axis=0)
-                for at, source, parts, weight, blocks in (
-                    (0, one, first, wc1, (0, 1, 7)),
-                    (4, two, second, wc2, (8, 9, 10)),
-                ):
-                    joined = jnp.concatenate(parts, axis=1)
-                    grads = dot_tn(source, joined)
-                    for j, b in enumerate(blocks):
-                        gw_ref[b] += grads[:, j * C : j * C + C]
-                    back = dot_nt(joined, weight[...]) * normed
-                    dvec_ref[at] += jnp.sum(back.reshape(tile // 8, 8, C), axis=0)
-                return carry
-
-            lax.fori_loop(0, tiles, conditioning, 0)
-
-
-def main_call(ids, atoms, low_msg, high_msg, cotangent, bias, cond, weights, vectors):
+        for at in (15, 16):
+            block(at)[...] = block(at)[...].T
+
+        def apply(source, normed, parts, weight, blocks, gain):
+            joined_parts = jnp.concatenate(parts, axis=1)
+            grads = dot_tn(source, joined_parts)
+            back = dot_nt(joined_parts, weight) * normed
+            for at, which in enumerate(blocks):
+                block(which)[...] += grads[:, at * C : at * C + C]
+            dvec_ref[gain] += jnp.sum(back.reshape(-1, 8, C), axis=0)
+
+        def bias_sum(at, part):
+            dvec_ref[at] += jnp.sum(part.astype(F32).reshape(-1, 8, C), axis=0)
+
+        def pre(total, gate):
+            return (total * gate * (1.0 - gate)).astype(BF16)
+
+        def conditioning(st, i):
+            rows = pl.ds(i * tile, tile)
+            normed, one, two = cond_rows(cond_ref[st, rows])
+            first = [
+                pre(a_s1[st, rows], t_s1[st, rows]),
+                a_h1[st, rows].astype(BF16),
+                pre(a_g1[st, rows], t_g1[st, rows]),
+            ]
+            second = [
+                pre(a_s2[st, rows], t_s2[st, rows]),
+                a_h2[st, rows].astype(BF16),
+                pre(a_g2[st, rows], t_g2[st, rows]),
+            ]
+            yield
+            for at, part in ((1, first[0]), (3, first[2]), (5, second[0]), (6, second[2])):
+                bias_sum(at, part)
+            apply(one, normed, first, wc1[...], (0, 1, 7), 0)
+            apply(two, normed, second, wc2[...], (8, 9, 10), 4)
+
+        def conditioning_halo(st):
+            source = jnp.concatenate([joined(clo_ref, st), joined(chi_ref, st)], axis=0)
+            normed, one, _ = cond_rows(source)
+            parts = [pre(a_hs[st], t_hs[st]), a_hh[st].astype(BF16)]
+            yield
+            bias_sum(1, parts[0])
+            apply(one, normed, parts, wc1[:, : 2 * C], (0, 1), 0)
+
+        items = [conditioning_halo(st) for st in range(structs)]
+        items += [conditioning(st, i) for st in range(structs) for i in range(tiles)]
+        for _ in pipeline(items):
+            pass
+
+        for at in range(chunks):
+            pair_copy(at).wait()
+            st, first = divmod(at * chunk, windows)
+            lefts = []
+            rights = []
+            for w in range(chunk):
+                lefts.append(
+                    pair_scr[at % SLOTS, w * QW : w * QW + QW].reshape(QW * PAIR, KW)
+                )
+                grad = dbias_ref[st, first + w] * root_ref[st, first + w].astype(F32)
+                rights.append(grad.astype(BF16))
+            left = jnp.concatenate(lefts, axis=1)
+            pair_total[...] += dot(left, jnp.concatenate(rights, axis=0))
+            if at + SLOTS < chunks:
+                pair_copy(at + SLOTS).start()
+        lanes = lax.broadcasted_iota(jnp.int32, (PAIR, C), 1) % QW
+        acc = jnp.zeros((PAIR, C), F32)
+        for q in range(QW):
+            acc = acc + jnp.where(lanes == q, pair_total[q * PAIR : q * PAIR + PAIR], 0.0)
+        small_ref[8:] = acc - jnp.mean(acc, axis=0, keepdims=True)
+        small_ref[:8] = jnp.concatenate(
+            [rows_sum(dvec_ref[at]) for at in range(7)] + [jnp.zeros((1, C), F32)], axis=0
+        )
+
+
+def main_call(
+    ids, atoms, low_msg, high_msg, cotangent, bias, root, pair, cond, weights, vectors
+):
     samples, rows, _ = atoms.shape
     structs = cond.shape[0]
     windows = rows // QW
@@ -599,6 +642,8 @@
                 per_sample(HALO, C),
                 per_sample(rows, C),
                 whole(structs, windows, KW, C),
+                whole(structs, windows, KW, C),
+                pl.BlockSpec(memory_space=pl.ANY),
                 whole(structs, rows, C),
                 cond_part,
                 cond_part,
@@ -608,16 +653,17 @@
             out_specs=[
                 per_sample(rows, C),
                 per_sample(rows, C),
-                per_sample(2 * HALO, C),
-                per_sample(HALO, 2 * C),
-                per_sample(HALO, 2 * C),
-                whole(structs, windows, KW, C),
-                whole(NBLK, C, C),
-                whole(7, 8, C),
-                whole(2, structs, 2 * HALO, C),
-                whole(2, structs, 2 * HALO, C),
+                per_sample(HALO, C),
+                per_sample(HALO, C),
+                whole(NBLK * C, C),
+                whole(8 + PAIR, C),
             ],
             scratch_shapes=[
+                pltpu.VMEM((structs, windows, KW, C), F32),
+                pltpu.VMEM((7, 8, C), F32),
+                pltpu.VMEM((SLOTS, min(rows, 8 * QW), PAIR, KW), BF16),
+                pltpu.SemaphoreType.DMA((SLOTS,)),
+                pltpu.VMEM((QW * PAIR, C), F32),
                 pltpu.VMEM((C, 4 * C), BF16),
                 pltpu.VMEM((C, C), BF16),
                 pltpu.VMEM((C, 2 * FF), BF16),
@@ -643,6 +689,11 @@
                 table(),
                 table(),
                 table(),
+                table(2 * HALO),
+                table(2 * HALO),
+                pltpu.VMEM((PACK, 2 * HALO, C), F32),
+                pltpu.VMEM((PACK, 2 * HALO, C), F32),
+                pltpu.VMEM((PACK, 2 * HALO, C), BF16),
                 pltpu.VMEM((PACK, padded, C), BF16),
                 pltpu.VMEM((PACK, padded, C), BF16),
                 pltpu.VMEM((PACK, rows, C), BF16),
@@ -663,115 +714,28 @@
         out_shape=[
             shape((samples, rows, C), BF16),
             shape((samples, rows, C), BF16),
-            shape((samples, 2 * HALO, C), F32),
-            shape((samples, HALO, 2 * C), BF16),
-            shape((samples, HALO, 2 * C), BF16),
-            shape((structs, windows, KW, C), F32),
-            shape((NBLK, C, C), F32),
-            shape((7, 8, C), F32),
-            shape((2, structs, 2 * HALO, C), F32),
-            shape((2, structs, 2 * HALO, C), F32),
+            shape((samples, HALO, C), BF16),
+            shape((samples, HALO, C), BF16),
+            shape((NBLK * C, C), F32),
+            shape((8 + PAIR, C), F32),
         ],
         compiler_params=pltpu.CompilerParams(vmem_limit_bytes=VMEM_LIMIT),
         name="block",
-    )(ids, atoms, low_msg, high_msg, cotangent, bias, cond, low_msg, high_msg, weights, vectors)
-
-
-def rim_kernel(
-    ids_ref,
-    below_ref,
-    above_ref,
-    first_ref,
-    last_ref,
-    gxb_ref,
-    tab_ref,
-    acc_ref,
-    w_ref,
-    vec_ref,
-    gw_ref,
-    dvec_ref,
-    dpair_ref,
-    grad_ref,
-    packed_ref,
-    sums,
-    dw,
-):
-    samples = below_ref.shape[0]
-    structs = tab_ref.shape[1]
-    sums[...] = acc_ref[...]
-    dw[...] = jnp.zeros_like(dw)
-    weight = jnp.concatenate([w_ref[3], w_ref[4]], axis=1).astype(BF16).T
-    vecs = VEC_AT
-    packed_ref[:vecs] = gw_ref[...].reshape(NBLK * C, C)
-    packed_ref[vecs : vecs + 8] = jnp.concatenate(
-        [jnp.sum(dvec_ref[at], axis=0, keepdims=True) for at in range(7)] + [jnp.zeros((1, C), F32)],
-        axis=0,
+    )(
+        ids,
+        atoms,
+        low_msg,
+        high_msg,
+        cotangent,
+        bias,
+        root,
+        pair,
+        cond,
+        low_msg,
+        high_msg,
+        weights,
+        vectors,
     )
-    packed_ref[PW_AT : PW_AT + PAIR] = dpair_ref[...]
-    packed_ref[PW_AT + PAIR :] = jnp.zeros((PACKED - PW_AT - PAIR, C), F32)
-
-    def one(i):
-        s = lax.rem(ids_ref[i], structs)
-        x = jnp.concatenate([first_ref[i], last_ref[i]], axis=0).astype(F32)
-        normed, inverse = layer_stats(x)
-        scale = tab_ref[0, s]
-        ada = (scale * normed + tab_ref[1, s]).astype(BF16)
-        dkv = jnp.concatenate([below_ref[i], above_ref[i]], axis=0)
-        dada = dot(dkv, weight)
-        yield
-        part = dot_tn(ada, dkv)
-        grad_norm = dada * scale
-        grad = gxb_ref[i] + layer_back(normed, inverse, grad_norm)
-        yield
-        dw[...] += part
-        sums[0, s] += dada * normed
-        sums[1, s] += dada
-        grad_ref[i] = grad.astype(BF16)
-
-    for _ in pipeline([one(i) for i in range(samples)]):
-        pass
-    packed_ref[3 * C : 4 * C] += dw[:, :C]
-    packed_ref[4 * C : 5 * C] += dw[:, C:]
-    weight = jnp.concatenate([w_ref[0], w_ref[1]], axis=1).astype(BF16)
-    for st in range(structs):
-        at = samples + st
-        cond = jnp.concatenate([first_ref[at], last_ref[at]], axis=0).astype(F32)
-        at = samples + structs + st
-        cond = cond + jnp.concatenate([first_ref[at], last_ref[at]], axis=0).astype(F32)
-        normed, _ = layer_stats(cond)
-        source = (normed * vec_ref[0:1]).astype(BF16)
-        scale = tab_ref[0, st]
-        pre_scale = (sums[0, st] * scale * (1.0 - scale)).astype(BF16)
-        pre_shift = sums[1, st].astype(BF16)
-        joined = jnp.concatenate([pre_scale, pre_shift], axis=1)
-        grads = dot_tn(source, joined)
-        packed_ref[:C] += grads[:, :C]
-        packed_ref[C : 2 * C] += grads[:, C:]
-        back = dot_nt(joined, weight) * normed
-        packed_ref[vecs : vecs + 1] += rows_sum(back)
-        packed_ref[vecs + 1 : vecs + 2] += rows_sum(pre_scale.astype(F32))
-
-
-def rim_call(ids, below, above, first, last, gxb, tab, acc, weights, vectors, gw, dvec, dpair):
-    samples = below.shape[0]
-    structs = tab.shape[1]
-    full = pl.BlockSpec(memory_space=pltpu.VMEM)
-    shape = jax.ShapeDtypeStruct
-    return pl.pallas_call(
-        rim_kernel,
-        in_specs=[pl.BlockSpec(memory_space=pltpu.SMEM)] + [full] * 12,
-        out_specs=[full] * 2,
-        out_shape=[
-            shape((samples, 2 * HALO, C), BF16),
-            shape((PACKED, C), F32),
-        ],
-        scratch_shapes=[
-            pltpu.VMEM((2, structs, 2 * HALO, C), F32),
-            pltpu.VMEM((C, 2 * C), F32),
-        ],
-        compiler_params=pltpu.CompilerParams(vmem_limit_bytes=VMEM_LIMIT),
-        name="rims",
-    )(ids, below, above, first, last, gxb, tab, acc, weights, vectors, gw, dvec, dpair)
 
 
 def split_low(values):
@@ -781,6 +745,7 @@
 
 def update_kernel(
     total_ref,
+    small_ref,
     sl_ref,
     sr_ref,
     rl_ref,
@@ -847,12 +812,16 @@
 
     for _ in pipeline([one(b) for b in range(NBLK)]):
         pass
-    sums = total_ref[PW_AT : PW_AT + PAIR]
-    pair_total = jnp.concatenate(
-        [jnp.sum(sums[:, h * QW : h * QW + QW], axis=1, keepdims=True) for h in range(HEADS)], axis=1
+    sums = small_ref[8:]
+    pair_total = lax.dot_general(
+        head_lanes(),
+        sums,
+        (((1,), (1,)), ((), ())),
+        precision=lax.Precision.HIGHEST,
+        preferred_element_type=F32,
     )
     for total, param, stat, ema, out, new_ref, stat_ref, ema_ref in (
-        (total_ref[VEC_AT : VEC_AT + 7], vec_ref, sv_ref, ev_ref, tv_ref, newv_ref, nsv_ref, newv_ema_ref),
+        (small_ref[:7], vec_ref, sv_ref, ev_ref, tv_ref, newv_ref, nsv_ref, newv_ema_ref),
         (pair_total, pw_ref, sp_ref, ep_ref, tp_ref, newp_ref, nsp_ref, newp_ema_ref),
     ):
         out[...] = total
@@ -864,33 +833,26 @@
 
 
 def update_call(*args):
-    rows = args[1].shape
-    vec = args[7].shape
-    pw = args[10].shape
+    rows = args[2].shape
+    vec = args[8].shape
+    pw = args[11].shape
     full = pl.BlockSpec(memory_space=pltpu.VMEM)
 
     def shape(dims, kind=F32):
         return jax.ShapeDtypeStruct(dims, kind)
 
+    def out_block(dims):
+        zeros = (0,) * len(dims)
+        return pl.BlockSpec(dims, lambda i: zeros)
+
+    outs = [rows, vec, pw, rows, rows, rows, rows, vec, pw, vec, pw, rows, vec, pw]
     return pl.pallas_call(
         update_kernel,
+        grid=(1,),
         in_specs=[full] * len(args),
-        out_specs=[full] * 14,
+        out_specs=[out_block(dims) for dims in outs],
         out_shape=[
-            shape(rows),
-            shape(vec),
-            shape(pw),
-            shape(rows),
-            shape(rows),
-            shape(rows),
-            shape(rows, BF16),
-            shape(vec),
-            shape(pw),
-            shape(vec),
-            shape(pw),
-            shape(rows),
-            shape(vec),
-            shape(pw),
+            shape(dims, BF16 if at == 6 else F32) for at, dims in enumerate(outs)
         ],
         scratch_shapes=[pltpu.VMEM((NBLK, C, C), F32)],
         compiler_params=pltpu.CompilerParams(vmem_limit_bytes=VMEM_LIMIT),
@@ -918,20 +880,39 @@
     return [(axis, 1 << at) for at in range((devices - 1).bit_length())]
 
 
-def summed(values):
+def summed(values, small, after):
     halvings = bits("samp")
+    count = small.shape[0]
+
+    def exchange(part, axis, bit):
+        high = rounded(small)
+        rest = rounded(small - high)
+        message = [part.astype(BF16), high.astype(BF16), rest.astype(BF16)]
+        got = partner(jnp.concatenate(message, axis=0), axis, bit).astype(F32)
+        size = part.shape[0]
+        total = (high + rest) + (got[size : size + count] + got[size + count :])
+        return got[:size], total
+
     for at, (axis, bit) in enumerate(halvings):
         side = (lax.axis_index(axis) // bit) % 2
         half = values.shape[0] // 2
         send = lax.dynamic_slice_in_dim(values, (1 - side) * half, half)
         keep = lax.dynamic_slice_in_dim(values, side * half, half)
-        wire = F32 if at == 0 else BF16
-        values = keep + partner(send.astype(wire), axis, bit).astype(F32)
-    for axis, bit in bits("win"):
+        if at == 0:
+            got = partner(jnp.concatenate([send, small], axis=0), axis, bit)
+            small = small + got[half:]
+            values = keep + got[:half]
+        else:
+            got, small = exchange(send, axis, bit)
+            values = keep + got
+    for at, (axis, bit) in enumerate(bits("win")):
         values = rounded(values)
-        values = values + partner(values.astype(BF16), axis, bit).astype(F32)
+        got, small = exchange(values, axis, bit)
+        values = values + got
+        if at == 1:
+            values, after = lax.optimization_barrier((values, after))
     values = values.astype(BF16)
-    for axis, bit in reversed(halvings):
+    for at, (axis, bit) in enumerate(reversed(halvings)):
         side = (lax.axis_index(axis) // bit) % 2
         other = partner(values, axis, bit)
         values = jnp.where(
@@ -939,7 +920,7 @@
             jnp.concatenate([values, other]),
             jnp.concatenate([other, values]),
         )
-    return values.astype(F32)
+    return values.astype(F32), small, after
 
 
 def body(
@@ -970,34 +951,37 @@
         messages.append(jnp.concatenate(parts, axis=0))
     first, last = messages
     low_msg, high_msg = passed(last, 1), passed(first, -1)
-    bias, root = bias_table(pair, jnp.repeat(pair_weight, QW, axis=1))
-    (result, grad_atoms, gxb, rim_low, rim_high, dbias, gw, dvec, accb, tabb) = main_call(
-        struct_ids, atoms, low_msg, high_msg, cotangent, bias, cond, weights, vectors
+    bias, root = bias_table(pair, pair_weight.T)
+    result, grad_atoms, rim_low, rim_high, packed, small = main_call(
+        struct_ids, atoms, low_msg, high_msg, cotangent, bias, root, pair, cond, weights, vectors
     )
     above = passed(rim_low, -1)
     below = passed(rim_high, 1)
-    dpair = pair_grad(pair, dbias, root)
-    grad_rim, packed = rim_call(
-        struct_ids, below, above, first, last, gxb, tabb, accb, weights, vectors, gw, dvec, dpair
+    packed, small, (below, above) = summed(packed, small, (below, above))
+    for span, part in ((slice(0, HALO), below), (slice(rows - HALO, rows), above)):
+        edge = grad_atoms[:, span].astype(F32) + part.astype(F32)
+        grad_atoms = grad_atoms.at[:, span].set(edge.astype(BF16))
+    outs = list(
+        update_call(
+            packed,
+            small,
+            stat_left,
+            stat_right,
+            root_left,
+            root_right,
+            weights,
+            ema_weights,
+            vectors,
+            stat_vectors,
+            ema_vectors,
+            pair_weight.T,
+            stat_pair.T,
+            ema_pair.T,
+        )
     )
-    grad_atoms = grad_atoms.at[:, :HALO].set(grad_rim[:, :HALO])
-    grad_atoms = grad_atoms.at[:, rows - HALO :].set(grad_rim[:, HALO:])
-    updated = update_call(
-        summed(packed),
-        stat_left,
-        stat_right,
-        root_left,
-        root_right,
-        weights,
-        ema_weights,
-        vectors,
-        stat_vectors,
-        ema_vectors,
-        pair_weight,
-        stat_pair,
-        ema_pair,
-    )
-    return (result, grad_atoms, *updated)
+    for at in (2, 8, 10, 13):
+        outs[at] = outs[at].T
+    return (result, grad_atoms, *outs)
 
 
 def solution(mesh):

time: 209 us -> 192 us (0.919)
  local copies, waits for them, and re-layouts: 13.6 us -> 3.06 us
  Pallas kernels: 140 us -> 132 us
  other arithmetic: 3.58 us -> 7.3 us
    pallas_call x3 -> x1, Pallas kernels: 20.8 us -> 5.74 us  [update_call(): pl.pallas_call(update_kernel, grid=(1,), in_specs=[full] * len(args), out...]
    unnamed x27 -> x12, local copies, waits for them, and re-layouts: 9.18 us -> 0.79 us
    pallas_call x1, Pallas kernels: 106 us -> 114 us  [main_call(): pl.pallas_call(main_kernel, grid_spec=pltpu.PrefetchScalarGridSpec(num_sc...]
    scatter x0 -> x2, other arithmetic: none -> 3.32 us  [body(): grad_atoms = grad_atoms.at[:, span].set(edge.astype(BF16))]
    ppermute x4, starting transfers between devices: 12.9 us -> 9.99 us  [passed(): return lax.ppermute(shard, 'win', pairs)]
    ppermute x7, starting transfers between devices: 10.7 us -> 13 us  [partner(): return lax.ppermute(values, axis, [(i, i ^ bit) for i in range(devices)])]
  transfers between devices with their start and end apart: 11 -> 11, of which waited for: 8 -> 7; matrix products, arithmetic and copies ran while one was open for 2% -> 2% of each run, Pallas kernels for 11% -> 7%
where the time goes in v3:
time: 192 us; the launch traced here: 191 us
  Pallas kernels  132 us (69%)
  waiting for transfers between devices  24.3 us (13%)
  starting transfers between devices  23 us (12%)
  other arithmetic  7.3 us (4%)
  local copies, waits for them, and re-layouts  3.06 us (2%)
    pallas_call x1, Pallas kernels, main_call(): pl.pallas_call(main_kernel, grid_spec=pltpu.PrefetchScalarGridSpec(num_sc...  114 us
    ppermute x7, waiting for transfers between devices, partner(): return lax.ppermute(values, axis, [(i, i ^ bit) for i in range(devices)])  18.1 us
    ppermute x7, starting transfers between devices, partner(): return lax.ppermute(values, axis, [(i, i ^ bit) for i in range(devices)])  13 us
    pallas_call x1, Pallas kernels, bias_table(): pl.pallas_call(bias_kernel, grid=(structs, atoms // rows), in_specs=[pl.B...  12.9 us
    ppermute x4, starting transfers between devices, passed(): return lax.ppermute(shard, 'win', pairs)  9.99 us
    ppermute x4, waiting for transfers between devices, passed(): return lax.ppermute(shard, 'win', pairs)  6.14 us
    pallas_call x1, Pallas kernels, update_call(): pl.pallas_call(update_kernel, grid=(1,), in_specs=[full] * len(args), out...  5.74 us
  transfers between devices with their start and end apart: 11, of which 7 were waited for; matrix products, arithmetic and copies ran while one was open for 2% of the time, Pallas kernels for 7%

profile of v3, /device:TPU:0, one launch (start us, length us, event | category | flops | bytes accessed | tf_op | source)
XLA Modules:
  0.0 191.1 jit_solution(14416663332729688706)
XLA Ops:
  0.6 0.8 reduce-precision_convert_fusion.1
  1.5 1.1 fusion.26
  2.6 4.9 %collective-permute-start = (bf16[20,48,128]{2,1,0:T(8,128)(2,1)S(1)}, bf16[20,48,128]{2,1,0:T(8,128)(2,1)S(1)}, u32[]{:S(2)}, u32[]{:S(2)}) collective-permute-start(bf16[20,48,128]{2,1,0:T(8,128)(2,1)S(1)} %pad_maximum_fusion.1), channel_id=1, source_target_pairs={{0,1},{1,2},{2,3},{3,4},{4,5},{5,6},{6,7},{8,9},{9,10},{10,11},{11... | collective-permute-start | bytes 737288 | tf_op jit(solution)/shard_map/ppermute | solution.py:866
  7.5 1.3 collective-permute-start.1
  8.9 12.9 %pair_bias.1 = (f32[2,32,128,128]{3,2,1,0:T(8,128)}, bf16[2,32,128,128]{3,2,1,0:T(8,128)(2,1)}) custom-call(bf16[2,1024,16,128]{3,2,1,0:T(8,128)(2,1)} %pair_ref.3, f32[4,16]{1,0:T(4,128)} %bitcast.7), custom_call_target="tpu_custom_call" | custom-call | flops 1000000000 | bytes 15728640 | tf_op jit(solution)/shard_map/pair_bias/pallas_call | solution.py:157
  22.6 113.7 %block.1 = (bf16[16,1024,128]{2,1,0:T(8,128)(2,1)}, bf16[16,1024,128]{2,1,0:T(8,128)(2,1)}, bf16[16,48,128]{2,1,0:T(8,128)(2,1)}, bf16[16,48,128]{2,1,0:T(8,128)...) custom-call(s32[16]{0:T(128)} %ids_ref.1, bf16[16,1024,128]{2,1,0:T(8,128)(2,1)} %x_ref.1, bf16[20,48,128]{2,1,0:T(8,128)(2,1)} %copy-done.1, ...), custom_call_target="tpu_custom_call" | custom-call | tf_op jit(solution)/shard_map/block/pallas_call | solution.py:634
  136.3 1.2 constant_dynamic-slice_fusion
  138.4 1.9 %collective-permute-done.2 = f32[1112,128]{1,0:T(8,128)S(1)} collective-permute-done((f32[1112,128]{1,0:T(8,128)S(1)}, f32[1112,128]{1,0:T(8,128)S(1)}, u32[]{:S(2)}, u32[]{:S(2)}) %collective-permute-start.2) | collective-permute-done | bytes 569376 | tf_op jit(solution)/shard_map/ppermute | solution.py:875
  140.5 1.6 collective-permute-start.3
  142.0 4.5 %collective-permute-done.3 = bf16[592,128]{1,0:T(8,128)(2,1)S(1)} collective-permute-done((bf16[592,128]{1,0:T(8,128)(2,1)S(1)}, bf16[592,128]{1,0:T(8,128)(2,1)S(1)}, u32[]{:S(2)}, u32[]{:S(2)}) %collective-permute-start.3) | collective-permute-done | bytes 151584 | tf_op jit(solution)/shard_map/ppermute | solution.py:875
  146.6 2.7 %collective-permute-start.4 = (bf16[592,128]{1,0:T(8,128)(2,1)S(1)}, bf16[592,128]{1,0:T(8,128)(2,1)S(1)}, u32[]{:S(2)}, u32[]{:S(2)}) collective-permute-start(bf16[592,128]{1,0:T(8,128)(2,1)S(1)} %pad_maximum_fusion.4), channel_id=1, source_target_pairs={{0,1},{1,0},{2,3},{3,2},{4,5},{5,4},{6,7},{7,6},{8,9},{9,8},{10,11... | collective-permute-start | bytes 454664 | tf_op jit(solution)/shard_map/ppermute | solution.py:875
  149.3 3.4 %collective-permute-done.4 = bf16[592,128]{1,0:T(8,128)(2,1)S(1)} collective-permute-done((bf16[592,128]{1,0:T(8,128)(2,1)S(1)}, bf16[592,128]{1,0:T(8,128)(2,1)S(1)}, u32[]{:S(2)}, u32[]{:S(2)}) %collective-permute-start.4) | collective-permute-done | bytes 151584 | tf_op jit(solution)/shard_map/ppermute | solution.py:875
  152.9 2.8 %collective-permute-start.5 = (bf16[592,128]{1,0:T(8,128)(2,1)S(1)}, bf16[592,128]{1,0:T(8,128)(2,1)S(1)}, u32[]{:S(2)}, u32[]{:S(2)}) collective-permute-start(bf16[592,128]{1,0:T(8,128)(2,1)S(1)} %pad_maximum_fusion.5), channel_id=1, source_target_pairs={{0,2},{1,3},{2,0},{3,1},{4,6},{5,7},{6,4},{7,5},{8,10},{9,11},{10,... | collective-permute-start | bytes 454664 | tf_op jit(solution)/shard_map/ppermute | solution.py:875
  155.7 2.5 %collective-permute-start.6 = (bf16[16,48,128]{2,1,0:T(8,128)(2,1)S(1)}, bf16[16,48,128]{2,1,0:T(8,128)(2,1)S(1)}, u32[]{:S(2)}, u32[]{:S(2)}) collective-permute-start(bf16[16,48,128]{2,1,0:T(8,128)(2,1)S(1)} %copy-done.5), channel_id=1, source_target_pairs={{0,1},{1,2},{2,3},{3,4},{4,5},{5,6},{6,7},{8,9},{9,10},{10,11},{11... | collective-permute-start | bytes 589832 | tf_op jit(solution)/shard_map/ppermute | solution.py:866
  158.2 1.3 collective-permute-start.7
  159.6 6.0 %collective-permute-done.6 = bf16[16,48,128]{2,1,0:T(8,128)(2,1)S(1)} collective-permute-done((bf16[16,48,128]{2,1,0:T(8,128)(2,1)S(1)}, bf16[16,48,128]{2,1,0:T(8,128)(2,1)S(1)}, u32[]{:S(2)}, u32[]{:S(2)}) %collective-permute-start.6) | collective-permute-done | bytes 196640 | tf_op jit(solution)/shard_map/ppermute | solution.py:866
  165.8 4.2 %collective-permute-start.8 = (bf16[592,128]{1,0:T(8,128)(2,1)S(1)}, bf16[592,128]{1,0:T(8,128)(2,1)S(1)}, u32[]{:S(2)}, u32[]{:S(2)}) collective-permute-start(bf16[592,128]{1,0:T(8,128)(2,1)S(1)} %pad_maximum_fusion.6), channel_id=1, source_target_pairs={{0,4},{1,5},{2,6},{3,7},{4,0},{5,1},{6,2},{7,3},{8,12},{9,13},{10,... | collective-permute-start | bytes 454664 | tf_op jit(solution)/shard_map/ppermute | solution.py:875
  170.0 6.4 %collective-permute-done.8 = bf16[592,128]{1,0:T(8,128)(2,1)S(1)} collective-permute-done((bf16[592,128]{1,0:T(8,128)(2,1)S(1)}, bf16[592,128]{1,0:T(8,128)(2,1)S(1)}, u32[]{:S(2)}, u32[]{:S(2)}) %collective-permute-start.8) | collective-permute-done | bytes 151584 | tf_op jit(solution)/shard_map/ppermute | solution.py:875
  176.5 1.6 collective-permute-start.9
  178.1 1.7 fusion.4
  179.8 1.9 collective-permute-done.9
  181.8 1.7 fusion.5
  184.1 1.1 fusion.total_ref
  185.2 5.7 %update.1 = (f32[17,16,128]{2,1,0:T(8,128)}, f32[7,128]{1,0:T(8,128)}, f32[4,16]{1,0:T(4,128)}, f32[17,16,128]{2,1,0:T(8,128)}, f32[17,16,128]{2,1,0:T(8,128)}, ...) custom-call(f32[2176,128]{1,0:T(8,128)} %fusion.total_ref, ...), custom_call_target="tpu_custom_call" | custom-call | tf_op jit(solution)/shard_map/update/pallas_call | solution.py:849
  (46 shorter events, 3.1 us)
Async XLA Ops:
  2.6 19.2 %collective-permute-start = (bf16[20,48,128]{2,1,0:T(8,128)(2,1)S(1)}, bf16[20,48,128]{2,1,0:T(8,128)(2,1)S(1)}, u32[]{:S(2)}, u32[]{:S(2)}) collective-permute-start(bf16[20,48,128]{2,1,0:T(8,128)(2,1)S(1)} %pad_maximum_fusion.1), channel_id=1, source_target_pairs={{0,1},{1,2},{2,3},{3,4},{4,5},{5,6},{6,7},{8,9},{9,10},{10,11},{11... | collective-permute-start | bytes 737288 | tf_op jit(solution)/shard_map/ppermute | solution.py:866
  7.5 14.3 %collective-permute-start.1 = (bf16[20,48,128]{2,1,0:T(8,128)(2,1)S(1)}, bf16[20,48,128]{2,1,0:T(8,128)(2,1)S(1)}, u32[]{:S(2)}, u32[]{:S(2)}) collective-permute-start(bf16[20,48,128]{2,1,0:T(8,128)(2,1)S(1)} %pad_maximum_fusion.2), channel_id=1, source_target_pairs={{1,0},{2,1},{3,2},{4,3},{5,4},{6,5},{7,6},{9,8},{10,9},{11,10},{12... | collective-permute-start | bytes 737288 | tf_op jit(solution)/shard_map/ppermute | solution.py:866
  21.8 0.7 copy-start.1
  21.8 0.8 copy-start.2
  136.3 4.0 %copy-start = (f32[2176,128]{1,0:T(8,128)S(1)}, f32[2176,128]{1,0:T(8,128)}, u32[]{:S(2)}) copy-start(f32[2176,128]{1,0:T(8,128)} %get-tuple-element.69) | copy-start | bytes 3342340
  136.3 4.1 %copy-start.3 = (f32[24,128]{1,0:T(8,128)S(1)}, f32[24,128]{1,0:T(8,128)}, u32[]{:S(2)}) copy-start(f32[24,128]{1,0:T(8,128)} %get-tuple-element.70) | copy-start | bytes 36868
  138.2 2.0 %collective-permute-start.2 = (f32[1112,128]{1,0:T(8,128)S(1)}, f32[1112,128]{1,0:T(8,128)S(1)}, u32[]{:S(2)}, u32[]{:S(2)}) collective-permute-start(f32[1112,128]{1,0:T(8,128)S(1)} %pad_maximum_fusion), channel_id=1, source_target_pairs={{0,8},{8,0},{16,24},{24,16},{1,9},{9,1},{17,25},{25,17},{2,10},{10... | collective-permute-start | bytes 1708040 | tf_op jit(solution)/shard_map/ppermute | solution.py:875
  140.4 15.3 %copy-start.5 = (bf16[16,48,128]{2,1,0:T(8,128)(2,1)S(1)}, bf16[16,48,128]{2,1,0:T(8,128)(2,1)}, u32[]{:S(2)}) copy-start(bf16[16,48,128]{2,1,0:T(8,128)(2,1)} %get-tuple-element.71) | copy-start | bytes 589828
  140.4 17.8 %copy-start.4 = (bf16[16,48,128]{2,1,0:T(8,128)(2,1)S(1)}, bf16[16,48,128]{2,1,0:T(8,128)(2,1)}, u32[]{:S(2)}) copy-start(bf16[16,48,128]{2,1,0:T(8,128)(2,1)} %get-tuple-element.72) | copy-start | bytes 589828
  140.5 6.0 %collective-permute-start.3 = (bf16[592,128]{1,0:T(8,128)(2,1)S(1)}, bf16[592,128]{1,0:T(8,128)(2,1)S(1)}, u32[]{:S(2)}, u32[]{:S(2)}) collective-permute-start(bf16[592,128]{1,0:T(8,128)(2,1)S(1)} %pad_maximum_fusion.3), channel_id=1, source_target_pairs={{0,16},{8,24},{16,0},{24,8},{1,17},{9,25},{17,1},{25,9},{2,18},{10... | collective-permute-start | bytes 454664 | tf_op jit(solution)/shard_map/ppermute | solution.py:875
  146.6 6.1 %collective-permute-start.4 = (bf16[592,128]{1,0:T(8,128)(2,1)S(1)}, bf16[592,128]{1,0:T(8,128)(2,1)S(1)}, u32[]{:S(2)}, u32[]{:S(2)}) collective-permute-start(bf16[592,128]{1,0:T(8,128)(2,1)S(1)} %pad_maximum_fusion.4), channel_id=1, source_target_pairs={{0,1},{1,0},{2,3},{3,2},{4,5},{5,4},{6,7},{7,6},{8,9},{9,8},{10,11... | collective-permute-start | bytes 454664 | tf_op jit(solution)/shard_map/ppermute | solution.py:875
  152.9 6.6 %collective-permute-start.5 = (bf16[592,128]{1,0:T(8,128)(2,1)S(1)}, bf16[592,128]{1,0:T(8,128)(2,1)S(1)}, u32[]{:S(2)}, u32[]{:S(2)}) collective-permute-start(bf16[592,128]{1,0:T(8,128)(2,1)S(1)} %pad_maximum_fusion.5), channel_id=1, source_target_pairs={{0,2},{1,3},{2,0},{3,1},{4,6},{5,7},{6,4},{7,5},{8,10},{9,11},{10,... | collective-permute-start | bytes 454664 | tf_op jit(solution)/shard_map/ppermute | solution.py:875
  155.7 9.9 %collective-permute-start.6 = (bf16[16,48,128]{2,1,0:T(8,128)(2,1)S(1)}, bf16[16,48,128]{2,1,0:T(8,128)(2,1)S(1)}, u32[]{:S(2)}, u32[]{:S(2)}) collective-permute-start(bf16[16,48,128]{2,1,0:T(8,128)(2,1)S(1)} %copy-done.5), channel_id=1, source_target_pairs={{0,1},{1,2},{2,3},{3,4},{4,5},{5,6},{6,7},{8,9},{9,10},{10,11},{11... | collective-permute-start | bytes 589832 | tf_op jit(solution)/shard_map/ppermute | solution.py:866
  158.2 7.6 %collective-permute-start.7 = (bf16[16,48,128]{2,1,0:T(8,128)(2,1)S(1)}, bf16[16,48,128]{2,1,0:T(8,128)(2,1)S(1)}, u32[]{:S(2)}, u32[]{:S(2)}) collective-permute-start(bf16[16,48,128]{2,1,0:T(8,128)(2,1)S(1)} %copy-done.4), channel_id=1, source_target_pairs={{1,0},{2,1},{3,2},{4,3},{5,4},{6,5},{7,6},{9,8},{10,9},{11,10},{12... | collective-permute-start | bytes 589832 | tf_op jit(solution)/shard_map/ppermute | solution.py:866
  165.8 10.6 %collective-permute-start.8 = (bf16[592,128]{1,0:T(8,128)(2,1)S(1)}, bf16[592,128]{1,0:T(8,128)(2,1)S(1)}, u32[]{:S(2)}, u32[]{:S(2)}) collective-permute-start(bf16[592,128]{1,0:T(8,128)(2,1)S(1)} %pad_maximum_fusion.6), channel_id=1, source_target_pairs={{0,4},{1,5},{2,6},{3,7},{4,0},{5,1},{6,2},{7,3},{8,12},{9,13},{10,... | collective-permute-start | bytes 454664 | tf_op jit(solution)/shard_map/ppermute | solution.py:875
  176.5 5.1 %collective-permute-start.9 = (bf16[544,128]{1,0:T(8,128)(2,1)S(1)}, bf16[544,128]{1,0:T(8,128)(2,1)S(1)}, u32[]{:S(2)}, u32[]{:S(2)}) collective-permute-start(bf16[544,128]{1,0:T(8,128)(2,1)S(1)} %fusion.1), channel_id=1, source_target_pairs={{0,16},{8,24},{16,0},{24,8},{1,17},{9,25},{17,1},{25,9},{2,18},{10... | collective-permute-start | bytes 417800 | tf_op jit(solution)/shard_map/ppermute | solution.py:875
  181.8 2.4 %collective-permute-start.10 = (bf16[1088,128]{1,0:T(8,128)(2,1)S(1)}, bf16[1088,128]{1,0:T(8,128)(2,1)S(1)}, u32[]{:S(2)}, u32[]{:S(2)}) collective-permute-start(bf16[1088,128]{1,0:T(8,128)(2,1)S(1)} %maximum_select_fusion.1), channel_id=1, source_target_pairs={{0,8},{8,0},{16,24},{24,16},{1,9},{9,1},{17,25},{25,17},{2,10},{10... | collective-permute-start | bytes 835592 | tf_op jit(solution)/shard_map/ppermute | solution.py:875

commit v4 on v3

--- a/solution.py
+++ b/solution.py
@@ -66,6 +66,13 @@
     while waiting or active:
         if waiting:
             active.append(waiting.pop(0))
+        active = [item for item in active if next(item, active) is None]
+        yield
+
+
+def beside(items):
+    active = list(items)
+    while active:
         active = [item for item in active if next(item, active) is None]
         yield
 
@@ -182,8 +189,8 @@
     xlo_ref,
     xhi_ref,
     g_ref,
-    bias_ref,
-    root_ref,
+    bias_hbm,
+    root_hbm,
     pair_ref,
     cond_ref,
     clo_ref,
@@ -192,10 +199,14 @@
     vec_ref,
     out_ref,
     grad_ref,
-    rlo_ref,
-    rhi_ref,
+    ride_ref,
+    away_ref,
+    send_ref,
+    keep_ref,
     packed_ref,
-    small_ref,
+    bias_ref,
+    root_ref,
+    table_sem,
     dbias_ref,
     dvec_ref,
     pair_scr,
@@ -267,6 +278,8 @@
     def joined(ref, st):
         return ref[st].astype(F32) + ref[structs + st].astype(F32)
 
+    bias_copy = pltpu.make_async_copy(bias_hbm, bias_ref, table_sem.at[0])
+    root_copy = pltpu.make_async_copy(root_hbm, root_ref, table_sem.at[1])
     chunk = min(8, windows)
     chunks = structs * windows // chunk
 
@@ -280,6 +293,8 @@
 
     @pl.when(step == 0)
     def _():
+        bias_copy.start()
+        root_copy.start()
         for at in range(min(SLOTS, chunks)):
             pair_copy(at).start()
 
@@ -327,6 +342,10 @@
             t_hs[st] = jax.nn.sigmoid(first[:, :C] + vec_ref[1:2])
             t_hh[st] = first[:, C:]
 
+    @pl.when(step == 0)
+    def _():
+        bias_copy.wait()
+
     def project(b, i):
         start = i * tile
         rows = pl.ds(start, tile)
@@ -518,8 +537,9 @@
         a_hs[s[b]] += dada * normed
         a_hh[s[b]] += dada
         rim = layer_back(normed, ih_scr[b], dada * t_hs[s[b]]).astype(BF16)
-        rlo_ref[b] = rim[:HALO]
-        rhi_ref[b] = rim[HALO:]
+        even = lax.axis_index("win") % 2 == 0
+        ride_ref[b] = jnp.where(even, rim[HALO:], rim[:HALO])
+        away_ref[b] = jnp.where(even, rim[:HALO], rim[HALO:])
 
     groups = [tuple(range(at, at + unroll)) for at in range(0, windows, unroll)]
 
@@ -585,6 +605,7 @@
         for _ in pipeline(items):
             pass
 
+        root_copy.wait()
         for at in range(chunks):
             pair_copy(at).wait()
             st, first = divmod(at * chunk, windows)
@@ -604,9 +625,14 @@
         acc = jnp.zeros((PAIR, C), F32)
         for q in range(QW):
             acc = acc + jnp.where(lanes == q, pair_total[q * PAIR : q * PAIR + PAIR], 0.0)
-        small_ref[8:] = acc - jnp.mean(acc, axis=0, keepdims=True)
-        small_ref[:8] = jnp.concatenate(
-            [rows_sum(dvec_ref[at]) for at in range(7)] + [jnp.zeros((1, C), F32)], axis=0
+        half = NBLK * C // 2
+        side = lax.axis_index("samp") % 2
+        send_ref[:half] = packed_ref[pl.ds(pl.multiple_of((1 - side) * half, 64), half)]
+        keep_ref[...] = packed_ref[pl.ds(pl.multiple_of(side * half, 64), half)]
+        send_ref[half:] = jnp.concatenate(
+            [rows_sum(dvec_ref[at]) for at in range(7)]
+            + [jnp.zeros((1, C), F32), acc - jnp.mean(acc, axis=0, keepdims=True)],
+            axis=0,
         )
 
 
@@ -641,8 +667,8 @@
                 per_sample(HALO, C),
                 per_sample(HALO, C),
                 per_sample(rows, C),
-                whole(structs, windows, KW, C),
-                whole(structs, windows, KW, C),
+                pl.BlockSpec(memory_space=pl.ANY),
+                pl.BlockSpec(memory_space=pl.ANY),
                 pl.BlockSpec(memory_space=pl.ANY),
                 whole(structs, rows, C),
                 cond_part,
@@ -655,10 +681,14 @@
                 per_sample(rows, C),
                 per_sample(HALO, C),
                 per_sample(HALO, C),
-                whole(NBLK * C, C),
-                whole(8 + PAIR, C),
+                whole(NBLK * C // 2 + 8 + PAIR, C),
+                whole(NBLK * C // 2, C),
             ],
             scratch_shapes=[
+                pltpu.VMEM((NBLK * C, C), F32),
+                pltpu.VMEM((structs, windows, KW, C), F32),
+                pltpu.VMEM((structs, windows, KW, C), BF16),
+                pltpu.SemaphoreType.DMA((2,)),
                 pltpu.VMEM((structs, windows, KW, C), F32),
                 pltpu.VMEM((7, 8, C), F32),
                 pltpu.VMEM((SLOTS, min(rows, 8 * QW), PAIR, KW), BF16),
@@ -716,8 +746,8 @@
             shape((samples, rows, C), BF16),
             shape((samples, HALO, C), BF16),
             shape((samples, HALO, C), BF16),
-            shape((NBLK * C, C), F32),
-            shape((8 + PAIR, C), F32),
+            shape((NBLK * C // 2 + 8 + PAIR, C), F32),
+            shape((NBLK * C // 2, C), F32),
         ],
         compiler_params=pltpu.CompilerParams(vmem_limit_bytes=VMEM_LIMIT),
         name="block",
@@ -744,7 +774,8 @@
 
 
 def update_kernel(
-    total_ref,
+    own_ref,
+    other_ref,
     small_ref,
     sl_ref,
     sr_ref,
@@ -773,7 +804,12 @@
     newv_ema_ref,
     newp_ema_ref,
     turned,
+    total_ref,
 ):
+    half = own_ref.shape[0]
+    side = lax.axis_index("samp") % 2
+    total_ref[pl.ds(pl.multiple_of(side * half, 64), half)] = own_ref[...].astype(F32)
+    total_ref[pl.ds(pl.multiple_of((1 - side) * half, 64), half)] = other_ref[...].astype(F32)
     count = sl_ref.shape[1]
     own = pl.ds(lax.axis_index("win") * count, count)
 
@@ -810,7 +846,7 @@
         low_ref[b] = new.astype(BF16)
         neww_ema_ref[b] = ema_decay * ew_ref[b] + (1.0 - ema_decay) * new
 
-    for _ in pipeline([one(b) for b in range(NBLK)]):
+    for _ in pipeline([beside([one(b) for b in range(at, min(at + 6, NBLK))]) for at in range(0, NBLK, 6)]):
         pass
     sums = small_ref[8:]
     pair_total = lax.dot_general(
@@ -833,9 +869,9 @@
 
 
 def update_call(*args):
-    rows = args[2].shape
-    vec = args[8].shape
-    pw = args[11].shape
+    rows = args[3].shape
+    vec = args[9].shape
+    pw = args[12].shape
     full = pl.BlockSpec(memory_space=pltpu.VMEM)
 
     def shape(dims, kind=F32):
@@ -854,7 +890,7 @@
         out_shape=[
             shape(dims, BF16 if at == 6 else F32) for at, dims in enumerate(outs)
         ],
-        scratch_shapes=[pltpu.VMEM((NBLK, C, C), F32)],
+        scratch_shapes=[pltpu.VMEM((NBLK, C, C), F32), pltpu.VMEM((NBLK * C, C), F32)],
         compiler_params=pltpu.CompilerParams(vmem_limit_bytes=VMEM_LIMIT),
         name="update",
     )(*args)
@@ -880,39 +916,48 @@
     return [(axis, 1 << at) for at in range((devices - 1).bit_length())]
 
 
-def summed(values, small, after):
-    halvings = bits("samp")
-    count = small.shape[0]
-
-    def exchange(part, axis, bit):
-        high = rounded(small)
-        rest = rounded(small - high)
-        message = [part.astype(BF16), high.astype(BF16), rest.astype(BF16)]
-        got = partner(jnp.concatenate(message, axis=0), axis, bit).astype(F32)
-        size = part.shape[0]
-        total = (high + rest) + (got[size : size + count] + got[size + count :])
-        return got[:size], total
-
-    for at, (axis, bit) in enumerate(halvings):
+def neighbours(values):
+    devices = lax.axis_size("win")
+    pairs = [(i, i + 1) for i in range(1, devices - 1, 2)]
+    return lax.ppermute(values, "win", pairs + [(j, i) for i, j in pairs])
+
+
+def exchange(part, small, axis, bit, extra=()):
+    count, size = small.shape[0], part.shape[0]
+    high = rounded(small)
+    rest = rounded(small - high)
+    message = [part.astype(BF16), high.astype(BF16), rest.astype(BF16), *extra]
+    got = partner(jnp.concatenate(message, axis=0), axis, bit)
+    theirs = got[size : size + 2 * count].astype(F32)
+    total = (high + rest) + (theirs[:count] + theirs[count:])
+    return got[:size].astype(F32), total, got[size + 2 * count :]
+
+
+def summed(send, keep, ride, away):
+    half = keep.shape[0]
+    arrived = neighbours(away)
+    first, *halvings = bits("samp")
+    got = partner(send, *first)
+    values = keep + got[:half]
+    small = send[half:] + got[half:]
+    for axis, bit in halvings:
         side = (lax.axis_index(axis) // bit) % 2
         half = values.shape[0] // 2
-        send = lax.dynamic_slice_in_dim(values, (1 - side) * half, half)
-        keep = lax.dynamic_slice_in_dim(values, side * half, half)
-        if at == 0:
-            got = partner(jnp.concatenate([send, small], axis=0), axis, bit)
-            small = small + got[half:]
-            values = keep + got[:half]
-        else:
-            got, small = exchange(send, axis, bit)
-            values = keep + got
+        kept = lax.dynamic_slice_in_dim(values, side * half, half)
+        got, small, _ = exchange(
+            lax.dynamic_slice_in_dim(values, (1 - side) * half, half), small, axis, bit
+        )
+        values = kept + got
+    values, arrived = lax.optimization_barrier((values, arrived))
     for at, (axis, bit) in enumerate(bits("win")):
         values = rounded(values)
-        got, small = exchange(values, axis, bit)
+        extra = [ride.reshape(-1, C)] if at == 0 else []
+        got, small, rest = exchange(values, small, axis, bit, extra)
         values = values + got
-        if at == 1:
-            values, after = lax.optimization_barrier((values, after))
+        if at == 0:
+            rode = rest.reshape(ride.shape)
     values = values.astype(BF16)
-    for at, (axis, bit) in enumerate(reversed(halvings)):
+    for axis, bit in reversed(halvings):
         side = (lax.axis_index(axis) // bit) % 2
         other = partner(values, axis, bit)
         values = jnp.where(
@@ -920,7 +965,7 @@
             jnp.concatenate([values, other]),
             jnp.concatenate([other, values]),
         )
-    return values.astype(F32), small, after
+    return values, first, small, rode, arrived
 
 
 def body(
@@ -952,18 +997,21 @@
     first, last = messages
     low_msg, high_msg = passed(last, 1), passed(first, -1)
     bias, root = bias_table(pair, pair_weight.T)
-    result, grad_atoms, rim_low, rim_high, packed, small = main_call(
+    result, grad_atoms, ride, away, send, keep = main_call(
         struct_ids, atoms, low_msg, high_msg, cotangent, bias, root, pair, cond, weights, vectors
     )
-    above = passed(rim_low, -1)
-    below = passed(rim_high, 1)
-    packed, small, (below, above) = summed(packed, small, (below, above))
+    own, last_step, small, rode, arrived = summed(send, keep, ride, away)
+    even = lax.axis_index("win") % 2 == 0
+    below = jnp.where(even, arrived, rode)
+    above = jnp.where(even, rode, arrived)
     for span, part in ((slice(0, HALO), below), (slice(rows - HALO, rows), above)):
         edge = grad_atoms[:, span].astype(F32) + part.astype(F32)
         grad_atoms = grad_atoms.at[:, span].set(edge.astype(BF16))
+    other = partner(own, *last_step)
     outs = list(
         update_call(
-            packed,
+            own,
+            other,
             small,
             stat_left,
             stat_right,

time: 192 us -> 188 us (0.979)
  Pallas kernels: 132 us -> 128 us
    ppermute x4 -> x2, waiting for transfers between devices: 6.14 us -> 0.01 us  [passed(): return lax.ppermute(shard, 'win', pairs)]
    ppermute x7, waiting for transfers between devices: 18.1 us -> 23.2 us  [partner(): return lax.ppermute(values, axis, [(i, i ^ bit) for i in range(devices)])]
    ppermute x4 -> x2, starting transfers between devices: 9.99 us -> 6.18 us  [passed(): return lax.ppermute(shard, 'win', pairs)]
    ppermute x7, starting transfers between devices: 13 us -> 16.3 us  [partner(): return lax.ppermute(values, axis, [(i, i ^ bit) for i in range(devices)])]
    pallas_call x1, Pallas kernels: 114 us -> 111 us  [main_call(): pl.pallas_call(main_kernel, grid_spec=pltpu.PrefetchScalarGridSpec(num_sc...]
  transfers between devices with their start and end apart: 11 -> 10, of which waited for: 7 -> 7; matrix products, arithmetic and copies ran while one was open for 2% -> 2% of each run, Pallas kernels for 7% -> 7%
where the time goes in v4:
time: 188 us; the launch traced here: 187 us
  Pallas kernels  128 us (68%)
  waiting for transfers between devices  23.3 us (12%)
  starting transfers between devices  23.2 us (12%)
  other arithmetic  8.87 us (5%)
  local copies, waits for them, and re-layouts  2.56 us (1%)
    pallas_call x1, Pallas kernels, main_call(): pl.pallas_call(main_kernel, grid_spec=pltpu.PrefetchScalarGridSpec(num_sc...  111 us
    ppermute x7, waiting for transfers between devices, partner(): return lax.ppermute(values, axis, [(i, i ^ bit) for i in range(devices)])  23.2 us
    ppermute x7, starting transfers between devices, partner(): return lax.ppermute(values, axis, [(i, i ^ bit) for i in range(devices)])  16.3 us
    pallas_call x1, Pallas kernels, bias_table(): pl.pallas_call(bias_kernel, grid=(structs, atoms // rows), in_specs=[pl.B...  13 us
    ppermute x2, starting transfers between devices, passed(): return lax.ppermute(shard, 'win', pairs)  6.18 us
    pallas_call x1, Pallas kernels, update_call(): pl.pallas_call(update_kernel, grid=(1,), in_specs=[full] * len(args), out...  4.08 us
  transfers between devices with their start and end apart: 10, of which 7 were waited for; matrix products, arithmetic and copies ran while one was open for 2% of the time, Pallas kernels for 7%

profile of v4, /device:TPU:0, one launch (start us, length us, event | category | flops | bytes accessed | tf_op | source)
XLA Modules:
  0.0 187.0 jit_solution(3901695432390610385)
XLA Ops:
  0.6 0.8 reduce-precision_convert_fusion.1
  1.5 1.1 fusion.21
  2.6 4.9 %collective-permute-start = (bf16[20,48,128]{2,1,0:T(8,128)(2,1)S(1)}, bf16[20,48,128]{2,1,0:T(8,128)(2,1)S(1)}, u32[]{:S(2)}, u32[]{:S(2)}) collective-permute-start(bf16[20,48,128]{2,1,0:T(8,128)(2,1)S(1)} %pad_maximum_fusion.1), channel_id=1, source_target_pairs={{0,1},{1,2},{2,3},{3,4},{4,5},{5,6},{6,7},{8,9},{9,10},{10,11},{11... | collective-permute-start | bytes 737288 | tf_op jit(solution)/shard_map/ppermute | solution.py:902
  7.5 1.3 collective-permute-start.1
  8.8 13.0 %pair_bias.1 = (f32[2,32,128,128]{3,2,1,0:T(8,128)}, bf16[2,32,128,128]{3,2,1,0:T(8,128)(2,1)}) custom-call(bf16[2,1024,16,128]{3,2,1,0:T(8,128)(2,1)} %pair_ref.3, f32[4,16]{1,0:T(4,128)} %bitcast.12), custom_call_target="tpu_custom_call" | custom-call | flops 1000000000 | bytes 15728640 | tf_op jit(solution)/shard_map/pair_bias/pallas_call | solution.py:164
  22.6 111.0 %block.1 = (bf16[16,1024,128]{2,1,0:T(8,128)(2,1)}, bf16[16,1024,128]{2,1,0:T(8,128)(2,1)}, bf16[16,48,128]{2,1,0:T(8,128)(2,1)}, bf16[16,48,128]{2,1,0:T(8,128)...) custom-call(s32[16]{0:T(128)} %ids_ref.1, bf16[16,1024,128]{2,1,0:T(8,128)(2,1)} %x_ref.1, ...), custom_call_target="tpu_custom_call" | custom-call | tf_op jit(solution)/shard_map/block/pallas_call | solution.py:660
  133.7 2.1 %collective-permute-done.2 = f32[1112,128]{1,0:T(8,128)S(1)} collective-permute-done((f32[1112,128]{1,0:T(8,128)}, f32[1112,128]{1,0:T(8,128)S(1)}, u32[]{:S(2)}, u32[]{:S(2)}) %collective-permute-start.2) | collective-permute-done | bytes 569376 | tf_op jit(solution)/shard_map/ppermute | solution.py:911
  135.9 1.1 slice_add_fusion
  137.0 0.7 reduce-precision_convert_fusion.6
  137.7 1.6 collective-permute-start.3
  140.0 3.8 %collective-permute-done.3 = bf16[592,128]{1,0:T(8,128)(2,1)S(1)} collective-permute-done((bf16[592,128]{1,0:T(8,128)(2,1)S(1)}, bf16[592,128]{1,0:T(8,128)(2,1)S(1)}, u32[]{:S(2)}, u32[]{:S(2)}) %collective-permute-start.3) | collective-permute-done | bytes 151584 | tf_op jit(solution)/shard_map/ppermute | solution.py:911
  143.8 0.7 reduce-precision_convert_fusion.5
  144.6 1.0 pad_maximum_fusion
  145.6 7.8 %collective-permute-start.5 = (bf16[1360,128]{1,0:T(8,128)(2,1)S(1)}, bf16[1360,128]{1,0:T(8,128)(2,1)S(1)}, u32[]{:S(2)}, u32[]{:S(2)}) collective-permute-start(bf16[1360,128]{1,0:T(8,128)(2,1)S(1)} %pad_maximum_fusion), channel_id=1, source_target_pairs={{0,1},{1,0},{2,3},{3,2},{4,5},{5,4},{6,7},{7,6},{8,9},{9,8},{10,11... | collective-permute-start | bytes 1044488 | tf_op jit(solution)/shard_map/ppermute | solution.py:911
  153.4 7.3 %collective-permute-done.5 = bf16[1360,128]{1,0:T(8,128)(2,1)S(1)} collective-permute-done((bf16[1360,128]{1,0:T(8,128)(2,1)S(1)}, bf16[1360,128]{1,0:T(8,128)(2,1)S(1)}, u32[]{:S(2)}, u32[]{:S(2)}) %collective-permute-start.5) | collective-permute-done | bytes 348192 | tf_op jit(solution)/shard_map/ppermute | solution.py:911
  160.8 2.7 %collective-permute-start.6 = (bf16[592,128]{1,0:T(8,128)(2,1)S(1)}, bf16[592,128]{1,0:T(8,128)(2,1)S(1)}, u32[]{:S(2)}, u32[]{:S(2)}) collective-permute-start(bf16[592,128]{1,0:T(8,128)(2,1)S(1)} %pad_maximum_fusion.4), channel_id=1, source_target_pairs={{0,2},{1,3},{2,0},{3,1},{4,6},{5,7},{6,4},{7,5},{8,10},{9,11},{10,... | collective-permute-start | bytes 454664 | tf_op jit(solution)/shard_map/ppermute | solution.py:911
  163.5 3.1 %collective-permute-done.6 = bf16[592,128]{1,0:T(8,128)(2,1)S(1)} collective-permute-done((bf16[592,128]{1,0:T(8,128)(2,1)S(1)}, bf16[592,128]{1,0:T(8,128)(2,1)S(1)}, u32[]{:S(2)}, u32[]{:S(2)}) %collective-permute-start.6) | collective-permute-done | bytes 151584 | tf_op jit(solution)/shard_map/ppermute | solution.py:911
  166.8 3.5 %collective-permute-start.7 = (bf16[592,128]{1,0:T(8,128)(2,1)S(1)}, bf16[592,128]{1,0:T(8,128)(2,1)S(1)}, u32[]{:S(2)}, u32[]{:S(2)}) collective-permute-start(bf16[592,128]{1,0:T(8,128)(2,1)S(1)} %pad_maximum_fusion.5), channel_id=1, source_target_pairs={{0,4},{1,5},{2,6},{3,7},{4,0},{5,1},{6,2},{7,3},{8,12},{9,13},{10,... | collective-permute-start | bytes 454664 | tf_op jit(solution)/shard_map/ppermute | solution.py:911
  170.3 1.7 fusion
  172.0 3.1 %collective-permute-done.7 = bf16[592,128]{1,0:T(8,128)(2,1)S(1)} collective-permute-done((bf16[592,128]{1,0:T(8,128)(2,1)S(1)}, bf16[592,128]{1,0:T(8,128)(2,1)S(1)}, u32[]{:S(2)}, u32[]{:S(2)}) %collective-permute-start.7) | collective-permute-done | bytes 151584 | tf_op jit(solution)/shard_map/ppermute | solution.py:911
  175.8 1.7 fusion.1
  177.5 2.8 %collective-permute-done.8 = bf16[544,128]{1,0:T(8,128)(2,1)S(1)} collective-permute-done((bf16[544,128]{1,0:T(8,128)(2,1)S(1)}, bf16[544,128]{1,0:T(8,128)(2,1)S(1)}, u32[]{:S(2)}, u32[]{:S(2)}) %collective-permute-start.8) | collective-permute-done | bytes 139296 | tf_op jit(solution)/shard_map/ppermute | solution.py:911
  181.1 0.9 collective-permute-done.9.other_ref
  182.7 4.1 %update.1 = (f32[17,16,128]{2,1,0:T(8,128)}, f32[7,128]{1,0:T(8,128)}, f32[4,16]{1,0:T(4,128)}, f32[17,16,128]{2,1,0:T(8,128)}, f32[17,16,128]{2,1,0:T(8,128)}, ...) custom-call(bf16[1088,128]{1,0:T(8,128)(2,1)} %copy-done, ...), custom_call_target="tpu_custom_call" | custom-call | tf_op jit(solution)/shard_map/update/pallas_call | solution.py:885
  (38 shorter events, 4.1 us)
Async XLA Ops:
  2.6 19.2 %collective-permute-start = (bf16[20,48,128]{2,1,0:T(8,128)(2,1)S(1)}, bf16[20,48,128]{2,1,0:T(8,128)(2,1)S(1)}, u32[]{:S(2)}, u32[]{:S(2)}) collective-permute-start(bf16[20,48,128]{2,1,0:T(8,128)(2,1)S(1)} %pad_maximum_fusion.1), channel_id=1, source_target_pairs={{0,1},{1,2},{2,3},{3,4},{4,5},{5,6},{6,7},{8,9},{9,10},{10,11},{11... | collective-permute-start | bytes 737288 | tf_op jit(solution)/shard_map/ppermute | solution.py:902
  7.5 14.3 %collective-permute-start.1 = (bf16[20,48,128]{2,1,0:T(8,128)(2,1)S(1)}, bf16[20,48,128]{2,1,0:T(8,128)(2,1)S(1)}, u32[]{:S(2)}, u32[]{:S(2)}) collective-permute-start(bf16[20,48,128]{2,1,0:T(8,128)(2,1)S(1)} %pad_maximum_fusion.2), channel_id=1, source_target_pairs={{1,0},{2,1},{3,2},{4,3},{5,4},{6,5},{7,6},{9,8},{10,9},{11,10},{12... | collective-permute-start | bytes 737288 | tf_op jit(solution)/shard_map/ppermute | solution.py:902
  21.8 0.7 copy-start.1
  21.8 0.8 copy-start.2
  133.6 2.3 %collective-permute-start.2 = (f32[1112,128]{1,0:T(8,128)}, f32[1112,128]{1,0:T(8,128)S(1)}, u32[]{:S(2)}, u32[]{:S(2)}) collective-permute-start(f32[1112,128]{1,0:T(8,128)} %get-tuple-element.69), channel_id=1, source_target_pairs={{0,8},{8,0},{16,24},{24,16},{1,9},{9,1},{17,25},{25,17},{2,10},{10... | collective-permute-start | bytes 1708040 | tf_op jit(solution)/shard_map/ppermute | solution.py:911
  137.7 6.0 %collective-permute-start.3 = (bf16[592,128]{1,0:T(8,128)(2,1)S(1)}, bf16[592,128]{1,0:T(8,128)(2,1)S(1)}, u32[]{:S(2)}, u32[]{:S(2)}) collective-permute-start(bf16[592,128]{1,0:T(8,128)(2,1)S(1)} %pad_maximum_fusion.3), channel_id=1, source_target_pairs={{0,16},{8,24},{16,0},{24,8},{1,17},{9,25},{17,1},{25,9},{2,18},{10... | collective-permute-start | bytes 454664 | tf_op jit(solution)/shard_map/ppermute | solution.py:911
  139.3 4.5 %collective-permute-start.4 = (bf16[16,48,128]{2,1,0:T(8,128)(2,1)}, bf16[16,48,128]{2,1,0:T(8,128)(2,1)S(1)}, u32[]{:S(2)}, u32[]{:S(2)}) collective-permute-start(bf16[16,48,128]{2,1,0:T(8,128)(2,1)} %get-tuple-element.70), channel_id=1, source_target_pairs={{1,2},{3,4},{5,6},{2,1},{4,3},{6,5},{9,10},{11,12},{13,14},{10,9},... | collective-permute-start | bytes 589832 | tf_op jit(solution)/shard_map/ppermute | solution.py:922
  145.6 15.1 %collective-permute-start.5 = (bf16[1360,128]{1,0:T(8,128)(2,1)S(1)}, bf16[1360,128]{1,0:T(8,128)(2,1)S(1)}, u32[]{:S(2)}, u32[]{:S(2)}) collective-permute-start(bf16[1360,128]{1,0:T(8,128)(2,1)S(1)} %pad_maximum_fusion), channel_id=1, source_target_pairs={{0,1},{1,0},{2,3},{3,2},{4,5},{5,4},{6,7},{7,6},{8,9},{9,8},{10,11... | collective-permute-start | bytes 1044488 | tf_op jit(solution)/shard_map/ppermute | solution.py:911
  160.8 5.9 %collective-permute-start.6 = (bf16[592,128]{1,0:T(8,128)(2,1)S(1)}, bf16[592,128]{1,0:T(8,128)(2,1)S(1)}, u32[]{:S(2)}, u32[]{:S(2)}) collective-permute-start(bf16[592,128]{1,0:T(8,128)(2,1)S(1)} %pad_maximum_fusion.4), channel_id=1, source_target_pairs={{0,2},{1,3},{2,0},{3,1},{4,6},{5,7},{6,4},{7,5},{8,10},{9,11},{10,... | collective-permute-start | bytes 454664 | tf_op jit(solution)/shard_map/ppermute | solution.py:911
  166.8 8.2 %collective-permute-start.7 = (bf16[592,128]{1,0:T(8,128)(2,1)S(1)}, bf16[592,128]{1,0:T(8,128)(2,1)S(1)}, u32[]{:S(2)}, u32[]{:S(2)}) collective-permute-start(bf16[592,128]{1,0:T(8,128)(2,1)S(1)} %pad_maximum_fusion.5), channel_id=1, source_target_pairs={{0,4},{1,5},{2,6},{3,7},{4,0},{5,1},{6,2},{7,3},{8,12},{9,13},{10,... | collective-permute-start | bytes 454664 | tf_op jit(solution)/shard_map/ppermute | solution.py:911
  175.2 5.1 %collective-permute-start.8 = (bf16[544,128]{1,0:T(8,128)(2,1)S(1)}, bf16[544,128]{1,0:T(8,128)(2,1)S(1)}, u32[]{:S(2)}, u32[]{:S(2)}) collective-permute-start(bf16[544,128]{1,0:T(8,128)(2,1)S(1)} %add_convert_fusion.2), channel_id=1, source_target_pairs={{0,16},{8,24},{16,0},{24,8},{1,17},{9,25},{17,1},{25,9},{2,18},{10... | collective-permute-start | bytes 417800 | tf_op jit(solution)/shard_map/ppermute | solution.py:911
  180.4 1.6 copy-start
  180.4 1.6 collective-permute-start.9
  182.0 0.7 copy-start.3

commit v5 on v4

--- a/solution.py
+++ b/solution.py
@@ -199,8 +199,8 @@
     vec_ref,
     out_ref,
     grad_ref,
-    ride_ref,
-    away_ref,
+    rlo_ref,
+    rhi_ref,
     send_ref,
     keep_ref,
     packed_ref,
@@ -321,26 +321,34 @@
             acc[...] = jnp.zeros_like(acc)
         dbias_ref[...] = jnp.zeros_like(dbias_ref)
         pair_total[...] = jnp.zeros_like(pair_total)
-        for st in range(structs):
-
-            def table(i, carry):
-                rows = pl.ds(pl.multiple_of(i * tile, tile), tile)
-                _, one, two = cond_rows(cond_ref[st, rows])
-                first = dot(one, wc1[...])
-                t_s1[st, rows] = jax.nn.sigmoid(first[:, :C] + vec_ref[1:2])
-                t_h1[st, rows] = first[:, C : 2 * C]
-                t_g1[st, rows] = jax.nn.sigmoid(first[:, 2 * C :] + vec_ref[3:4])
-                second = dot(two, wc2[...])
-                t_s2[st, rows] = jax.nn.sigmoid(second[:, :C] + vec_ref[5:6])
-                t_h2[st, rows] = second[:, C : 2 * C]
-                t_g2[st, rows] = jax.nn.sigmoid(second[:, 2 * C :] + vec_ref[6:7])
-                return carry
-
-            lax.fori_loop(0, tiles, table, 0)
-            _, one, _ = cond_rows(jnp.concatenate([joined(clo_ref, st), joined(chi_ref, st)], axis=0))
+
+        def table(st, i):
+            rows = pl.ds(i * tile, tile)
+            _, one, two = cond_rows(cond_ref[st, rows])
+            yield
+            first = dot(one, wc1[...])
+            second = dot(two, wc2[...])
+            yield
+            t_s1[st, rows] = jax.nn.sigmoid(first[:, :C] + vec_ref[1:2])
+            t_h1[st, rows] = first[:, C : 2 * C]
+            t_g1[st, rows] = jax.nn.sigmoid(first[:, 2 * C :] + vec_ref[3:4])
+            t_s2[st, rows] = jax.nn.sigmoid(second[:, :C] + vec_ref[5:6])
+            t_h2[st, rows] = second[:, C : 2 * C]
+            t_g2[st, rows] = jax.nn.sigmoid(second[:, 2 * C :] + vec_ref[6:7])
+
+        def table_halo(st):
+            source = jnp.concatenate([joined(clo_ref, st), joined(chi_ref, st)], axis=0)
+            _, one, _ = cond_rows(source)
+            yield
             first = dot(one, wc1[:, : 2 * C])
+            yield
             t_hs[st] = jax.nn.sigmoid(first[:, :C] + vec_ref[1:2])
             t_hh[st] = first[:, C:]
+
+        items = [table_halo(st) for st in range(structs)]
+        items += [table(st, i) for st in range(structs) for i in range(tiles)]
+        for _ in pipeline(items):
+            pass
 
     @pl.when(step == 0)
     def _():
@@ -467,8 +475,6 @@
             block(11 + at)[...] += dwin[:, at * C : at * C + C]
         block(6)[...] += dw6
 
-    dk_scr[...] = jnp.zeros_like(dk_scr)
-    dv_scr[...] = jnp.zeros_like(dv_scr)
     ones = jnp.ones((KW, C), BF16)
 
     def attend_back(b, group):
@@ -499,8 +505,11 @@
             dq = gathered(fulls[u]) * FACTOR
             dvec_ref[2] += jnp.sum(dq.reshape(QW // 8, 8, C), axis=0)
             d4_scr[b, w * QW : w * QW + QW, :C] = dq.astype(BF16)
-            dk_scr[b, w * QW : w * QW + KW] += dks[u]
-            dv_scr[b, w * QW : w * QW + KW] += dvs[u]
+            seen = KW - QW if w else 0
+            for scr, part in ((dk_scr, dks[u]), (dv_scr, dvs[u])):
+                if seen:
+                    scr[b, w * QW : w * QW + seen] += part[:seen]
+                scr[b, w * QW + seen : w * QW + KW] = part[seen:]
 
     def finish(b, i):
         start = i * tile
@@ -537,9 +546,8 @@
         a_hs[s[b]] += dada * normed
         a_hh[s[b]] += dada
         rim = layer_back(normed, ih_scr[b], dada * t_hs[s[b]]).astype(BF16)
-        even = lax.axis_index("win") % 2 == 0
-        ride_ref[b] = jnp.where(even, rim[HALO:], rim[:HALO])
-        away_ref[b] = jnp.where(even, rim[:HALO], rim[HALO:])
+        rlo_ref[b] = rim[:HALO]
+        rhi_ref[b] = rim[HALO:]
 
     groups = [tuple(range(at, at + unroll)) for at in range(0, windows, unroll)]
 
@@ -626,14 +634,17 @@
         for q in range(QW):
             acc = acc + jnp.where(lanes == q, pair_total[q * PAIR : q * PAIR + PAIR], 0.0)
         half = NBLK * C // 2
-        side = lax.axis_index("samp") % 2
-        send_ref[:half] = packed_ref[pl.ds(pl.multiple_of((1 - side) * half, 64), half)]
+        side = (lax.axis_index("samp") // 2) % 2
+        send = packed_ref[pl.ds(pl.multiple_of((1 - side) * half, 64), half)]
         keep_ref[...] = packed_ref[pl.ds(pl.multiple_of(side * half, 64), half)]
-        send_ref[half:] = jnp.concatenate(
+        small = jnp.concatenate(
             [rows_sum(dvec_ref[at]) for at in range(7)]
             + [jnp.zeros((1, C), F32), acc - jnp.mean(acc, axis=0, keepdims=True)],
             axis=0,
         )
+        high, low = split_low(small)
+        send_ref[:half] = send.astype(BF16)
+        send_ref[half:] = jnp.concatenate([high, low], axis=0)
 
 
 def main_call(
@@ -681,7 +692,7 @@
                 per_sample(rows, C),
                 per_sample(HALO, C),
                 per_sample(HALO, C),
-                whole(NBLK * C // 2 + 8 + PAIR, C),
+                whole(NBLK * C // 2 + 2 * (8 + PAIR), C),
                 whole(NBLK * C // 2, C),
             ],
             scratch_shapes=[
@@ -746,7 +757,7 @@
             shape((samples, rows, C), BF16),
             shape((samples, HALO, C), BF16),
             shape((samples, HALO, C), BF16),
-            shape((NBLK * C // 2 + 8 + PAIR, C), F32),
+            shape((NBLK * C // 2 + 2 * (8 + PAIR), C), BF16),
             shape((NBLK * C // 2, C), F32),
         ],
         compiler_params=pltpu.CompilerParams(vmem_limit_bytes=VMEM_LIMIT),
@@ -806,10 +817,12 @@
     turned,
     total_ref,
 ):
-    half = own_ref.shape[0]
+    chunks, size, _ = own_ref.shape
     side = lax.axis_index("samp") % 2
-    total_ref[pl.ds(pl.multiple_of(side * half, 64), half)] = own_ref[...].astype(F32)
-    total_ref[pl.ds(pl.multiple_of((1 - side) * half, 64), half)] = other_ref[...].astype(F32)
+    for at in range(chunks):
+        for ref, place in ((own_ref, side), (other_ref, 1 - side)):
+            start = pl.multiple_of((2 * at + place) * size, 16)
+            total_ref[pl.ds(start, size)] = ref[at].astype(F32)
     count = sl_ref.shape[1]
     own = pl.ds(lax.axis_index("win") * count, count)
 
@@ -916,47 +929,49 @@
     return [(axis, 1 << at) for at in range((devices - 1).bit_length())]
 
 
-def neighbours(values):
-    devices = lax.axis_size("win")
-    pairs = [(i, i + 1) for i in range(1, devices - 1, 2)]
-    return lax.ppermute(values, "win", pairs + [(j, i) for i, j in pairs])
-
-
-def exchange(part, small, axis, bit, extra=()):
-    count, size = small.shape[0], part.shape[0]
+def exchange(part, small, axis, bit):
+    size = part.shape[0]
     high = rounded(small)
     rest = rounded(small - high)
-    message = [part.astype(BF16), high.astype(BF16), rest.astype(BF16), *extra]
+    message = [part.astype(BF16), high.astype(BF16), rest.astype(BF16)]
     got = partner(jnp.concatenate(message, axis=0), axis, bit)
-    theirs = got[size : size + 2 * count].astype(F32)
-    total = (high + rest) + (theirs[:count] + theirs[count:])
-    return got[:size].astype(F32), total, got[size + 2 * count :]
-
-
-def summed(send, keep, ride, away):
-    half = keep.shape[0]
-    arrived = neighbours(away)
-    first, *halvings = bits("samp")
-    got = partner(send, *first)
-    values = keep + got[:half]
-    small = send[half:] + got[half:]
-    for axis, bit in halvings:
-        side = (lax.axis_index(axis) // bit) % 2
-        half = values.shape[0] // 2
-        kept = lax.dynamic_slice_in_dim(values, side * half, half)
-        got, small, _ = exchange(
-            lax.dynamic_slice_in_dim(values, (1 - side) * half, half), small, axis, bit
-        )
-        values = kept + got
-    values, arrived = lax.optimization_barrier((values, arrived))
-    for at, (axis, bit) in enumerate(bits("win")):
+    return got[:size].astype(F32), joined_terms(got[size:]) + (high + rest)
+
+
+def joined_terms(terms):
+    count = terms.shape[0] // 2
+    wide = terms.astype(F32)
+    return wide[:count] + wide[count:]
+
+
+def summed(send, keep, edges):
+    last, *halvings = bits("samp")
+    size = keep.shape[0]
+    for at, (axis, bit) in enumerate(halvings):
+        if at == 0:
+            got, edges = lax.optimization_barrier((partner(send, axis, bit), edges))
+            values = keep + got[:size].astype(F32)
+            small = joined_terms(send[size:]) + joined_terms(got[size:])
+        else:
+            side = (lax.axis_index(axis) // bit) % 2
+            size = values.shape[0] // 2
+            kept = lax.dynamic_slice_in_dim(values, side * size, size)
+            part = lax.dynamic_slice_in_dim(values, (1 - side) * size, size)
+            got, small = exchange(part, small, axis, bit)
+            values = kept + got
+    axis, bit = last
+    side = (lax.axis_index(axis) // bit) % 2
+    size = values.shape[0] // 2
+    kept = lax.dynamic_slice_in_dim(values, side * size, size)
+    part = lax.dynamic_slice_in_dim(values, (1 - side) * size, size)
+    got = partner(jnp.concatenate([part, small], axis=0), axis, bit)
+    values = kept + got[:size]
+    small = small + got[size:]
+    for axis, bit in bits("win"):
         values = rounded(values)
-        extra = [ride.reshape(-1, C)] if at == 0 else []
-        got, small, rest = exchange(values, small, axis, bit, extra)
+        got, small = exchange(values, small, axis, bit)
         values = values + got
-        if at == 0:
-            rode = rest.reshape(ride.shape)
-    values = values.astype(BF16)
+    values = values.astype(BF16)[None]
     for axis, bit in reversed(halvings):
         side = (lax.axis_index(axis) // bit) % 2
         other = partner(values, axis, bit)
@@ -965,7 +980,7 @@
             jnp.concatenate([values, other]),
             jnp.concatenate([other, values]),
         )
-    return values, first, small, rode, arrived
+    return values, partner(values, *last), small, edges
 
 
 def body(
@@ -997,17 +1012,14 @@
     first, last = messages
     low_msg, high_msg = passed(last, 1), passed(first, -1)
     bias, root = bias_table(pair, pair_weight.T)
-    result, grad_atoms, ride, away, send, keep = main_call(
+    result, grad_atoms, rim_low, rim_high, send, keep = main_call(
         struct_ids, atoms, low_msg, high_msg, cotangent, bias, root, pair, cond, weights, vectors
     )
-    own, last_step, small, rode, arrived = summed(send, keep, ride, away)
-    even = lax.axis_index("win") % 2 == 0
-    below = jnp.where(even, arrived, rode)
-    above = jnp.where(even, rode, arrived)
+    edges = (passed(rim_high, 1), passed(rim_low, -1))
+    own, other, small, (below, above) = summed(send, keep, edges)
     for span, part in ((slice(0, HALO), below), (slice(rows - HALO, rows), above)):
         edge = grad_atoms[:, span].astype(F32) + part.astype(F32)
         grad_atoms = grad_atoms.at[:, span].set(edge.astype(BF16))
-    other = partner(own, *last_step)
     outs = list(
         update_call(
             own,

time: 188 us -> 185 us (0.984)
    ppermute x2 -> x4, waiting for transfers between devices: 0.01 us -> 6.28 us  [passed(): return lax.ppermute(shard, 'win', pairs)]
    ppermute x7, waiting for transfers between devices: 23.2 us -> 17.2 us  [partner(): return lax.ppermute(values, axis, [(i, i ^ bit) for i in range(devices)])]
    ppermute x2 -> x4, starting transfers between devices: 6.18 us -> 12 us  [passed(): return lax.ppermute(shard, 'win', pairs)]
    ppermute x7, starting transfers between devices: 16.3 us -> 10.8 us  [partner(): return lax.ppermute(values, axis, [(i, i ^ bit) for i in range(devices)])]
  transfers between devices with their start and end apart: 10 -> 11, of which waited for: 7 -> 8; matrix products, arithmetic and copies ran while one was open for 2% -> 3% of each run, Pallas kernels for 7% -> 7%
where the time goes in v5:
time: 185 us; the launch traced here: 184 us
  Pallas kernels  127 us (69%)
  waiting for transfers between devices  23.5 us (13%)
  starting transfers between devices  22.8 us (12%)
  other arithmetic  7.04 us (4%)
  local copies, waits for them, and re-layouts  2.55 us (1%)
    pallas_call x1, Pallas kernels, main_call(): pl.pallas_call(main_kernel, grid_spec=pltpu.PrefetchScalarGridSpec(num_sc...  110 us
    ppermute x7, waiting for transfers between devices, partner(): return lax.ppermute(values, axis, [(i, i ^ bit) for i in range(devices)])  17.2 us
    pallas_call x1, Pallas kernels, bias_table(): pl.pallas_call(bias_kernel, grid=(structs, atoms // rows), in_specs=[pl.B...  13 us
    ppermute x4, starting transfers between devices, passed(): return lax.ppermute(shard, 'win', pairs)  12 us
    ppermute x7, starting transfers between devices, partner(): return lax.ppermute(values, axis, [(i, i ^ bit) for i in range(devices)])  10.8 us
    ppermute x4, waiting for transfers between devices, passed(): return lax.ppermute(shard, 'win', pairs)  6.28 us
    pallas_call x1, Pallas kernels, update_call(): pl.pallas_call(update_kernel, grid=(1,), in_specs=[full] * len(args), out...  4.09 us
  transfers between devices with their start and end apart: 11, of which 8 were waited for; matrix products, arithmetic and copies ran while one was open for 3% of the time, Pallas kernels for 7%

profile of v5, /device:TPU:0, one launch (start us, length us, event | category | flops | bytes accessed | tf_op | source)
XLA Modules:
  0.0 183.8 jit_solution(9653805787386602999)
XLA Ops:
  0.6 0.8 reduce-precision_convert_fusion
  1.5 1.1 fusion.22
  2.6 4.9 %collective-permute-start = (bf16[20,48,128]{2,1,0:T(8,128)(2,1)S(1)}, bf16[20,48,128]{2,1,0:T(8,128)(2,1)S(1)}, u32[]{:S(2)}, u32[]{:S(2)}) collective-permute-start(bf16[20,48,128]{2,1,0:T(8,128)(2,1)S(1)} %pad_maximum_fusion.1), channel_id=1, source_target_pairs={{0,1},{1,2},{2,3},{3,4},{4,5},{5,6},{6,7},{8,9},{9,10},{10,11},{11... | collective-permute-start | bytes 737288 | tf_op jit(solution)/shard_map/ppermute | solution.py:915
  7.5 1.3 collective-permute-start.1
  8.8 13.0 %pair_bias.1 = (f32[2,32,128,128]{3,2,1,0:T(8,128)}, bf16[2,32,128,128]{3,2,1,0:T(8,128)(2,1)}) custom-call(bf16[2,1024,16,128]{3,2,1,0:T(8,128)(2,1)} %pair_ref.3, f32[4,16]{1,0:T(4,128)} %bitcast.9), custom_call_target="tpu_custom_call" | custom-call | flops 1000000000 | bytes 15728640 | tf_op jit(solution)/shard_map/pair_bias/pallas_call | solution.py:164
  22.6 109.8 %block.1 = (bf16[16,1024,128]{2,1,0:T(8,128)(2,1)}, bf16[16,1024,128]{2,1,0:T(8,128)(2,1)}, bf16[16,48,128]{2,1,0:T(8,128)(2,1)}, bf16[16,48,128]{2,1,0:T(8,128)...) custom-call(s32[16]{0:T(128)} %ids_ref.1, bf16[16,1024,128]{2,1,0:T(8,128)(2,1)} %x_ref.1, ...), custom_call_target="tpu_custom_call" | custom-call | tf_op jit(solution)/shard_map/block/pallas_call | solution.py:671
  132.4 1.6 collective-permute-start.2
  134.0 4.5 %collective-permute-start.3 = (bf16[16,48,128]{2,1,0:T(8,128)(2,1)}, bf16[16,48,128]{2,1,0:T(8,128)(2,1)S(1)}, u32[]{:S(2)}, u32[]{:S(2)}) collective-permute-start(bf16[16,48,128]{2,1,0:T(8,128)(2,1)} %get-tuple-element.70), channel_id=1, source_target_pairs={{0,1},{1,2},{2,3},{3,4},{4,5},{5,6},{6,7},{8,9},{9,10},{10,11},{11... | collective-permute-start | bytes 589832 | tf_op jit(solution)/shard_map/ppermute | solution.py:915
  138.5 1.3 collective-permute-start.4
  140.6 1.6 collective-permute-done.3
  142.1 4.7 %collective-permute-done.4 = bf16[16,48,128]{2,1,0:T(8,128)(2,1)S(1)} collective-permute-done((bf16[16,48,128]{2,1,0:T(8,128)(2,1)}, bf16[16,48,128]{2,1,0:T(8,128)(2,1)S(1)}, u32[]{:S(2)}, u32[]{:S(2)}) %collective-permute-start.4) | collective-permute-done | bytes 196640 | tf_op jit(solution)/shard_map/ppermute | solution.py:915
  146.8 1.1 convert_add_fusion
  148.1 1.6 collective-permute-done.5
  149.7 2.8 %collective-permute-start.6 = (bf16[592,128]{1,0:T(8,128)(2,1)S(1)}, bf16[592,128]{1,0:T(8,128)(2,1)S(1)}, u32[]{:S(2)}, u32[]{:S(2)}) collective-permute-start(bf16[592,128]{1,0:T(8,128)(2,1)S(1)} %pad_maximum_fusion.3), channel_id=1, source_target_pairs={{0,1},{1,0},{2,3},{3,2},{4,5},{5,4},{6,7},{7,6},{8,9},{9,8},{10,11... | collective-permute-start | bytes 454664 | tf_op jit(solution)/shard_map/ppermute | solution.py:924
  152.6 4.2 %collective-permute-done.6 = bf16[592,128]{1,0:T(8,128)(2,1)S(1)} collective-permute-done((bf16[592,128]{1,0:T(8,128)(2,1)S(1)}, bf16[592,128]{1,0:T(8,128)(2,1)S(1)}, u32[]{:S(2)}, u32[]{:S(2)}) %collective-permute-start.6) | collective-permute-done | bytes 151584 | tf_op jit(solution)/shard_map/ppermute | solution.py:924
  156.9 2.8 %collective-permute-start.7 = (bf16[592,128]{1,0:T(8,128)(2,1)S(1)}, bf16[592,128]{1,0:T(8,128)(2,1)S(1)}, u32[]{:S(2)}, u32[]{:S(2)}) collective-permute-start(bf16[592,128]{1,0:T(8,128)(2,1)S(1)} %pad_maximum_fusion.4), channel_id=1, source_target_pairs={{0,2},{1,3},{2,0},{3,1},{4,6},{5,7},{6,4},{7,5},{8,10},{9,11},{10,... | collective-permute-start | bytes 454664 | tf_op jit(solution)/shard_map/ppermute | solution.py:924
  159.7 3.4 %collective-permute-done.7 = bf16[592,128]{1,0:T(8,128)(2,1)S(1)} collective-permute-done((bf16[592,128]{1,0:T(8,128)(2,1)S(1)}, bf16[592,128]{1,0:T(8,128)(2,1)S(1)}, u32[]{:S(2)}, u32[]{:S(2)}) %collective-permute-start.7) | collective-permute-done | bytes 151584 | tf_op jit(solution)/shard_map/ppermute | solution.py:924
  163.2 2.9 %collective-permute-start.8 = (bf16[592,128]{1,0:T(8,128)(2,1)S(1)}, bf16[592,128]{1,0:T(8,128)(2,1)S(1)}, u32[]{:S(2)}, u32[]{:S(2)}) collective-permute-start(bf16[592,128]{1,0:T(8,128)(2,1)S(1)} %pad_maximum_fusion.5), channel_id=1, source_target_pairs={{0,4},{1,5},{2,6},{3,7},{4,0},{5,1},{6,2},{7,3},{8,12},{9,13},{10,... | collective-permute-start | bytes 454664 | tf_op jit(solution)/shard_map/ppermute | solution.py:924
  166.1 1.7 fusion.1
  167.7 4.2 %collective-permute-done.8 = bf16[592,128]{1,0:T(8,128)(2,1)S(1)} collective-permute-done((bf16[592,128]{1,0:T(8,128)(2,1)S(1)}, bf16[592,128]{1,0:T(8,128)(2,1)S(1)}, u32[]{:S(2)}, u32[]{:S(2)}) %collective-permute-start.8) | collective-permute-done | bytes 151584 | tf_op jit(solution)/shard_map/ppermute | solution.py:924
  172.6 1.7 fusion.2
  174.3 2.9 %collective-permute-done.9 = bf16[1,544,128]{2,1,0:T(8,128)(2,1)S(1)} collective-permute-done((bf16[1,544,128]{2,1,0:T(8,128)(2,1)S(1)}, bf16[1,544,128]{2,1,0:T(8,128)(2,1)S(1)}, u32[]{:S(2)}, u32[]{:S(2)}) %collective-permute-start.9) | collective-permute-done | bytes 139296 | tf_op jit(solution)/shard_map/ppermute | solution.py:924
  177.9 0.9 collective-permute-done.10.other_ref
  179.5 4.1 %update.1 = (f32[17,16,128]{2,1,0:T(8,128)}, f32[7,128]{1,0:T(8,128)}, f32[4,16]{1,0:T(4,128)}, f32[17,16,128]{2,1,0:T(8,128)}, f32[17,16,128]{2,1,0:T(8,128)}, ...) custom-call(bf16[2,544,128]{2,1,0:T(8,128)(2,1)} %copy-done, ...), custom_call_target="tpu_custom_call" | custom-call | tf_op jit(solution)/shard_map/update/pallas_call | solution.py:898
  (38 shorter events, 4.0 us)
Async XLA Ops:
  2.6 19.2 %collective-permute-start = (bf16[20,48,128]{2,1,0:T(8,128)(2,1)S(1)}, bf16[20,48,128]{2,1,0:T(8,128)(2,1)S(1)}, u32[]{:S(2)}, u32[]{:S(2)}) collective-permute-start(bf16[20,48,128]{2,1,0:T(8,128)(2,1)S(1)} %pad_maximum_fusion.1), channel_id=1, source_target_pairs={{0,1},{1,2},{2,3},{3,4},{4,5},{5,6},{6,7},{8,9},{9,10},{10,11},{11... | collective-permute-start | bytes 737288 | tf_op jit(solution)/shard_map/ppermute | solution.py:915
  7.5 14.3 %collective-permute-start.1 = (bf16[20,48,128]{2,1,0:T(8,128)(2,1)S(1)}, bf16[20,48,128]{2,1,0:T(8,128)(2,1)S(1)}, u32[]{:S(2)}, u32[]{:S(2)}) collective-permute-start(bf16[20,48,128]{2,1,0:T(8,128)(2,1)S(1)} %pad_maximum_fusion.2), channel_id=1, source_target_pairs={{1,0},{2,1},{3,2},{4,3},{5,4},{6,5},{7,6},{9,8},{10,9},{11,10},{12... | collective-permute-start | bytes 737288 | tf_op jit(solution)/shard_map/ppermute | solution.py:915
  21.8 0.7 copy-start.1
  21.8 0.8 copy-start.2
  132.4 14.4 %collective-permute-start.2 = (bf16[1136,128]{1,0:T(8,128)(2,1)}, bf16[1136,128]{1,0:T(8,128)(2,1)S(1)}, u32[]{:S(2)}, u32[]{:S(2)}) collective-permute-start(bf16[1136,128]{1,0:T(8,128)(2,1)} %get-tuple-element.69), channel_id=1, source_target_pairs={{0,16},{8,24},{16,0},{24,8},{1,17},{9,25},{17,1},{25,9},{2,18},{10... | collective-permute-start | bytes 872456 | tf_op jit(solution)/shard_map/ppermute | solution.py:924
  134.0 8.2 %collective-permute-start.3 = (bf16[16,48,128]{2,1,0:T(8,128)(2,1)}, bf16[16,48,128]{2,1,0:T(8,128)(2,1)S(1)}, u32[]{:S(2)}, u32[]{:S(2)}) collective-permute-start(bf16[16,48,128]{2,1,0:T(8,128)(2,1)} %get-tuple-element.70), channel_id=1, source_target_pairs={{0,1},{1,2},{2,3},{3,4},{4,5},{5,6},{6,7},{8,9},{9,10},{10,11},{11... | collective-permute-start | bytes 589832 | tf_op jit(solution)/shard_map/ppermute | solution.py:915
  138.5 8.3 %collective-permute-start.4 = (bf16[16,48,128]{2,1,0:T(8,128)(2,1)}, bf16[16,48,128]{2,1,0:T(8,128)(2,1)S(1)}, u32[]{:S(2)}, u32[]{:S(2)}) collective-permute-start(bf16[16,48,128]{2,1,0:T(8,128)(2,1)} %get-tuple-element.71), channel_id=1, source_target_pairs={{1,0},{2,1},{3,2},{4,3},{5,4},{6,5},{7,6},{9,8},{10,9},{11,10},{12... | collective-permute-start | bytes 589832 | tf_op jit(solution)/shard_map/ppermute | solution.py:915
  148.0 1.6 collective-permute-start.5
  149.7 7.1 %collective-permute-start.6 = (bf16[592,128]{1,0:T(8,128)(2,1)S(1)}, bf16[592,128]{1,0:T(8,128)(2,1)S(1)}, u32[]{:S(2)}, u32[]{:S(2)}) collective-permute-start(bf16[592,128]{1,0:T(8,128)(2,1)S(1)} %pad_maximum_fusion.3), channel_id=1, source_target_pairs={{0,1},{1,0},{2,3},{3,2},{4,5},{5,4},{6,7},{7,6},{8,9},{9,8},{10,11... | collective-permute-start | bytes 454664 | tf_op jit(solution)/shard_map/ppermute | solution.py:924
  156.9 6.2 %collective-permute-start.7 = (bf16[592,128]{1,0:T(8,128)(2,1)S(1)}, bf16[592,128]{1,0:T(8,128)(2,1)S(1)}, u32[]{:S(2)}, u32[]{:S(2)}) collective-permute-start(bf16[592,128]{1,0:T(8,128)(2,1)S(1)} %pad_maximum_fusion.4), channel_id=1, source_target_pairs={{0,2},{1,3},{2,0},{3,1},{4,6},{5,7},{6,4},{7,5},{8,10},{9,11},{10,... | collective-permute-start | bytes 454664 | tf_op jit(solution)/shard_map/ppermute | solution.py:924
  163.2 8.7 %collective-permute-start.8 = (bf16[592,128]{1,0:T(8,128)(2,1)S(1)}, bf16[592,128]{1,0:T(8,128)(2,1)S(1)}, u32[]{:S(2)}, u32[]{:S(2)}) collective-permute-start(bf16[592,128]{1,0:T(8,128)(2,1)S(1)} %pad_maximum_fusion.5), channel_id=1, source_target_pairs={{0,4},{1,5},{2,6},{3,7},{4,0},{5,1},{6,2},{7,3},{8,12},{9,13},{10,... | collective-permute-start | bytes 454664 | tf_op jit(solution)/shard_map/ppermute | solution.py:924
  172.0 5.1 %collective-permute-start.9 = (bf16[1,544,128]{2,1,0:T(8,128)(2,1)S(1)}, bf16[1,544,128]{2,1,0:T(8,128)(2,1)S(1)}, u32[]{:S(2)}, u32[]{:S(2)}) collective-permute-start(bf16[1,544,128]{2,1,0:T(8,128)(2,1)S(1)} %fusion.4), channel_id=1, source_target_pairs={{0,16},{8,24},{16,0},{24,8},{1,17},{9,25},{17,1},{25,9},{2,18},{10... | collective-permute-start | bytes 417800 | tf_op jit(solution)/shard_map/ppermute | solution.py:924
  177.2 1.6 copy-start
  177.2 1.6 collective-permute-start.10
  178.8 0.7 copy-start.3

commit v6 on v5

--- a/solution.py
+++ b/solution.py
@@ -18,6 +18,7 @@
 NBLK = 17
 UNROLL = 16
 PACK = 2
+BACK = 8
 SLOTS = 3
 TILE = 512
 
@@ -550,13 +551,15 @@
         rhi_ref[b] = rim[HALO:]
 
     groups = [tuple(range(at, at + unroll)) for at in range(0, windows, unroll)]
+    width = min(BACK, windows)
+    backs = [tuple(range(at, at + width)) for at in range(0, windows, width)]
 
     def phases(b):
         return [
             (3, [project_halo(b)] + [project(b, i) for i in range(tiles)]),
             (4, [attend(b, group) for group in groups]),
             (11, [middle(b, i) for i in range(tiles)]),
-            (4, [attend_back(b, group) for group in groups]),
+            (4, [attend_back(b, group) for group in backs]),
             (3, [finish_halo(b)] + [finish(b, i) for i in range(tiles)]),
         ]
 

time: 185 us -> 183 us (0.989)
  Pallas kernels: 127 us -> 125 us
where the time goes in v6:
time: 183 us; the launch traced here: 182 us
  Pallas kernels  125 us (68%)
  waiting for transfers between devices  23.5 us (13%)
  starting transfers between devices  22.8 us (12%)
  other arithmetic  7.04 us (4%)
  local copies, waits for them, and re-layouts  2.55 us (1%)
    pallas_call x1, Pallas kernels, main_call(): pl.pallas_call(main_kernel, grid_spec=pltpu.PrefetchScalarGridSpec(num_sc...  108 us
    ppermute x7, waiting for transfers between devices, partner(): return lax.ppermute(values, axis, [(i, i ^ bit) for i in range(devices)])  17.2 us
    pallas_call x1, Pallas kernels, bias_table(): pl.pallas_call(bias_kernel, grid=(structs, atoms // rows), in_specs=[pl.B...  13 us
    ppermute x4, starting transfers between devices, passed(): return lax.ppermute(shard, 'win', pairs)  12 us
    ppermute x7, starting transfers between devices, partner(): return lax.ppermute(values, axis, [(i, i ^ bit) for i in range(devices)])  10.8 us
    ppermute x4, waiting for transfers between devices, passed(): return lax.ppermute(shard, 'win', pairs)  6.28 us
    pallas_call x1, Pallas kernels, update_call(): pl.pallas_call(update_kernel, grid=(1,), in_specs=[full] * len(args), out...  4.09 us
  transfers between devices with their start and end apart: 11, of which 8 were waited for; matrix products, arithmetic and copies ran while one was open for 3% of the time, Pallas kernels for 7%

profile of v6, /device:TPU:0, one launch (start us, length us, event | category | flops | bytes accessed | tf_op | source)
XLA Modules:
  0.0 182.0 jit_solution(2960828378997361804)
XLA Ops:
  0.6 0.8 reduce-precision_convert_fusion
  1.5 1.1 fusion.22
  2.6 4.9 %collective-permute-start = (bf16[20,48,128]{2,1,0:T(8,128)(2,1)S(1)}, bf16[20,48,128]{2,1,0:T(8,128)(2,1)S(1)}, u32[]{:S(2)}, u32[]{:S(2)}) collective-permute-start(bf16[20,48,128]{2,1,0:T(8,128)(2,1)S(1)} %pad_maximum_fusion.1), channel_id=1, source_target_pairs={{0,1},{1,2},{2,3},{3,4},{4,5},{5,6},{6,7},{8,9},{9,10},{10,11},{11... | collective-permute-start | bytes 737288 | tf_op jit(solution)/shard_map/ppermute | solution.py:918
  7.5 1.3 collective-permute-start.1
  8.8 13.0 %pair_bias.1 = (f32[2,32,128,128]{3,2,1,0:T(8,128)}, bf16[2,32,128,128]{3,2,1,0:T(8,128)(2,1)}) custom-call(bf16[2,1024,16,128]{3,2,1,0:T(8,128)(2,1)} %pair_ref.3, f32[4,16]{1,0:T(4,128)} %bitcast.9), custom_call_target="tpu_custom_call" | custom-call | flops 1000000000 | bytes 15728640 | tf_op jit(solution)/shard_map/pair_bias/pallas_call | solution.py:165
  22.6 108.1 %block.1 = (bf16[16,1024,128]{2,1,0:T(8,128)(2,1)}, bf16[16,1024,128]{2,1,0:T(8,128)(2,1)}, bf16[16,48,128]{2,1,0:T(8,128)(2,1)}, bf16[16,48,128]{2,1,0:T(8,128)...) custom-call(s32[16]{0:T(128)} %ids_ref.1, bf16[16,1024,128]{2,1,0:T(8,128)(2,1)} %x_ref.1, ...), custom_call_target="tpu_custom_call" | custom-call | tf_op jit(solution)/shard_map/block/pallas_call | solution.py:674
  130.7 1.6 collective-permute-start.2
  132.2 4.5 %collective-permute-start.3 = (bf16[16,48,128]{2,1,0:T(8,128)(2,1)}, bf16[16,48,128]{2,1,0:T(8,128)(2,1)S(1)}, u32[]{:S(2)}, u32[]{:S(2)}) collective-permute-start(bf16[16,48,128]{2,1,0:T(8,128)(2,1)} %get-tuple-element.70), channel_id=1, source_target_pairs={{0,1},{1,2},{2,3},{3,4},{4,5},{5,6},{6,7},{8,9},{9,10},{10,11},{11... | collective-permute-start | bytes 589832 | tf_op jit(solution)/shard_map/ppermute | solution.py:918
  136.8 1.3 collective-permute-start.4
  138.8 1.6 collective-permute-done.3
  140.4 4.7 %collective-permute-done.4 = bf16[16,48,128]{2,1,0:T(8,128)(2,1)S(1)} collective-permute-done((bf16[16,48,128]{2,1,0:T(8,128)(2,1)}, bf16[16,48,128]{2,1,0:T(8,128)(2,1)S(1)}, u32[]{:S(2)}, u32[]{:S(2)}) %collective-permute-start.4) | collective-permute-done | bytes 196640 | tf_op jit(solution)/shard_map/ppermute | solution.py:918
  145.1 1.1 convert_add_fusion
  146.3 1.6 collective-permute-done.5
  148.0 2.8 %collective-permute-start.6 = (bf16[592,128]{1,0:T(8,128)(2,1)S(1)}, bf16[592,128]{1,0:T(8,128)(2,1)S(1)}, u32[]{:S(2)}, u32[]{:S(2)}) collective-permute-start(bf16[592,128]{1,0:T(8,128)(2,1)S(1)} %pad_maximum_fusion.3), channel_id=1, source_target_pairs={{0,1},{1,0},{2,3},{3,2},{4,5},{5,4},{6,7},{7,6},{8,9},{9,8},{10,11... | collective-permute-start | bytes 454664 | tf_op jit(solution)/shard_map/ppermute | solution.py:927
  150.8 4.2 %collective-permute-done.6 = bf16[592,128]{1,0:T(8,128)(2,1)S(1)} collective-permute-done((bf16[592,128]{1,0:T(8,128)(2,1)S(1)}, bf16[592,128]{1,0:T(8,128)(2,1)S(1)}, u32[]{:S(2)}, u32[]{:S(2)}) %collective-permute-start.6) | collective-permute-done | bytes 151584 | tf_op jit(solution)/shard_map/ppermute | solution.py:927
  155.1 2.8 %collective-permute-start.7 = (bf16[592,128]{1,0:T(8,128)(2,1)S(1)}, bf16[592,128]{1,0:T(8,128)(2,1)S(1)}, u32[]{:S(2)}, u32[]{:S(2)}) collective-permute-start(bf16[592,128]{1,0:T(8,128)(2,1)S(1)} %pad_maximum_fusion.4), channel_id=1, source_target_pairs={{0,2},{1,3},{2,0},{3,1},{4,6},{5,7},{6,4},{7,5},{8,10},{9,11},{10,... | collective-permute-start | bytes 454664 | tf_op jit(solution)/shard_map/ppermute | solution.py:927
  157.9 3.4 %collective-permute-done.7 = bf16[592,128]{1,0:T(8,128)(2,1)S(1)} collective-permute-done((bf16[592,128]{1,0:T(8,128)(2,1)S(1)}, bf16[592,128]{1,0:T(8,128)(2,1)S(1)}, u32[]{:S(2)}, u32[]{:S(2)}) %collective-permute-start.7) | collective-permute-done | bytes 151584 | tf_op jit(solution)/shard_map/ppermute | solution.py:927
  161.4 2.8 %collective-permute-start.8 = (bf16[592,128]{1,0:T(8,128)(2,1)S(1)}, bf16[592,128]{1,0:T(8,128)(2,1)S(1)}, u32[]{:S(2)}, u32[]{:S(2)}) collective-permute-start(bf16[592,128]{1,0:T(8,128)(2,1)S(1)} %pad_maximum_fusion.5), channel_id=1, source_target_pairs={{0,4},{1,5},{2,6},{3,7},{4,0},{5,1},{6,2},{7,3},{8,12},{9,13},{10,... | collective-permute-start | bytes 454664 | tf_op jit(solution)/shard_map/ppermute | solution.py:927
  164.3 1.7 fusion.1
  165.9 4.2 %collective-permute-done.8 = bf16[592,128]{1,0:T(8,128)(2,1)S(1)} collective-permute-done((bf16[592,128]{1,0:T(8,128)(2,1)S(1)}, bf16[592,128]{1,0:T(8,128)(2,1)S(1)}, u32[]{:S(2)}, u32[]{:S(2)}) %collective-permute-start.8) | collective-permute-done | bytes 151584 | tf_op jit(solution)/shard_map/ppermute | solution.py:927
  170.9 1.7 fusion.2
  172.5 2.9 %collective-permute-done.9 = bf16[1,544,128]{2,1,0:T(8,128)(2,1)S(1)} collective-permute-done((bf16[1,544,128]{2,1,0:T(8,128)(2,1)S(1)}, bf16[1,544,128]{2,1,0:T(8,128)(2,1)S(1)}, u32[]{:S(2)}, u32[]{:S(2)}) %collective-permute-start.9) | collective-permute-done | bytes 139296 | tf_op jit(solution)/shard_map/ppermute | solution.py:927
  176.1 0.9 collective-permute-done.10.other_ref
  177.8 4.1 %update.1 = (f32[17,16,128]{2,1,0:T(8,128)}, f32[7,128]{1,0:T(8,128)}, f32[4,16]{1,0:T(4,128)}, f32[17,16,128]{2,1,0:T(8,128)}, f32[17,16,128]{2,1,0:T(8,128)}, ...) custom-call(bf16[2,544,128]{2,1,0:T(8,128)(2,1)} %copy-done, ...), custom_call_target="tpu_custom_call" | custom-call | tf_op jit(solution)/shard_map/update/pallas_call | solution.py:901
  (38 shorter events, 4.0 us)
Async XLA Ops:
  2.6 19.2 %collective-permute-start = (bf16[20,48,128]{2,1,0:T(8,128)(2,1)S(1)}, bf16[20,48,128]{2,1,0:T(8,128)(2,1)S(1)}, u32[]{:S(2)}, u32[]{:S(2)}) collective-permute-start(bf16[20,48,128]{2,1,0:T(8,128)(2,1)S(1)} %pad_maximum_fusion.1), channel_id=1, source_target_pairs={{0,1},{1,2},{2,3},{3,4},{4,5},{5,6},{6,7},{8,9},{9,10},{10,11},{11... | collective-permute-start | bytes 737288 | tf_op jit(solution)/shard_map/ppermute | solution.py:918
  7.5 14.3 %collective-permute-start.1 = (bf16[20,48,128]{2,1,0:T(8,128)(2,1)S(1)}, bf16[20,48,128]{2,1,0:T(8,128)(2,1)S(1)}, u32[]{:S(2)}, u32[]{:S(2)}) collective-permute-start(bf16[20,48,128]{2,1,0:T(8,128)(2,1)S(1)} %pad_maximum_fusion.2), channel_id=1, source_target_pairs={{1,0},{2,1},{3,2},{4,3},{5,4},{6,5},{7,6},{9,8},{10,9},{11,10},{12... | collective-permute-start | bytes 737288 | tf_op jit(solution)/shard_map/ppermute | solution.py:918
  21.8 0.7 copy-start.1
  21.8 0.8 copy-start.2
  130.7 14.4 %collective-permute-start.2 = (bf16[1136,128]{1,0:T(8,128)(2,1)}, bf16[1136,128]{1,0:T(8,128)(2,1)S(1)}, u32[]{:S(2)}, u32[]{:S(2)}) collective-permute-start(bf16[1136,128]{1,0:T(8,128)(2,1)} %get-tuple-element.69), channel_id=1, source_target_pairs={{0,16},{8,24},{16,0},{24,8},{1,17},{9,25},{17,1},{25,9},{2,18},{10... | collective-permute-start | bytes 872456 | tf_op jit(solution)/shard_map/ppermute | solution.py:927
  132.2 8.2 %collective-permute-start.3 = (bf16[16,48,128]{2,1,0:T(8,128)(2,1)}, bf16[16,48,128]{2,1,0:T(8,128)(2,1)S(1)}, u32[]{:S(2)}, u32[]{:S(2)}) collective-permute-start(bf16[16,48,128]{2,1,0:T(8,128)(2,1)} %get-tuple-element.70), channel_id=1, source_target_pairs={{0,1},{1,2},{2,3},{3,4},{4,5},{5,6},{6,7},{8,9},{9,10},{10,11},{11... | collective-permute-start | bytes 589832 | tf_op jit(solution)/shard_map/ppermute | solution.py:918
  136.8 8.3 %collective-permute-start.4 = (bf16[16,48,128]{2,1,0:T(8,128)(2,1)}, bf16[16,48,128]{2,1,0:T(8,128)(2,1)S(1)}, u32[]{:S(2)}, u32[]{:S(2)}) collective-permute-start(bf16[16,48,128]{2,1,0:T(8,128)(2,1)} %get-tuple-element.71), channel_id=1, source_target_pairs={{1,0},{2,1},{3,2},{4,3},{5,4},{6,5},{7,6},{9,8},{10,9},{11,10},{12... | collective-permute-start | bytes 589832 | tf_op jit(solution)/shard_map/ppermute | solution.py:918
  146.2 1.6 collective-permute-start.5
  148.0 7.1 %collective-permute-start.6 = (bf16[592,128]{1,0:T(8,128)(2,1)S(1)}, bf16[592,128]{1,0:T(8,128)(2,1)S(1)}, u32[]{:S(2)}, u32[]{:S(2)}) collective-permute-start(bf16[592,128]{1,0:T(8,128)(2,1)S(1)} %pad_maximum_fusion.3), channel_id=1, source_target_pairs={{0,1},{1,0},{2,3},{3,2},{4,5},{5,4},{6,7},{7,6},{8,9},{9,8},{10,11... | collective-permute-start | bytes 454664 | tf_op jit(solution)/shard_map/ppermute | solution.py:927
  155.1 6.2 %collective-permute-start.7 = (bf16[592,128]{1,0:T(8,128)(2,1)S(1)}, bf16[592,128]{1,0:T(8,128)(2,1)S(1)}, u32[]{:S(2)}, u32[]{:S(2)}) collective-permute-start(bf16[592,128]{1,0:T(8,128)(2,1)S(1)} %pad_maximum_fusion.4), channel_id=1, source_target_pairs={{0,2},{1,3},{2,0},{3,1},{4,6},{5,7},{6,4},{7,5},{8,10},{9,11},{10,... | collective-permute-start | bytes 454664 | tf_op jit(solution)/shard_map/ppermute | solution.py:927
  161.4 8.7 %collective-permute-start.8 = (bf16[592,128]{1,0:T(8,128)(2,1)S(1)}, bf16[592,128]{1,0:T(8,128)(2,1)S(1)}, u32[]{:S(2)}, u32[]{:S(2)}) collective-permute-start(bf16[592,128]{1,0:T(8,128)(2,1)S(1)} %pad_maximum_fusion.5), channel_id=1, source_target_pairs={{0,4},{1,5},{2,6},{3,7},{4,0},{5,1},{6,2},{7,3},{8,12},{9,13},{10,... | collective-permute-start | bytes 454664 | tf_op jit(solution)/shard_map/ppermute | solution.py:927
  170.3 5.1 %collective-permute-start.9 = (bf16[1,544,128]{2,1,0:T(8,128)(2,1)S(1)}, bf16[1,544,128]{2,1,0:T(8,128)(2,1)S(1)}, u32[]{:S(2)}, u32[]{:S(2)}) collective-permute-start(bf16[1,544,128]{2,1,0:T(8,128)(2,1)S(1)} %fusion.4), channel_id=1, source_target_pairs={{0,16},{8,24},{16,0},{24,8},{1,17},{9,25},{17,1},{25,9},{2,18},{10... | collective-permute-start | bytes 417800 | tf_op jit(solution)/shard_map/ppermute | solution.py:927
  175.4 1.6 copy-start
  175.4 1.6 collective-permute-start.10
  177.1 0.7 copy-start.3

commit v7 on v6

--- a/solution.py
+++ b/solution.py
@@ -159,7 +159,7 @@
 
 def bias_table(pair, turned_weight):
     structs, atoms = pair.shape[:2]
-    count = min(8, atoms // QW)
+    count = min(16, atoms // QW)
     rows = count * QW
     table = pl.BlockSpec((1, count, KW, C), lambda s, i: (s, i, 0, 0))
     return pl.pallas_call(
@@ -862,7 +862,7 @@
         low_ref[b] = new.astype(BF16)
         neww_ema_ref[b] = ema_decay * ew_ref[b] + (1.0 - ema_decay) * new
 
-    for _ in pipeline([beside([one(b) for b in range(at, min(at + 6, NBLK))]) for at in range(0, NBLK, 6)]):
+    for _ in pipeline([beside([one(b) for b in range(at, min(at + 9, NBLK))]) for at in range(0, NBLK, 9)]):
         pass
     sums = small_ref[8:]
     pair_total = lax.dot_general(

time: 183 us -> 182 us (level)
  no operation moved by 1% of the time
where the time goes in v7:
time: 182 us
  Pallas kernels  125 us (69%)
  waiting for transfers between devices  23.5 us (13%)
  starting transfers between devices  22.8 us (13%)
  other arithmetic  7.04 us (4%)
  local copies, waits for them, and re-layouts  2.55 us (1%)
    pallas_call x1, Pallas kernels, main_call(): pl.pallas_call(main_kernel, grid_spec=pltpu.PrefetchScalarGridSpec(num_sc...  108 us
    ppermute x7, waiting for transfers between devices, partner(): return lax.ppermute(values, axis, [(i, i ^ bit) for i in range(devices)])  17.2 us
    pallas_call x1, Pallas kernels, bias_table(): pl.pallas_call(bias_kernel, grid=(structs, atoms // rows), in_specs=[pl.B...  12.2 us
    ppermute x4, starting transfers between devices, passed(): return lax.ppermute(shard, 'win', pairs)  12 us
    ppermute x7, starting transfers between devices, partner(): return lax.ppermute(values, axis, [(i, i ^ bit) for i in range(devices)])  10.8 us
    ppermute x4, waiting for transfers between devices, passed(): return lax.ppermute(shard, 'win', pairs)  6.3 us
    pallas_call x1, Pallas kernels, update_call(): pl.pallas_call(update_kernel, grid=(1,), in_specs=[full] * len(args), out...  4.12 us
  transfers between devices with their start and end apart: 11, of which 8 were waited for; matrix products, arithmetic and copies ran while one was open for 3% of the time, Pallas kernels for 7%

profile of v7, /device:TPU:0, one launch (start us, length us, event | category | flops | bytes accessed | tf_op | source)
XLA Modules:
  0.0 181.5 jit_solution(68173511140914864)
XLA Ops:
  0.6 0.8 reduce-precision_convert_fusion
  1.5 1.1 fusion.22
  2.6 4.9 %collective-permute-start = (bf16[20,48,128]{2,1,0:T(8,128)(2,1)S(1)}, bf16[20,48,128]{2,1,0:T(8,128)(2,1)S(1)}, u32[]{:S(2)}, u32[]{:S(2)}) collective-permute-start(bf16[20,48,128]{2,1,0:T(8,128)(2,1)S(1)} %pad_maximum_fusion.1), channel_id=1, source_target_pairs={{0,1},{1,2},{2,3},{3,4},{4,5},{5,6},{6,7},{8,9},{9,10},{10,11},{11... | collective-permute-start | bytes 737288 | tf_op jit(solution)/shard_map/ppermute | solution.py:918
  7.5 1.3 collective-permute-start.1
  8.8 12.2 %pair_bias.1 = (f32[2,32,128,128]{3,2,1,0:T(8,128)}, bf16[2,32,128,128]{3,2,1,0:T(8,128)(2,1)}) custom-call(bf16[2,1024,16,128]{3,2,1,0:T(8,128)(2,1)} %pair_ref.3, f32[4,16]{1,0:T(4,128)} %bitcast.9), custom_call_target="tpu_custom_call" | custom-call | flops 1000000000 | bytes 15728640 | tf_op jit(solution)/shard_map/pair_bias/pallas_call | solution.py:165
  21.8 108.3 %block.1 = (bf16[16,1024,128]{2,1,0:T(8,128)(2,1)}, bf16[16,1024,128]{2,1,0:T(8,128)(2,1)}, bf16[16,48,128]{2,1,0:T(8,128)(2,1)}, bf16[16,48,128]{2,1,0:T(8,128)...) custom-call(s32[16]{0:T(128)} %ids_ref.1, bf16[16,1024,128]{2,1,0:T(8,128)(2,1)} %x_ref.1, ...), custom_call_target="tpu_custom_call" | custom-call | tf_op jit(solution)/shard_map/block/pallas_call | solution.py:674
  130.1 1.6 collective-permute-start.2
  131.7 4.5 %collective-permute-start.3 = (bf16[16,48,128]{2,1,0:T(8,128)(2,1)}, bf16[16,48,128]{2,1,0:T(8,128)(2,1)S(1)}, u32[]{:S(2)}, u32[]{:S(2)}) collective-permute-start(bf16[16,48,128]{2,1,0:T(8,128)(2,1)} %get-tuple-element.70), channel_id=1, source_target_pairs={{0,1},{1,2},{2,3},{3,4},{4,5},{5,6},{6,7},{8,9},{9,10},{10,11},{11... | collective-permute-start | bytes 589832 | tf_op jit(solution)/shard_map/ppermute | solution.py:918
  136.2 1.3 collective-permute-start.4
  138.2 1.6 collective-permute-done.3
  139.8 4.7 %collective-permute-done.4 = bf16[16,48,128]{2,1,0:T(8,128)(2,1)S(1)} collective-permute-done((bf16[16,48,128]{2,1,0:T(8,128)(2,1)}, bf16[16,48,128]{2,1,0:T(8,128)(2,1)S(1)}, u32[]{:S(2)}, u32[]{:S(2)}) %collective-permute-start.4) | collective-permute-done | bytes 196640 | tf_op jit(solution)/shard_map/ppermute | solution.py:918
  144.5 1.1 convert_add_fusion
  145.8 1.6 collective-permute-done.5
  147.4 2.8 %collective-permute-start.6 = (bf16[592,128]{1,0:T(8,128)(2,1)S(1)}, bf16[592,128]{1,0:T(8,128)(2,1)S(1)}, u32[]{:S(2)}, u32[]{:S(2)}) collective-permute-start(bf16[592,128]{1,0:T(8,128)(2,1)S(1)} %pad_maximum_fusion.3), channel_id=1, source_target_pairs={{0,1},{1,0},{2,3},{3,2},{4,5},{5,4},{6,7},{7,6},{8,9},{9,8},{10,11... | collective-permute-start | bytes 454664 | tf_op jit(solution)/shard_map/ppermute | solution.py:927
  150.2 4.2 %collective-permute-done.6 = bf16[592,128]{1,0:T(8,128)(2,1)S(1)} collective-permute-done((bf16[592,128]{1,0:T(8,128)(2,1)S(1)}, bf16[592,128]{1,0:T(8,128)(2,1)S(1)}, u32[]{:S(2)}, u32[]{:S(2)}) %collective-permute-start.6) | collective-permute-done | bytes 151584 | tf_op jit(solution)/shard_map/ppermute | solution.py:927
  154.6 2.8 %collective-permute-start.7 = (bf16[592,128]{1,0:T(8,128)(2,1)S(1)}, bf16[592,128]{1,0:T(8,128)(2,1)S(1)}, u32[]{:S(2)}, u32[]{:S(2)}) collective-permute-start(bf16[592,128]{1,0:T(8,128)(2,1)S(1)} %pad_maximum_fusion.4), channel_id=1, source_target_pairs={{0,2},{1,3},{2,0},{3,1},{4,6},{5,7},{6,4},{7,5},{8,10},{9,11},{10,... | collective-permute-start | bytes 454664 | tf_op jit(solution)/shard_map/ppermute | solution.py:927
  157.4 3.4 %collective-permute-done.7 = bf16[592,128]{1,0:T(8,128)(2,1)S(1)} collective-permute-done((bf16[592,128]{1,0:T(8,128)(2,1)S(1)}, bf16[592,128]{1,0:T(8,128)(2,1)S(1)}, u32[]{:S(2)}, u32[]{:S(2)}) %collective-permute-start.7) | collective-permute-done | bytes 151584 | tf_op jit(solution)/shard_map/ppermute | solution.py:927
  160.9 2.8 %collective-permute-start.8 = (bf16[592,128]{1,0:T(8,128)(2,1)S(1)}, bf16[592,128]{1,0:T(8,128)(2,1)S(1)}, u32[]{:S(2)}, u32[]{:S(2)}) collective-permute-start(bf16[592,128]{1,0:T(8,128)(2,1)S(1)} %pad_maximum_fusion.5), channel_id=1, source_target_pairs={{0,4},{1,5},{2,6},{3,7},{4,0},{5,1},{6,2},{7,3},{8,12},{9,13},{10,... | collective-permute-start | bytes 454664 | tf_op jit(solution)/shard_map/ppermute | solution.py:927
  163.7 1.7 fusion.1
  165.4 4.2 %collective-permute-done.8 = bf16[592,128]{1,0:T(8,128)(2,1)S(1)} collective-permute-done((bf16[592,128]{1,0:T(8,128)(2,1)S(1)}, bf16[592,128]{1,0:T(8,128)(2,1)S(1)}, u32[]{:S(2)}, u32[]{:S(2)}) %collective-permute-start.8) | collective-permute-done | bytes 151584 | tf_op jit(solution)/shard_map/ppermute | solution.py:927
  170.3 1.7 fusion.2
  172.0 2.9 %collective-permute-done.9 = bf16[1,544,128]{2,1,0:T(8,128)(2,1)S(1)} collective-permute-done((bf16[1,544,128]{2,1,0:T(8,128)(2,1)S(1)}, bf16[1,544,128]{2,1,0:T(8,128)(2,1)S(1)}, u32[]{:S(2)}, u32[]{:S(2)}) %collective-permute-start.9) | collective-permute-done | bytes 139296 | tf_op jit(solution)/shard_map/ppermute | solution.py:927
  175.6 0.9 collective-permute-done.10.other_ref
  177.2 4.1 %update.1 = (f32[17,16,128]{2,1,0:T(8,128)}, f32[7,128]{1,0:T(8,128)}, f32[4,16]{1,0:T(4,128)}, f32[17,16,128]{2,1,0:T(8,128)}, f32[17,16,128]{2,1,0:T(8,128)}, ...) custom-call(bf16[2,544,128]{2,1,0:T(8,128)(2,1)} %copy-done, ...), custom_call_target="tpu_custom_call" | custom-call | tf_op jit(solution)/shard_map/update/pallas_call | solution.py:901
  (38 shorter events, 4.0 us)
Async XLA Ops:
  2.6 18.4 %collective-permute-start = (bf16[20,48,128]{2,1,0:T(8,128)(2,1)S(1)}, bf16[20,48,128]{2,1,0:T(8,128)(2,1)S(1)}, u32[]{:S(2)}, u32[]{:S(2)}) collective-permute-start(bf16[20,48,128]{2,1,0:T(8,128)(2,1)S(1)} %pad_maximum_fusion.1), channel_id=1, source_target_pairs={{0,1},{1,2},{2,3},{3,4},{4,5},{5,6},{6,7},{8,9},{9,10},{10,11},{11... | collective-permute-start | bytes 737288 | tf_op jit(solution)/shard_map/ppermute | solution.py:918
  7.5 13.5 %collective-permute-start.1 = (bf16[20,48,128]{2,1,0:T(8,128)(2,1)S(1)}, bf16[20,48,128]{2,1,0:T(8,128)(2,1)S(1)}, u32[]{:S(2)}, u32[]{:S(2)}) collective-permute-start(bf16[20,48,128]{2,1,0:T(8,128)(2,1)S(1)} %pad_maximum_fusion.2), channel_id=1, source_target_pairs={{1,0},{2,1},{3,2},{4,3},{5,4},{6,5},{7,6},{9,8},{10,9},{11,10},{12... | collective-permute-start | bytes 737288 | tf_op jit(solution)/shard_map/ppermute | solution.py:918
  21.0 0.7 copy-start.1
  21.0 0.8 copy-start.2
  130.1 14.4 %collective-permute-start.2 = (bf16[1136,128]{1,0:T(8,128)(2,1)}, bf16[1136,128]{1,0:T(8,128)(2,1)S(1)}, u32[]{:S(2)}, u32[]{:S(2)}) collective-permute-start(bf16[1136,128]{1,0:T(8,128)(2,1)} %get-tuple-element.69), channel_id=1, source_target_pairs={{0,16},{8,24},{16,0},{24,8},{1,17},{9,25},{17,1},{25,9},{2,18},{10... | collective-permute-start | bytes 872456 | tf_op jit(solution)/shard_map/ppermute | solution.py:927
  131.7 8.2 %collective-permute-start.3 = (bf16[16,48,128]{2,1,0:T(8,128)(2,1)}, bf16[16,48,128]{2,1,0:T(8,128)(2,1)S(1)}, u32[]{:S(2)}, u32[]{:S(2)}) collective-permute-start(bf16[16,48,128]{2,1,0:T(8,128)(2,1)} %get-tuple-element.70), channel_id=1, source_target_pairs={{0,1},{1,2},{2,3},{3,4},{4,5},{5,6},{6,7},{8,9},{9,10},{10,11},{11... | collective-permute-start | bytes 589832 | tf_op jit(solution)/shard_map/ppermute | solution.py:918
  136.2 8.3 %collective-permute-start.4 = (bf16[16,48,128]{2,1,0:T(8,128)(2,1)}, bf16[16,48,128]{2,1,0:T(8,128)(2,1)S(1)}, u32[]{:S(2)}, u32[]{:S(2)}) collective-permute-start(bf16[16,48,128]{2,1,0:T(8,128)(2,1)} %get-tuple-element.71), channel_id=1, source_target_pairs={{1,0},{2,1},{3,2},{4,3},{5,4},{6,5},{7,6},{9,8},{10,9},{11,10},{12... | collective-permute-start | bytes 589832 | tf_op jit(solution)/shard_map/ppermute | solution.py:918
  145.7 1.6 collective-permute-start.5
  147.4 7.1 %collective-permute-start.6 = (bf16[592,128]{1,0:T(8,128)(2,1)S(1)}, bf16[592,128]{1,0:T(8,128)(2,1)S(1)}, u32[]{:S(2)}, u32[]{:S(2)}) collective-permute-start(bf16[592,128]{1,0:T(8,128)(2,1)S(1)} %pad_maximum_fusion.3), channel_id=1, source_target_pairs={{0,1},{1,0},{2,3},{3,2},{4,5},{5,4},{6,7},{7,6},{8,9},{9,8},{10,11... | collective-permute-start | bytes 454664 | tf_op jit(solution)/shard_map/ppermute | solution.py:927
  154.6 6.2 %collective-permute-start.7 = (bf16[592,128]{1,0:T(8,128)(2,1)S(1)}, bf16[592,128]{1,0:T(8,128)(2,1)S(1)}, u32[]{:S(2)}, u32[]{:S(2)}) collective-permute-start(bf16[592,128]{1,0:T(8,128)(2,1)S(1)} %pad_maximum_fusion.4), channel_id=1, source_target_pairs={{0,2},{1,3},{2,0},{3,1},{4,6},{5,7},{6,4},{7,5},{8,10},{9,11},{10,... | collective-permute-start | bytes 454664 | tf_op jit(solution)/shard_map/ppermute | solution.py:927
  160.9 8.7 %collective-permute-start.8 = (bf16[592,128]{1,0:T(8,128)(2,1)S(1)}, bf16[592,128]{1,0:T(8,128)(2,1)S(1)}, u32[]{:S(2)}, u32[]{:S(2)}) collective-permute-start(bf16[592,128]{1,0:T(8,128)(2,1)S(1)} %pad_maximum_fusion.5), channel_id=1, source_target_pairs={{0,4},{1,5},{2,6},{3,7},{4,0},{5,1},{6,2},{7,3},{8,12},{9,13},{10,... | collective-permute-start | bytes 454664 | tf_op jit(solution)/shard_map/ppermute | solution.py:927
  169.7 5.1 %collective-permute-start.9 = (bf16[1,544,128]{2,1,0:T(8,128)(2,1)S(1)}, bf16[1,544,128]{2,1,0:T(8,128)(2,1)S(1)}, u32[]{:S(2)}, u32[]{:S(2)}) collective-permute-start(bf16[1,544,128]{2,1,0:T(8,128)(2,1)S(1)} %fusion.4), channel_id=1, source_target_pairs={{0,16},{8,24},{16,0},{24,8},{1,17},{9,25},{17,1},{25,9},{2,18},{10... | collective-permute-start | bytes 417800 | tf_op jit(solution)/shard_map/ppermute | solution.py:927
  174.9 1.6 copy-start
  174.9 1.6 collective-permute-start.10
  176.5 0.7 copy-start.3
